TPU v7x, 512 devices: a whole 4x8x8 slice. The times are simulated.
512 devices in a mesh: seq: 64 (over x, y, core), tp: 8 (over z).
Axes of the slice: x: 4, y: 8, z: 8, core: 2. Of those that a mesh axis runs over, the one named last changes fastest.
Arguments:
- queries: bfloat16 [10240, 8192], P('seq', 'tp'), may hold values from -6 to 6
- key_vectors: bfloat16 [10240, 8192], P('seq', 'tp'), may hold values from -6 to 6
- values: bfloat16 [10240, 8192], P('seq', 'tp'), may hold values from -6 to 6
- decay_log: float32 [10240, 64], P('seq', 'tp'), may hold values from -1 to 0, as said below
- norm_gain: float32 [8192], P('tp'), may hold values from 0.1 to 1.9
- grad_out: bfloat16 [10240, 8192], P('seq', 'tp'), may hold values from -6 to 6
Outputs:
- normed: bfloat16 [10240, 8192], P('seq', 'tp')
- grad_query: bfloat16 [10240, 8192], P('seq', 'tp')
- grad_key: bfloat16 [10240, 8192], P('seq', 'tp')
- grad_value: bfloat16 [10240, 8192], P('seq', 'tp')
Inputs may be any that keep to these rules, and one draw needn't show every extreme that they name: `decay_log`: every entry is negative.
All inputs are finite; a program needn't handle non-finite values.
Results may differ from a plain program's by a relative error of at most 0.0062.
Values sent between devices are 32-bit elements; how exact they have to be, the bound alone decides.
No kernel may reach another device: no remote copies, remote signals or barrier semaphores. Data moves between devices by JAX's collectives and lax.ppermute only.
A program may use at most 128 MiB of HBM per device.

v0:
```python
import jax
import jax.numpy as jnp
from jax import lax
from jax.sharding import PartitionSpec as P

HEAD_COUNT = 64
HEAD = 128


EPSILON = 1e-06
HIGH = lax.Precision.HIGHEST


def carried_in(part, axis, combine, identity, reverse):
    count = lax.axis_size(axis)
    place = lax.axis_index(axis)
    ahead = count - 1 - place if reverse else place
    gathered = jax.tree.map(lambda a: lax.all_gather(a, axis), part)
    state = jax.tree.map(lambda a, e: jnp.zeros_like(a) + jnp.asarray(e, a.dtype), part, identity)

    def one(turn, state):
        source = count - 1 - turn if reverse else turn
        return combine(
            state, jax.tree.map(lambda a: lax.dynamic_index_in_dim(a, source, 0, False), gathered)
        )

    return lax.fori_loop(0, ahead, one, state)


def forward_join(earlier, later):
    decay_one, state_one = earlier
    decay_two, state_two = later
    return (decay_one + decay_two, jnp.exp(decay_two)[:, None, None] * state_one + state_two)


def reverse_join(earlier, later):
    decay_far, grad_far = earlier
    decay_near, grad_near = later
    return (decay_far + decay_near, grad_near + jnp.exp(decay_near)[:, None, None] * grad_far)


def decay_tables(decay_part):
    inside = jnp.cumsum(decay_part, axis=0)
    totals = inside[-1]
    length = decay_part.shape[0]
    across = inside.T
    spread = across[:, :, None] - across[:, None, :]
    causal = jnp.tril(jnp.ones((length, length), jnp.bool_))[None]
    weights = jnp.where(causal, jnp.exp(jnp.where(causal, spread, 0.0)), 0.0)
    return (inside, totals, weights)


def body(queries, key_vectors, values, decay_log, norm_gain, grad_out):
    row_count = queries.shape[0]
    heads_here = decay_log.shape[1]
    head_width = queries.shape[1] // heads_here
    total_width = HEAD_COUNT * HEAD
    query3 = queries.reshape(row_count, heads_here, head_width)
    key3 = key_vectors.reshape(row_count, heads_here, head_width)
    value3 = values.reshape(row_count, heads_here, head_width)
    inside, totals, weights = decay_tables(decay_log)
    query_decayed = (query3.astype(jnp.float32) * jnp.exp(inside)[:, :, None]).astype(jnp.bfloat16)
    key_decayed = (key3.astype(jnp.float32) * jnp.exp(totals[None] - inside)[:, :, None]).astype(
        jnp.bfloat16
    )
    local_state = jnp.einsum(
        "thd,the->hde", key_decayed, value3, preferred_element_type=jnp.float32
    )
    zero_decay = jnp.zeros((heads_here,), jnp.float32)
    zero_state = jnp.zeros_like(local_state)
    unused_decay, entering = carried_in(
        (totals, local_state), "seq", forward_join, (zero_decay, zero_state), False
    )
    scores = jnp.einsum("thd,uhd->htu", query3, key3, preferred_element_type=jnp.float32)
    mixing = (scores * weights).astype(jnp.bfloat16)
    attended = jnp.einsum("htu,uhe->the", mixing, value3, preferred_element_type=jnp.float32)
    attended = attended + jnp.einsum(
        "thd,hde->the", query_decayed.astype(jnp.float32), entering, precision=HIGH
    )
    flat = attended.reshape(row_count, heads_here * head_width)
    scaled_grad = grad_out.astype(jnp.float32) * norm_gain[None]
    squares = jnp.sum(flat * flat, axis=-1)
    crossed = jnp.sum(scaled_grad * flat, axis=-1)
    square_sum = lax.psum(squares, "tp")
    cross_sum = lax.psum(crossed, "tp")
    inverse = lax.rsqrt(square_sum / total_width + EPSILON)
    normed = (flat * inverse[:, None] * norm_gain[None]).astype(jnp.bfloat16)
    cross_mean = cross_sum / total_width
    grad_flat = (
        inverse[:, None] * scaled_grad - flat * (inverse**3 * cross_mean)[:, None]
    ).astype(jnp.bfloat16)
    grad3 = grad_flat.reshape(row_count, heads_here, head_width)
    grad_scores = jnp.einsum("thd,uhd->htu", grad3, value3, preferred_element_type=jnp.float32)
    grad_mix = (grad_scores * weights).astype(jnp.bfloat16)
    rebuilt_state = jnp.einsum(
        "thd,the->hde", key_decayed, value3, preferred_element_type=jnp.float32
    )
    unused_again, state_used = carried_in(
        (totals, rebuilt_state), "seq", forward_join, (zero_decay, zero_state), False
    )
    grad_query = jnp.einsum("htu,uhd->thd", grad_mix, key3, preferred_element_type=jnp.float32)
    grad_query = grad_query + jnp.exp(inside)[:, :, None] * jnp.einsum(
        "the,hde->thd", grad3.astype(jnp.float32), state_used, precision=HIGH
    )
    grad_local = jnp.einsum(
        "thd,the->hde", query_decayed, grad3, preferred_element_type=jnp.float32
    )
    unused_total, arriving = carried_in(
        (totals, grad_local), "seq", reverse_join, (zero_decay, zero_state), True
    )
    grad_key = jnp.einsum("htu,thd->uhd", grad_mix, query3, preferred_element_type=jnp.float32)
    grad_key = grad_key + jnp.exp(totals[None] - inside)[:, :, None] * jnp.einsum(
        "uhe,hde->uhd", value3.astype(jnp.float32), arriving, precision=HIGH
    )
    grad_value = jnp.einsum("htu,the->uhe", mixing, grad3, preferred_element_type=jnp.float32)
    grad_value = grad_value + jnp.einsum(
        "uhd,hde->uhe", key_decayed.astype(jnp.float32), arriving, precision=HIGH
    )
    flat_shape = (row_count, heads_here * head_width)
    return (
        normed,
        grad_query.reshape(flat_shape).astype(jnp.bfloat16),
        grad_key.reshape(flat_shape).astype(jnp.bfloat16),
        grad_value.reshape(flat_shape).astype(jnp.bfloat16),
    )


def solution(mesh):
    in_specs = (
        P("seq", "tp"),
        P("seq", "tp"),
        P("seq", "tp"),
        P("seq", "tp"),
        P("tp"),
        P("seq", "tp"),
    )
    out_specs = (P("seq", "tp"), P("seq", "tp"), P("seq", "tp"), P("seq", "tp"))
    return jax.shard_map(body, mesh=mesh, in_specs=in_specs, out_specs=out_specs, check_vma=False)
```

profile of v0, /device:TPU:1, one launch (start us, length us, event | category | flops | bytes accessed | tf_op | source)
XLA Modules:
  0.0 491.6 jit_solution(17638336711089858700)
XLA Ops:
  9.1 2.6 fusion.27
  11.7 39.7 %all-gather.2 = f32[64,1,8]{2,1,0:T(1,128)S(1)} all-gather(f32[1,1,8]{2,1,0:T(1,128)S(1)} %bitcast.184), channel_id=1, replica_groups=mesh['seq'=64,'tp'=8] {'seq'}, dimensions={0}, use_global_device_ids=true | all-gather | bytes 2080 | tf_op jit(solution)/shard_map/all_gather | solution.py:18
  53.7 111.7 %all-gather.6.cloned.1.call-done = f32[512,128,128]{2,1,0:T(8,128)} async-done(((f32[8,128,128]{2,1,0:T(8,128)}), f32[512,128,128]{2,1,0:T(8,128)}) %all-gather.6.cloned.1.call-update) | async-done | bytes 33554448 | tf_op jit(solution)/shard_map/all_gather | solution.py:18
  165.4 1.2 while.31
  165.4 1.2 bitcast_add_fusion.4
  166.7 1.8 multiply_reduce_fusion
  168.6 14.3 %all-reduce.1 = (f32[160]{0:T(256)S(1)}, f32[160]{0:T(256)S(1)}) all-reduce(f32[160]{0:T(256)S(1)} %get-tuple-element.175, f32[160]{0:T(256)S(1)} %fusion.15), channel_id=1, replica_groups=mesh['seq'=64,'tp'=8] {'tp'}, use_global_device_ids=true, to_apply=%region_5.6 | all-reduce | flops 320 | bytes 2560 | tf_op jit(solution)/shard_map/psum | solution.py:84
  183.0 1.9 fusion.18
  184.9 1.5 fusion.21
  189.2 216.2 %all-gather.8.cloned.1.call-done = f32[512,128,128]{2,1,0:T(8,128)} async-done(((f32[8,128,128]{2,1,0:T(8,128)}), f32[512,128,128]{2,1,0:T(8,128)}) %all-gather.8.cloned.1.call-update) | async-done | bytes 33554448 | tf_op jit(solution)/shard_map/all_gather | solution.py:18
  405.4 76.8 %while.32 = (s32[]{:T(128)}, f32[8,128,128]{2,1,0:T(8,128)S(1)}, s32[]{:T(128)}, f32[64,8,128,128]{3,2,1,0:T(8,128)}, f32[64,8]{1,0:T(8,128)S(1)}, /*index=5*/s32[]{:T(128)}, s32[]{:T(128)}, s32[]{:T(128)}, s32[]{:T(128)}) while((s32[]{:T(128)}, f32[8,128,128]{2,1,0:T(8,128)S(1)}, s32[]{:T(128)}, f32[64,8,128,128]{3,2,1,0:T(8,128)}, ...), condition=%wide.region_9.10_spmd, body=%wide.region_8.9_spmd.sunk | while | flops 262150 | bytes 1573107 | solution.py:27
  405.4 1.2 bitcast_add_fusion.5
  406.7 1.2 bitcast_add_fusion.5
  407.9 1.2 bitcast_add_fusion.5
  411.6 1.2 bitcast_add_fusion.5
  416.6 1.2 bitcast_add_fusion.5
  421.5 1.2 bitcast_add_fusion.5
  426.5 1.2 bitcast_add_fusion.5
  430.2 1.2 bitcast_add_fusion.5
  431.4 1.2 bitcast_add_fusion.5
  435.1 1.2 bitcast_add_fusion.5
  440.1 1.2 bitcast_add_fusion.5
  445.0 1.2 bitcast_add_fusion.5
  450.0 1.2 bitcast_add_fusion.5
  453.7 1.2 bitcast_add_fusion.5
  454.9 1.2 bitcast_add_fusion.5
  458.7 1.2 bitcast_add_fusion.5
  463.6 1.2 bitcast_add_fusion.5
  468.6 1.2 bitcast_add_fusion.5
  473.5 1.2 bitcast_add_fusion.5
  477.2 1.2 bitcast_add_fusion.5
  478.5 1.2 bitcast_add_fusion.5
  (142 shorter events, 59.3 us)
Async XLA Ops:
  7.2 44.3 %copy-start = (bf16[160,1024]{1,0:T(8,128)(2,1)S(1)}, bf16[160,1024]{1,0:T(8,128)(2,1)}, u32[]{:S(2)}) copy-start(bf16[160,1024]{1,0:T(8,128)(2,1)} %param.10) | copy-start | bytes 983044
  7.2 44.3 %copy-start.2 = (bf16[160,1024]{1,0:T(8,128)(2,1)S(1)}, bf16[160,1024]{1,0:T(8,128)(2,1)}, u32[]{:S(2)}) copy-start(bf16[160,1024]{1,0:T(8,128)(2,1)} %param.11) | copy-start | bytes 983044
  7.2 158.2 %all-gather.6.cloned.1.call-start = ((), (), s32[]{:S(2)}) async-start(), calls=%async_computation | async-start | bytes 34078720 | tf_op jit(solution)/shard_map/all_gather | solution.py:18
  11.7 393.6 %all-gather.8.cloned.1.call-start = ((), (), s32[]{:S(2)}) async-start(), calls=%async_computation.1 | async-start | bytes 34078720 | tf_op jit(solution)/shard_map/all_gather | solution.py:18
  51.5 1.0 copy-start.1
  166.6 1.8 copy-start.3
  166.7 1.8 copy-start.4
Sparse Core Ops, SparseCore 0:
  11.8 153.4 all-gather.5
  186.5 218.7 all-gather.7
where the time goes:
time: 495 us; the launch traced here: 492 us
  waiting for transfers between devices  328 us (66%)
  other arithmetic  77.9 us (16%)
  blocking collectives  54.1 us (11%)
  between operations  14.2 us (3%)
  matrix products  11 us (2%)
    all_gather x2, waiting for transfers between devices, carried_in(): gathered = jax.tree.map(lambda a: lax.all_gather(a, axis), part)  328 us
    add x62, other arithmetic, reverse_join(): grad_near + jnp.exp(decay_near)[:, None, None] * grad_far  73.8 us
    all_gather x1, blocking collectives, carried_in(): gathered = jax.tree.map(lambda a: lax.all_gather(a, axis), part)  39.7 us
    psum x1, blocking collectives, body(): square_sum = lax.psum(squares, 'tp')  14.3 us
  transfers between devices with their start and end apart: 2, of which 2 were waited for; matrix products, arithmetic and copies ran while one was open for 1% of the time, Pallas kernels for 0%

commit v1 on v0

v1 whole, which is shorter than its diff:
```python
import functools

import jax
import jax.numpy as jnp
from jax import lax
from jax.experimental import pallas as pl
from jax.experimental.pallas import tpu as pltpu
from jax.sharding import PartitionSpec as P

HEAD_COUNT = 64
HEAD = 128
EPSILON = 1e-06
HIGH = lax.Precision.HIGHEST
F32 = jnp.float32
BF16 = jnp.bfloat16
VMEM_LIMIT = 48 * 1024 * 1024


def dot_nn(a, b):
    return lax.dot_general(a, b, (((1,), (0,)), ((), ())), preferred_element_type=F32)


def dot_nt(a, b):
    return lax.dot_general(a, b, (((1,), (1,)), ((), ())), preferred_element_type=F32)


def dot_tn(a, b):
    return lax.dot_general(a, b, (((0,), (0,)), ((), ())), preferred_element_type=F32)


def call(kernel, outs, args, flops, bytes_accessed, smem=0):
    specs = [pl.BlockSpec(memory_space=pltpu.SMEM)] * smem
    specs += [pl.BlockSpec(memory_space=pltpu.VMEM)] * (len(args) - smem)
    return pl.pallas_call(
        kernel,
        out_shape=[jax.ShapeDtypeStruct(s, d) for s, d in outs],
        in_specs=specs,
        out_specs=[pl.BlockSpec(memory_space=pltpu.VMEM)] * len(outs),
        compiler_params=pltpu.CompilerParams(vmem_limit_bytes=VMEM_LIMIT),
        cost_estimate=pl.CostEstimate(
            flops=flops, bytes_accessed=bytes_accessed, transcendentals=0
        ),
    )(*args)


def head_cols(h):
    return slice(h * HEAD, (h + 1) * HEAD)


def local_kernel(k_ref, v_ref, decay_ref, pay_ref, inside_ref, across_ref):
    rows, heads = decay_ref.shape
    per_head = pay_ref.shape[0] // heads
    slab = HEAD // per_head
    decay = decay_ref[...]
    first = lax.broadcasted_iota(jnp.int32, (rows, rows), 0)
    second = lax.broadcasted_iota(jnp.int32, (rows, rows), 1)
    inside = lax.dot_general(
        (first >= second).astype(F32), decay, (((1,), (0,)), ((), ())),
        precision=HIGH, preferred_element_type=F32,
    )
    inside_ref[...] = inside
    across_ref[...] = lax.dot_general(
        decay, (first <= second).astype(F32), (((0,), (0,)), ((), ())),
        precision=HIGH, preferred_element_type=F32,
    )
    totals = inside[rows - 1 : rows, :]
    shares = jnp.exp(totals - inside)
    kept = jnp.exp(totals)
    for h in range(heads):
        key_decayed = (k_ref[:, head_cols(h)].astype(F32) * shares[:, h : h + 1]).astype(BF16)
        state = dot_tn(key_decayed, v_ref[:, head_cols(h)])
        here = slice(h * per_head, (h + 1) * per_head)
        pay_ref[here, 0:slab, :] = state.reshape(per_head, slab, HEAD)
        pay_ref[here, slab : slab + 8, :] = jnp.broadcast_to(
            kept[:, h : h + 1].reshape(1, 1, 1), (per_head, 8, HEAD)
        )


def weights_of(inside_ref, across_ref, h):
    rows = inside_ref.shape[0]
    first = lax.broadcasted_iota(jnp.int32, (rows, rows), 0)
    second = lax.broadcasted_iota(jnp.int32, (rows, rows), 1)
    spread = inside_ref[:, h : h + 1] - across_ref[h : h + 1, :]
    return jnp.exp(jnp.where(first >= second, spread, -1e30))


def mixing_kernel(q_ref, k_ref, v_ref, inside_ref, across_ref, mix_ref, near_ref):
    for h in range(inside_ref.shape[1]):
        cols = head_cols(h)
        scores = dot_nt(q_ref[:, cols], k_ref[:, cols])
        mixing = (scores * weights_of(inside_ref, across_ref, h)).astype(BF16)
        mix_ref[h] = mixing
        near_ref[:, cols] = dot_nn(mixing, v_ref[:, cols])


def forward_scan_kernel(core_ref, own_ref, other_ref, out_ref, kept_ref):
    count, slab = out_ref.shape[0], out_ref.shape[1]

    def run(first_ref, second_ref, second_core):
        state = jnp.zeros((slab // 8, 8, HEAD), F32)
        for j in range(count):
            kept0, kept1 = first_ref[j, slab:, :], second_ref[j, slab:, :]
            kept_ref[j, 0:8, :] = kept0
            kept_ref[j, 8:16, :] = kept1
            middle = kept0 * state + first_ref[j, 0:slab, :].reshape(state.shape)
            out_ref[j] = (middle if second_core else state).reshape(slab, HEAD)
            state = kept1 * middle + second_ref[j, 0:slab, :].reshape(state.shape)

    @pl.when(core_ref[0] == 0)
    def _():
        run(own_ref, other_ref, False)

    @pl.when(core_ref[0] == 1)
    def _():
        run(other_ref, own_ref, True)


def reverse_scan_kernel(core_ref, own_ref, other_ref, kept_ref, out_ref):
    count, slab = out_ref.shape[0], out_ref.shape[1]

    def run(first_ref, second_ref, second_core):
        state = jnp.zeros((slab // 8, 8, HEAD), F32)
        for j in reversed(range(count)):
            middle = kept_ref[j, 8:16, :] * state + second_ref[j].reshape(state.shape)
            out_ref[j] = (state if second_core else middle).reshape(slab, HEAD)
            state = kept_ref[j, 0:8, :] * middle + first_ref[j].reshape(state.shape)

    @pl.when(core_ref[0] == 0)
    def _():
        run(own_ref, other_ref, False)

    @pl.when(core_ref[0] == 1)
    def _():
        run(other_ref, own_ref, True)


def attend_kernel(q_ref, near_ref, state_ref, inside_ref, g_ref, gain_ref, att_ref, sums_ref):
    rows, heads = inside_ref.shape
    grown = jnp.exp(inside_ref[...])
    squares = jnp.zeros((rows, HEAD), F32)
    crossed = jnp.zeros((rows, HEAD), F32)
    for h in range(heads):
        cols = head_cols(h)
        query_decayed = (q_ref[:, cols].astype(F32) * grown[:, h : h + 1]).astype(BF16)
        attended = near_ref[:, cols] + dot_nn(query_decayed, state_ref[h].astype(BF16))
        att_ref[:, cols] = attended
        squares += attended * attended
        crossed += g_ref[:, cols].astype(F32) * gain_ref[:, cols] * attended
    ones = jnp.ones((8, HEAD), F32)
    dims = (((1,), (1,)), ((), ()))
    square_rows = lax.dot_general(ones, squares, dims, precision=HIGH, preferred_element_type=F32)
    cross_rows = lax.dot_general(ones, crossed, dims, precision=HIGH, preferred_element_type=F32)
    which = lax.broadcasted_iota(jnp.int32, (8, rows), 0)
    both = jnp.where(which == 0, square_rows, cross_rows)
    for peer in range(sums_ref.shape[0]):
        sums_ref[peer] = both


def norm_columns(sums_ref, rows):
    whole = jnp.sum(sums_ref[...], axis=0)
    first = lax.broadcasted_iota(jnp.int32, (rows, rows), 0)
    second = lax.broadcasted_iota(jnp.int32, (rows, rows), 1)
    same = first == second
    square_sum = jnp.sum(jnp.where(same, whole[0:1, :], 0.0), axis=1, keepdims=True)
    cross_sum = jnp.sum(jnp.where(same, whole[1:2, :], 0.0), axis=1, keepdims=True)
    width = HEAD_COUNT * HEAD
    inverse = lax.rsqrt(square_sum / width + EPSILON)
    return inverse, inverse * inverse * inverse * (cross_sum / width)


def norm_grad_kernel(sums_ref, att_ref, g_ref, gain_ref, q_ref, inside_ref, gf_ref, pay_ref):
    rows, heads = inside_ref.shape
    per_head = pay_ref.shape[0] // heads
    slab = HEAD // per_head
    inverse, factor = norm_columns(sums_ref, rows)
    grown = jnp.exp(inside_ref[...])
    for h in range(heads):
        cols = head_cols(h)
        scaled = g_ref[:, cols].astype(F32) * gain_ref[:, cols]
        grad_flat = (inverse * scaled - att_ref[:, cols] * factor).astype(BF16)
        gf_ref[:, cols] = grad_flat
        query_decayed = (q_ref[:, cols].astype(F32) * grown[:, h : h + 1]).astype(BF16)
        state = dot_tn(query_decayed, grad_flat)
        pay_ref[h * per_head : (h + 1) * per_head] = state.reshape(per_head, slab, HEAD)


def near_grad_kernel(
    sums_ref, att_ref, gain_ref, gf_ref, q_ref, k_ref, v_ref, mix_ref, state_ref, inside_ref, across_ref,
    normed_ref, gq_ref, gk_ref, gv_ref,
):
    rows, heads = inside_ref.shape
    inverse, _ = norm_columns(sums_ref, rows)
    grown = jnp.exp(inside_ref[...])
    for h in range(heads):
        cols = head_cols(h)
        normed_ref[:, cols] = (att_ref[:, cols] * inverse * gain_ref[:, cols]).astype(BF16)
        grad_flat = gf_ref[:, cols]
        grad_scores = dot_nt(grad_flat, v_ref[:, cols])
        grad_mix = (grad_scores * weights_of(inside_ref, across_ref, h)).astype(BF16)
        far = dot_nt(grad_flat, state_ref[h].astype(BF16))
        gq_ref[:, cols] = (dot_nn(grad_mix, k_ref[:, cols]) + grown[:, h : h + 1] * far).astype(BF16)
        gk_ref[:, cols] = dot_tn(grad_mix, q_ref[:, cols])
        gv_ref[:, cols] = dot_tn(mix_ref[h], grad_flat)


def far_grad_kernel(gk_near_ref, gv_near_ref, k_ref, v_ref, state_ref, inside_ref, gk_ref, gv_ref):
    rows, heads = inside_ref.shape
    inside = inside_ref[...]
    shares = jnp.exp(inside[rows - 1 : rows, :] - inside)
    for h in range(heads):
        cols = head_cols(h)
        share = shares[:, h : h + 1]
        arriving = state_ref[h].astype(BF16)
        far = dot_nt(v_ref[:, cols], arriving)
        gk_ref[:, cols] = (gk_near_ref[:, cols] + share * far).astype(BF16)
        key_decayed = (k_ref[:, cols].astype(F32) * share).astype(BF16)
        gv_ref[:, cols] = (gv_near_ref[:, cols] + dot_nn(key_decayed, arriving)).astype(BF16)


def body(chips, tp_size, queries, key_vectors, values, decay_log, norm_gain, grad_out):
    rows, width = queries.shape
    heads = decay_log.shape[1]
    slab = heads * HEAD // chips
    groups = [[2 * chip + core for chip in range(chips)] for core in range(2)]
    swap = [(i, i ^ 1) for i in range(2 * chips)]
    core = (lax.axis_index("seq") % 2).astype(jnp.int32).reshape(1)
    gain = norm_gain.reshape(1, width)
    wide, tile = (rows, width), (chips, slab, HEAD)
    whole = rows * width

    def across_chips(array):
        return lax.all_to_all(array, "seq", 0, 0, axis_index_groups=groups)

    pay, inside, across = call(
        local_kernel,
        [((chips, slab + 8, HEAD), F32), ((rows, heads), F32), ((heads, rows), F32)],
        [key_vectors, values, decay_log],
        2 * whole * HEAD, 8 * whole,
    )
    mixing, near = call(
        mixing_kernel,
        [((heads, rows, rows), BF16), (wide, F32)],
        [queries, key_vectors, values, inside, across],
        4 * whole * rows, 12 * whole,
    )
    own = across_chips(pay)
    other = lax.ppermute(own, "seq", swap)
    entering_tiles, kept = call(
        forward_scan_kernel,
        [(tile, F32), ((chips, 16, HEAD), F32)],
        [core, own, other],
        4 * heads * HEAD * HEAD, 12 * heads * HEAD * HEAD, smem=1,
    )
    entering = across_chips(entering_tiles).reshape(heads, HEAD, HEAD)
    attended, sums = call(
        attend_kernel,
        [(wide, F32), ((tp_size, 8, rows), F32)],
        [queries, near, entering, inside, grad_out, gain],
        2 * whole * HEAD, 12 * whole,
    )
    sums = lax.all_to_all(sums, "tp", 0, 0)
    grad_flat, pay_back = call(
        norm_grad_kernel,
        [(wide, BF16), (tile, F32)],
        [sums, attended, grad_out, gain, queries, inside],
        2 * whole * HEAD, 12 * whole,
    )
    normed, grad_query, grad_key_near, grad_value_near = call(
        near_grad_kernel,
        [(wide, BF16), (wide, BF16), (wide, F32), (wide, F32)],
        [sums, attended, gain, grad_flat, queries, key_vectors, values, mixing, entering, inside, across],
        10 * whole * rows, 24 * whole,
    )
    own_back = across_chips(pay_back)
    other_back = lax.ppermute(own_back, "seq", swap)
    (arriving_tiles,) = call(
        reverse_scan_kernel,
        [(tile, F32)],
        [core, own_back, other_back, kept],
        4 * heads * HEAD * HEAD, 12 * heads * HEAD * HEAD, smem=1,
    )
    arriving = across_chips(arriving_tiles).reshape(heads, HEAD, HEAD)
    grad_key, grad_value = call(
        far_grad_kernel,
        [(wide, BF16), (wide, BF16)],
        [grad_key_near, grad_value_near, key_vectors, values, arriving, inside],
        4 * whole * HEAD, 16 * whole,
    )
    return normed, grad_query, grad_key, grad_value


def solution(mesh):
    spec = P("seq", "tp")
    return jax.shard_map(
        functools.partial(body, mesh.shape["seq"] // 2, mesh.shape["tp"]),
        mesh=mesh,
        in_specs=(spec, spec, spec, spec, P("tp"), spec),
        out_specs=(spec, spec, spec, spec),
        check_vma=False,
    )
```

time: 495 us -> 138 us (0.28)
  the two profiles are of different devices: /device:TPU:1 before, /device:TPU:8 now
where the time goes in v1:
time: 138 us; the launch traced here: 137 us
  blocking collectives  69.6 us (50%)
  waiting for transfers between devices  32.3 us (23%)
  starting transfers between devices  13.8 us (10%)
  local copies, waits for them, and re-layouts  11 us (8%)
  Pallas kernels  9.66 us (7%)
    all_to_all x2, blocking collectives, across_chips(): return lax.all_to_all(array, 'seq', 0, 0, axis_index_groups=groups)  51.1 us
    all_to_all x2, waiting for transfers between devices, across_chips(): return lax.all_to_all(array, 'seq', 0, 0, axis_index_groups=groups)  28.4 us
    all_to_all x1, blocking collectives, body(): sums = lax.all_to_all(sums, 'tp', 0, 0)  18.5 us
    unnamed x35, local copies, waits for them, and re-layouts  11 us
    all_to_all x2, starting transfers between devices, across_chips(): return lax.all_to_all(array, 'seq', 0, 0, axis_index_groups=groups)  10 us
    pallas_call x8, Pallas kernels, call(): pl.pallas_call(kernel, out_shape=[jax.ShapeDtypeStruct(s, d) for s, d in...  9.66 us
  transfers between devices with their start and end apart: 4, of which 4 were waited for; matrix products, arithmetic and copies ran while one was open for 0% of the time, Pallas kernels for 3%

profile of v1, /device:TPU:8, one launch (start us, length us, event | category | flops | bytes accessed | tf_op | source)
XLA Modules:
  0.0 137.1 jit_solution(4924357875962473867)
XLA Ops:
  0.6 0.8 copy.10.decay_ref
  1.4 1.0 copy-done
  2.4 1.0 copy-done.2
  3.4 1.0 shard_map.93
  4.4 30.2 %all_to_all.25.own_ref = f32[32,40,128]{2,1,0:T(8,128)S(1)} all-to-all(f32[32,40,128]{2,1,0:T(8,128)S(1)} %get-tuple-element.24), channel_id=1, replica_groups={{0,16,32,48,64,80,96,112,128,144,160,176,192,208,224,240,256,272,288,30..., dimensions={0} | all-to-all | bytes 1310720 | tf_op jit(solution)/shard_map/all_to_all | solution.py:232
  34.6 1.9 %collective-permute-start = (f32[32,40,128]{2,1,0:T(8,128)S(1)}, f32[32,40,128]{2,1,0:T(8,128)S(1)}, u32[]{:S(2)}, u32[]{:S(2)}) collective-permute-start(f32[32,40,128]{2,1,0:T(8,128)S(1)} %all_to_all.25.own_ref), channel_id=1, source_target_pairs={{0,8},{8,0},{16,24},{24,16},{32,40},{40,32},{48,56},{56,48},{64,72... | collective-permute-start | bytes 1966088 | tf_op jit(solution)/shard_map/ppermute | solution.py:247
  36.6 2.1 %collective-permute-done.other_ref = f32[32,40,128]{2,1,0:T(8,128)S(1)} collective-permute-done((f32[32,40,128]{2,1,0:T(8,128)S(1)}, f32[32,40,128]{2,1,0:T(8,128)S(1)}, u32[]{:S(2)}, u32[]{:S(2)}) %collective-permute-start) | collective-permute-done | bytes 655392 | tf_op jit(solution)/shard_map/ppermute | solution.py:247
  38.6 0.9 shard_map.95
  39.6 0.7 copy-done.14
  40.3 5.2 %all-to-all-start.1 = ((f32[32,32,128]{2,1,0:T(8,128)}), f32[32,32,128]{2,1,0:T(8,128)S(1)}, u32[]{:S(2)}, u32[]{:S(2)}) async-start(f32[32,32,128]{2,1,0:T(8,128)} %get-tuple-element.25), calls=%async_computation.1 | async-start | bytes 1048576 | tf_op jit(solution)/shard_map/all_to_all | solution.py:232
  45.5 0.0 copy-start.5
  45.5 0.7 shard_map.94
  46.2 0.8 copy-done.10
  47.0 16.3 %all-to-all-done.1 = f32[32,32,128]{2,1,0:T(8,128)S(1)} async-done(((f32[32,32,128]{2,1,0:T(8,128)}), f32[32,32,128]{2,1,0:T(8,128)S(1)}, u32[]{:S(2)}, u32[]{:S(2)}) %all-to-all-start.1) | async-done | bytes 524320 | tf_op jit(solution)/shard_map/all_to_all | solution.py:232
  63.4 1.1 copy-done.11
  64.4 0.7 shard_map.96
  65.2 18.5 %all_to_all.26.sums_ref = f32[8,8,160]{2,1,0:T(8,128)S(1)} all-to-all(f32[8,8,160]{2,1,0:T(8,128)S(1)} %get-tuple-element.26), channel_id=1, replica_groups=mesh['seq'=64,'tp'=8] {'tp'}, dimensions={0} | all-to-all | bytes 81920 | tf_op jit(solution)/shard_map/all_to_all | solution.py:261
  83.7 0.9 shard_map.97
  84.6 0.7 copy-done.12
  85.3 20.9 %all_to_all.27.own_ref = f32[32,32,128]{2,1,0:T(8,128)S(1)} all-to-all(f32[32,32,128]{2,1,0:T(8,128)S(1)} %get-tuple-element.34), channel_id=1, replica_groups={{0,16,32,48,64,80,96,112,128,144,160,176,192,208,224,240,256,272,288,30..., dimensions={0} | all-to-all | bytes 1048576 | tf_op jit(solution)/shard_map/all_to_all | solution.py:232
  106.2 1.9 %collective-permute-start.1 = (f32[32,32,128]{2,1,0:T(8,128)S(1)}, f32[32,32,128]{2,1,0:T(8,128)S(1)}, u32[]{:S(2)}, u32[]{:S(2)}) collective-permute-start(f32[32,32,128]{2,1,0:T(8,128)S(1)} %all_to_all.27.own_ref), channel_id=1, source_target_pairs={{0,8},{8,0},{16,24},{24,16},{32,40},{40,32},{48,56},{56,48},{64,72... | collective-permute-start | bytes 1572872 | tf_op jit(solution)/shard_map/ppermute | solution.py:275
  108.1 1.9 %collective-permute-done.1.other_ref = f32[32,32,128]{2,1,0:T(8,128)S(1)} collective-permute-done((f32[32,32,128]{2,1,0:T(8,128)S(1)}, f32[32,32,128]{2,1,0:T(8,128)S(1)}, u32[]{:S(2)}, u32[]{:S(2)}) %collective-permute-start.1) | collective-permute-done | bytes 524320 | tf_op jit(solution)/shard_map/ppermute | solution.py:275
  110.0 0.9 shard_map.99
  110.9 4.8 %all-to-all-start.4 = ((f32[32,32,128]{2,1,0:T(8,128)}), f32[32,32,128]{2,1,0:T(8,128)S(1)}, u32[]{:S(2)}, u32[]{:S(2)}) async-start(f32[32,32,128]{2,1,0:T(8,128)} %shard_map.99), calls=%async_computation.4 | async-start | bytes 1048576 | tf_op jit(solution)/shard_map/all_to_all | solution.py:232
  115.8 1.0 copy-done.13
  116.7 3.1 %shard_map.98 = (bf16[160,1024]{1,0:T(8,128)(2,1)}, bf16[160,1024]{1,0:T(8,128)(2,1)}, f32[160,1024]{1,0:T(8,128)S(1)}, f32[160,1024]{1,0:T(8,128)S(1)}) custom-call(f32[8,8,160]{2,1,0:T(8,128)S(1)} %all_to_all.26.sums_ref, f32[160,1024]{1,0:T(8,128)S(1)} %get-tuple-element.27.att_ref, f32[1,1024]{1,0:T(1,128)S(1)} %bitcast.9, ...), custom_call_target="tpu_custom_call" | custom-call | flops 262144000 | bytes 3932160 | tf_op jit(solution)/shard_map/pallas_call | solution.py:34
  119.9 0.8 copy-done.6
  120.7 0.9 copy-done.8
  121.6 12.1 %all-to-all-done.4 = f32[32,32,128]{2,1,0:T(8,128)S(1)} async-done(((f32[32,32,128]{2,1,0:T(8,128)}), f32[32,32,128]{2,1,0:T(8,128)S(1)}, u32[]{:S(2)}, u32[]{:S(2)}) %all-to-all-start.4) | async-done | bytes 524320 | tf_op jit(solution)/shard_map/all_to_all | solution.py:232
  133.7 1.1 copy-done.7
  134.8 1.1 copy-done.9
  135.9 1.3 shard_map.100
  (22 shorter events, 0.0 us)
Async XLA Ops:
  1.4 1.0 copy-start
  2.4 1.0 copy-start.2
  34.6 4.0 %collective-permute-start = (f32[32,40,128]{2,1,0:T(8,128)S(1)}, f32[32,40,128]{2,1,0:T(8,128)S(1)}, u32[]{:S(2)}, u32[]{:S(2)}) collective-permute-start(f32[32,40,128]{2,1,0:T(8,128)S(1)} %all_to_all.25.own_ref), channel_id=1, source_target_pairs={{0,8},{8,0},{16,24},{24,16},{32,40},{40,32},{48,56},{56,48},{64,72... | collective-permute-start | bytes 1966088 | tf_op jit(solution)/shard_map/ppermute | solution.py:247
  39.5 0.7 copy-start.14
  40.3 5.2 %copy-start.1 = (bf16[160,1024]{1,0:T(8,128)(2,1)S(1)}, bf16[160,1024]{1,0:T(8,128)(2,1)}, u32[]{:S(2)}) copy-start(bf16[160,1024]{1,0:T(8,128)(2,1)} %k_ref.7) | copy-start | bytes 983044
  40.3 5.2 %copy-start.3 = (bf16[160,1024]{1,0:T(8,128)(2,1)S(1)}, bf16[160,1024]{1,0:T(8,128)(2,1)}, u32[]{:S(2)}) copy-start(bf16[160,1024]{1,0:T(8,128)(2,1)} %v_ref.7) | copy-start | bytes 983044
  40.3 5.2 %copy-start.4 = (bf16[160,1024]{1,0:T(8,128)(2,1)S(1)}, bf16[160,1024]{1,0:T(8,128)(2,1)}, u32[]{:S(2)}) copy-start(bf16[160,1024]{1,0:T(8,128)(2,1)} %q_ref.7) | copy-start | bytes 983044
  40.3 23.1 %all-to-all-start.1 = ((f32[32,32,128]{2,1,0:T(8,128)}), f32[32,32,128]{2,1,0:T(8,128)S(1)}, u32[]{:S(2)}, u32[]{:S(2)}) async-start(f32[32,32,128]{2,1,0:T(8,128)} %get-tuple-element.25), calls=%async_computation.1 | async-start | bytes 1048576 | tf_op jit(solution)/shard_map/all_to_all | solution.py:232
  45.5 17.9 %copy-start.5 = (bf16[160,1024]{1,0:T(8,128)(2,1)S(1)}, bf16[160,1024]{1,0:T(8,128)(2,1)}, u32[]{:S(2)}) copy-start(bf16[160,1024]{1,0:T(8,128)(2,1)} %g_ref.3) | copy-start | bytes 983044
  46.2 0.8 copy-start.10
  47.0 16.3 %copy-start.16 = (f32[1024]{0:T(1024)S(1)}, f32[1024]{0:T(1024)}, u32[]{:S(2)}) copy-start(f32[1024]{0:T(1024)} %param.10) | copy-start | bytes 12292
  63.4 1.1 copy-start.11
  84.6 0.7 copy-start.12
  85.3 24.7 %copy-start.15 = (f32[32,16,128]{2,1,0:T(8,128)S(1)}, f32[32,16,128]{2,1,0:T(8,128)}, u32[]{:S(2)}) copy-start(f32[32,16,128]{2,1,0:T(8,128)} %copy-done.14) | copy-start | bytes 786436
  106.2 3.8 %collective-permute-start.1 = (f32[32,32,128]{2,1,0:T(8,128)S(1)}, f32[32,32,128]{2,1,0:T(8,128)S(1)}, u32[]{:S(2)}, u32[]{:S(2)}) collective-permute-start(f32[32,32,128]{2,1,0:T(8,128)S(1)} %all_to_all.27.own_ref), channel_id=1, source_target_pairs={{0,8},{8,0},{16,24},{24,16},{32,40},{40,32},{48,56},{56,48},{64,72... | collective-permute-start | bytes 1572872 | tf_op jit(solution)/shard_map/ppermute | solution.py:275
  110.9 22.8 %all-to-all-start.4 = ((f32[32,32,128]{2,1,0:T(8,128)}), f32[32,32,128]{2,1,0:T(8,128)S(1)}, u32[]{:S(2)}, u32[]{:S(2)}) async-start(f32[32,32,128]{2,1,0:T(8,128)} %shard_map.99), calls=%async_computation.4 | async-start | bytes 1048576 | tf_op jit(solution)/shard_map/all_to_all | solution.py:232
  115.8 1.0 copy-start.13
  119.9 0.8 copy-start.6
  120.7 0.9 copy-start.8
  133.7 1.1 copy-start.7
  134.8 1.1 copy-start.9

commit v2 on v1

v2 whole, which is shorter than its diff:
```python
import functools

import jax
import jax.numpy as jnp
from jax import lax
from jax.experimental import pallas as pl
from jax.experimental.pallas import tpu as pltpu
from jax.sharding import Mesh
from jax.sharding import PartitionSpec as P

HEAD_COUNT = 64
HEAD = 128
EPSILON = 1e-06
HIGH = lax.Precision.HIGHEST
F32 = jnp.float32
BF16 = jnp.bfloat16
VMEM_LIMIT = 16 * 1024 * 1024
NN = (((1,), (0,)), ((), ()))
NT = (((1,), (1,)), ((), ()))
TN = (((0,), (0,)), ((), ()))


def dot(a, b, dims, precision=None):
    return lax.dot_general(a, b, dims, precision=precision, preferred_element_type=F32)


def call(kernel, outs, args, flops, bytes_accessed, smem=0, hbm=0, scratch=()):
    specs = [pl.BlockSpec(memory_space=pltpu.SMEM)] * smem
    specs += [pl.BlockSpec(memory_space=pltpu.HBM)] * hbm
    specs += [pl.BlockSpec(memory_space=pltpu.VMEM)] * (len(args) - smem - hbm)
    return pl.pallas_call(
        kernel,
        out_shape=[jax.ShapeDtypeStruct(s, d) for s, d in outs],
        in_specs=specs,
        out_specs=[pl.BlockSpec(memory_space=pltpu.VMEM)] * len(outs),
        scratch_shapes=list(scratch),
        compiler_params=pltpu.CompilerParams(vmem_limit_bytes=VMEM_LIMIT),
        cost_estimate=pl.CostEstimate(
            flops=flops, bytes_accessed=bytes_accessed, transcendentals=0
        ),
    )(*args)


def head_cols(h):
    return slice(h * HEAD, (h + 1) * HEAD)


def head_rows(h):
    return slice(h * HEAD, (h + 1) * HEAD)


def local_kernel(k_hbm, v_hbm, decay_ref, pay_ref, kept_ref, inside_ref, across_ref, k_ref, v_ref, sems):
    heads, rows = decay_ref.shape
    copies = [
        pltpu.make_async_copy(k_hbm, k_ref, sems.at[0]),
        pltpu.make_async_copy(v_hbm, v_ref, sems.at[1]),
    ]
    for copy in copies:
        copy.start()
    decay = decay_ref[...]
    first = lax.broadcasted_iota(jnp.int32, (rows, rows), 0)
    second = lax.broadcasted_iota(jnp.int32, (rows, rows), 1)
    inside = dot((first >= second).astype(F32), decay, NT, HIGH)
    across = dot(decay, (first <= second).astype(F32), NN, HIGH)
    inside_ref[...] = inside
    across_ref[...] = across
    shares = jnp.exp(inside[rows - 1 : rows, :] - inside)
    kept = jnp.broadcast_to(jnp.exp(across[:, rows - 1 : rows]), (heads, HEAD))
    kept_ref[...] = kept
    pay_ref[heads * HEAD :, :] = kept
    for copy in copies:
        copy.wait()
    for h in range(heads):
        key_decayed = (k_ref[:, head_cols(h)].astype(F32) * shares[:, h : h + 1]).astype(BF16)
        pay_ref[head_rows(h), :] = dot(key_decayed, v_ref[:, head_cols(h)], TN)


def forward_join_kernel(core_ref, own_ref, other_ref, pay_ref):
    half = pay_ref.shape[0] // 17 * 16 // HEAD
    core = core_ref[0]
    base = pl.multiple_of(core * half * HEAD, half * HEAD)
    kept_own = own_ref[2 * half * HEAD :, :]
    kept_other = other_ref[2 * half * HEAD :, :]
    kept_both = kept_own * kept_other
    kept_second = jnp.where(core == 0, kept_other, kept_own)

    def half_of(rows, i):
        return jnp.where(core == 0, rows[i : i + 1], rows[half + i : half + i + 1])

    for i in range(half):
        here = pl.ds(base + i * HEAD, HEAD)
        own, other = own_ref[here, :], other_ref[here, :]
        first = jnp.where(core == 0, own, other)
        second = jnp.where(core == 0, other, own)
        joined = half_of(kept_second, i) * first + second
        kept = half_of(kept_both, i)
        for part in range(8):
            at = 17 * (8 * i + part)
            pay_ref[at : at + 16, :] = joined[16 * part : 16 * part + 16]
            pay_ref[at + 16 : at + 17, :] = kept


def forward_scan_kernel(got_ref, out_ref, kept_ref):
    count = out_ref.shape[0]
    state = jnp.zeros(out_ref.shape[1:], F32)
    for j in range(count):
        out_ref[j] = state
        kept = got_ref[17 * j + 16 : 17 * j + 17, :]
        kept_ref[j : j + 1, :] = kept
        state = kept * state + got_ref[17 * j : 17 * j + 16, :]


def reverse_join_kernel(core_ref, own_ref, other_ref, kept_own_ref, got_ref, out_ref):
    half = own_ref.shape[0] // HEAD // 2
    core = core_ref[0]
    base = pl.multiple_of(core * half * HEAD, half * HEAD)
    kept_first = jnp.where(core == 0, kept_own_ref[...], got_ref[2 * half * HEAD :, :])
    for i in range(half):
        here = pl.ds(base + i * HEAD, HEAD)
        own, other = own_ref[here, :], other_ref[here, :]
        first = jnp.where(core == 0, own, other)
        second = jnp.where(core == 0, other, own)
        kept = jnp.where(core == 0, kept_first[i : i + 1], kept_first[half + i : half + i + 1])
        out_ref[head_rows(i), :] = first + kept * second


def reverse_scan_kernel(got_ref, kept_ref, out_ref):
    count = out_ref.shape[0]
    state = jnp.zeros(out_ref.shape[1:], F32)
    for j in reversed(range(count)):
        out_ref[j] = state
        state = kept_ref[j : j + 1, :] * state + got_ref[j]


def weights_of(inside_ref, across_ref, h):
    rows = inside_ref.shape[0]
    first = lax.broadcasted_iota(jnp.int32, (rows, rows), 0)
    second = lax.broadcasted_iota(jnp.int32, (rows, rows), 1)
    spread = inside_ref[:, h : h + 1] - across_ref[h : h + 1, :]
    return jnp.exp(jnp.where(first >= second, spread, -1e30))


def mixing_kernel(q_ref, k_ref, inside_ref, across_ref, mix_ref):
    for h in range(inside_ref.shape[1]):
        cols = head_cols(h)
        scores = dot(q_ref[:, cols], k_ref[:, cols], NT)
        mix_ref[h] = (scores * weights_of(inside_ref, across_ref, h)).astype(BF16)


def attend_kernel(
    core_ref, q_ref, v_ref, mix_ref, half_ref, half_other_ref, got_ref, inside_ref, g_ref, gain_ref,
    att_ref, sums_ref, state_ref,
):
    rows, heads = inside_ref.shape
    half = heads // 2
    core = core_ref[0]
    state_ref[pl.ds(core * half, half)] = half_ref[...]
    state_ref[pl.ds((1 - core) * half, half)] = half_other_ref[...]

    @pl.when(core == 1)
    def _():
        for h in range(heads):
            kept = got_ref[heads * HEAD + h : heads * HEAD + h + 1, :]
            state_ref[h] = kept * state_ref[h] + got_ref[head_rows(h), :]

    grown = jnp.exp(inside_ref[...])
    squares = jnp.zeros((rows, HEAD), F32)
    crossed = jnp.zeros((rows, HEAD), F32)
    for h in range(heads):
        cols = head_cols(h)
        query_decayed = (q_ref[:, cols].astype(F32) * grown[:, h : h + 1]).astype(BF16)
        attended = dot(mix_ref[h], v_ref[:, cols], NN) + dot(query_decayed, state_ref[h].astype(BF16), NN)
        att_ref[:, cols] = attended
        squares += attended * attended
        crossed += g_ref[:, cols].astype(F32) * gain_ref[:, cols] * attended
    ones = jnp.ones((8, HEAD), F32)
    square_rows = dot(ones, squares, NT, HIGH)
    cross_rows = dot(ones, crossed, NT, HIGH)
    which = lax.broadcasted_iota(jnp.int32, (8, rows), 0)
    both = jnp.where(which == 0, square_rows, cross_rows)
    for peer in range(sums_ref.shape[0]):
        sums_ref[peer] = both


def norm_columns(sums_ref, rows):
    whole = jnp.sum(sums_ref[...], axis=0)
    first = lax.broadcasted_iota(jnp.int32, (rows, rows), 0)
    second = lax.broadcasted_iota(jnp.int32, (rows, rows), 1)
    same = first == second
    square_sum = jnp.sum(jnp.where(same, whole[0:1, :], 0.0), axis=1, keepdims=True)
    cross_sum = jnp.sum(jnp.where(same, whole[1:2, :], 0.0), axis=1, keepdims=True)
    width = HEAD_COUNT * HEAD
    inverse = lax.rsqrt(square_sum / width + EPSILON)
    return inverse, inverse * inverse * inverse * (cross_sum / width)


def grad_flat_of(inverse, factor, att_ref, g_ref, gain_ref, cols):
    scaled = g_ref[:, cols].astype(F32) * gain_ref[:, cols]
    return (inverse * scaled - att_ref[:, cols] * factor).astype(BF16)


def norm_grad_kernel(sums_ref, att_ref, g_ref, gain_ref, q_ref, inside_ref, pay_ref):
    rows, heads = inside_ref.shape
    inverse, factor = norm_columns(sums_ref, rows)
    grown = jnp.exp(inside_ref[...])
    for h in range(heads):
        cols = head_cols(h)
        grad_flat = grad_flat_of(inverse, factor, att_ref, g_ref, gain_ref, cols)
        query_decayed = (q_ref[:, cols].astype(F32) * grown[:, h : h + 1]).astype(BF16)
        pay_ref[head_rows(h), :] = dot(query_decayed, grad_flat, TN)


def near_grad_kernel(
    sums_ref, att_ref, g_ref, gain_ref, q_ref, k_ref, v_ref, mix_ref, state_ref, inside_ref, across_ref,
    normed_ref, gq_ref, gk_ref, gv_ref,
):
    rows, heads = inside_ref.shape
    inverse, factor = norm_columns(sums_ref, rows)
    grown = jnp.exp(inside_ref[...])
    for h in range(heads):
        cols = head_cols(h)
        normed_ref[:, cols] = (att_ref[:, cols] * inverse * gain_ref[:, cols]).astype(BF16)
        grad_flat = grad_flat_of(inverse, factor, att_ref, g_ref, gain_ref, cols)
        grad_scores = dot(grad_flat, v_ref[:, cols], NT)
        grad_mix = (grad_scores * weights_of(inside_ref, across_ref, h)).astype(BF16)
        far = dot(grad_flat, state_ref[h].astype(BF16), NT)
        gq_ref[:, cols] = (dot(grad_mix, k_ref[:, cols], NN) + grown[:, h : h + 1] * far).astype(BF16)
        gk_ref[:, cols] = dot(grad_mix, q_ref[:, cols], TN)
        gv_ref[:, cols] = dot(mix_ref[h], grad_flat, TN)


def far_grad_kernel(
    core_ref, gk_near_ref, gv_near_ref, k_ref, v_ref, half_ref, half_other_ref, other_ref, kept_got_ref,
    inside_ref, gk_ref, gv_ref, state_ref,
):
    rows, heads = inside_ref.shape
    half = heads // 2
    core = core_ref[0]
    state_ref[pl.ds(core * half, half)] = half_ref[...]
    state_ref[pl.ds((1 - core) * half, half)] = half_other_ref[...]

    @pl.when(core == 0)
    def _():
        for h in range(heads):
            kept = kept_got_ref[heads * HEAD + h : heads * HEAD + h + 1, :]
            state_ref[h] = kept * state_ref[h] + other_ref[head_rows(h), :]

    inside = inside_ref[...]
    shares = jnp.exp(inside[rows - 1 : rows, :] - inside)
    for h in range(heads):
        cols = head_cols(h)
        share = shares[:, h : h + 1]
        arriving = state_ref[h].astype(BF16)
        far = dot(v_ref[:, cols], arriving, NT)
        gk_ref[:, cols] = (gk_near_ref[:, cols] + share * far).astype(BF16)
        key_decayed = (k_ref[:, cols].astype(F32) * share).astype(BF16)
        gv_ref[:, cols] = (gv_near_ref[:, cols] + dot(key_decayed, arriving, NN)).astype(BF16)


def body(chips, tp_size, queries, key_vectors, values, decay_log, norm_gain, grad_out):
    rows, width = queries.shape
    heads = decay_log.shape[1]
    half = heads // 2
    slab = half * HEAD // chips
    core = lax.axis_index("core").astype(jnp.int32).reshape(1)
    gain = norm_gain.reshape(1, width)
    wide, tile = (rows, width), (chips, slab, HEAD)
    state_rows, half_state = (heads * HEAD, HEAD), (half, HEAD, HEAD)
    whole, size = rows * width, heads * HEAD * HEAD

    def across_chips(array):
        return lax.all_to_all(array, ("x", "y"), 0, 0)

    def swap(array):
        return lax.ppermute(array, "core", [(0, 1), (1, 0)])

    own, kept_own, inside, across = call(
        local_kernel,
        [((heads * HEAD + heads, HEAD), F32), ((heads, HEAD), F32), ((rows, heads), F32), ((heads, rows), F32)],
        [key_vectors, values, decay_log.T],
        2 * whole * HEAD, 8 * whole, hbm=2,
        scratch=[pltpu.VMEM(wide, BF16), pltpu.VMEM(wide, BF16), pltpu.SemaphoreType.DMA((2,))],
    )
    (mixing,) = call(
        mixing_kernel,
        [((heads, rows, rows), BF16)],
        [queries, key_vectors, inside, across],
        2 * whole * rows, 12 * whole,
    )
    got = swap(own)
    (pay,) = call(
        forward_join_kernel,
        [((chips * (slab + 1), HEAD), F32)],
        [core, own, got],
        2 * size, 12 * size, smem=1,
    )
    pay = across_chips(pay.reshape(chips, 1, (slab + 1) * HEAD)).reshape(chips * (slab + 1), HEAD)
    tiles, kept_chips = call(
        forward_scan_kernel,
        [(tile, F32), ((chips, HEAD), F32)],
        [pay],
        size, 4 * size,
    )
    half_in = across_chips(tiles).reshape(half_state)
    half_other = swap(half_in)
    attended, sums, entering = call(
        attend_kernel,
        [(wide, F32), ((tp_size, 8, rows), F32), ((heads, HEAD, HEAD), F32)],
        [core, queries, values, mixing, half_in, half_other, got, inside, grad_out, gain],
        2 * whole * (HEAD + rows), 12 * whole, smem=1,
    )
    sums = lax.all_to_all(sums, "tp", 0, 0)
    (back,) = call(
        norm_grad_kernel,
        [(state_rows, F32)],
        [sums, attended, grad_out, gain, queries, inside],
        2 * whole * HEAD, 12 * whole,
    )
    back_other = swap(back)
    normed, grad_query, grad_key_near, grad_value_near = call(
        near_grad_kernel,
        [(wide, BF16), (wide, BF16), (wide, F32), (wide, F32)],
        [sums, attended, grad_out, gain, queries, key_vectors, values, mixing, entering, inside, across],
        10 * whole * rows, 24 * whole,
    )
    (pay_back,) = call(
        reverse_join_kernel,
        [((half * HEAD, HEAD), F32)],
        [core, back, back_other, kept_own, got],
        2 * size, 12 * size, smem=1,
    )
    (tiles_back,) = call(
        reverse_scan_kernel,
        [(tile, F32)],
        [across_chips(pay_back.reshape(tile)), kept_chips],
        size, 4 * size,
    )
    half_back = across_chips(tiles_back).reshape(half_state)
    half_back_other = swap(half_back)
    grad_key, grad_value = call(
        far_grad_kernel,
        [(wide, BF16), (wide, BF16)],
        [
            core, grad_key_near, grad_value_near, key_vectors, values,
            half_back, half_back_other, back_other, got, inside,
        ],
        4 * whole * HEAD, 16 * whole, smem=1,
        scratch=[pltpu.VMEM((heads, HEAD, HEAD), F32)],
    )
    return normed, grad_query, grad_key, grad_value


def solution(mesh):
    seq, tp = mesh.shape["seq"], mesh.shape["tp"]
    fine = Mesh(mesh.devices.reshape(seq // 16, 8, 2, tp), ("x", "y", "core", "tp"))
    spec = P(("x", "y", "core"), "tp")
    return jax.shard_map(
        functools.partial(body, seq // 2, tp),
        mesh=fine,
        in_specs=(spec, spec, spec, spec, P("tp"), spec),
        out_specs=(spec, spec, spec, spec),
        check_vma=False,
    )
```

time: 138 us -> 117 us (0.85)
  the two profiles are of different devices: /device:TPU:8 before, /device:TPU:1 now
where the time goes in v2:
time: 117 us; the launch traced here: 116 us
  blocking collectives  77.6 us (66%)
  starting transfers between devices  23.4 us (20%)
  Pallas kernels  8.29 us (7%)
  waiting for transfers between devices  3.74 us (3%)
  local copies, waits for them, and re-layouts  2.66 us (2%)
    all_to_all x4, blocking collectives, across_chips(): return lax.all_to_all(array, ('x', 'y'), 0, 0)  60.5 us
    ppermute x4, starting transfers between devices, swap(): return lax.ppermute(array, 'core', [(0, 1), (1, 0)])  23.4 us
    all_to_all x1, blocking collectives, body(): sums = lax.all_to_all(sums, 'tp', 0, 0)  17.1 us
    pallas_call x10, Pallas kernels, call(): pl.pallas_call(kernel, out_shape=[jax.ShapeDtypeStruct(s, d) for s, d in...  8.29 us
    ppermute x4, waiting for transfers between devices, swap(): return lax.ppermute(array, 'core', [(0, 1), (1, 0)])  3.74 us
    unnamed x16, local copies, waits for them, and re-layouts  2.66 us
  transfers between devices with their start and end apart: 4, of which 3 were waited for; matrix products, arithmetic and copies ran while one was open for 0% of the time, Pallas kernels for 3%

profile of v2, /device:TPU:1, one launch (start us, length us, event | category | flops | bytes accessed | tf_op | source)
XLA Modules:
  0.0 116.5 jit_solution(11784800062884417732)
XLA Ops:
  0.6 0.0 copy-start
  0.6 1.0 copy-done
  1.6 1.0 copy-done.2
  2.6 0.7 copy-done.7
  3.3 1.2 %shard_map.93 = (f32[1032,128]{1,0:T(8,128)S(1)}, f32[8,128]{1,0:T(8,128)S(1)}, f32[160,8]{1,0:T(8,128)S(1)}, f32[8,160]{1,0:T(8,128)S(1)}) custom-call(bf16[160,1024]{1,0:T(8,128)(2,1)S(1)} %copy-done.2, bf16[160,1024]{1,0:T(8,128)(2,1)S(1)} %copy-done, f32[8,160]{1,0:T(8,128)S(1)} %bitcast.18), custom_call_target="tpu_custom_call" | custom-call | flops 41943040 | bytes 1310720 | tf_op jit(solution)/shard_map/pallas_call | solution.py:31
  4.5 8.8 %collective-permute-start = (f32[1032,128]{1,0:T(8,128)S(1)}, f32[1032,128]{1,0:T(8,128)S(1)}, u32[]{:S(2)}, u32[]{:S(2)}) collective-permute-start(f32[1032,128]{1,0:T(8,128)S(1)} %get-tuple-element.21.own_ref), channel_id=1, source_target_pairs={{0,8},{8,0},{1,9},{9,1},{2,10},{10,2},{3,11},{11,3},{4,12},{12,4},... | collective-permute-start | bytes 1585160 | tf_op jit(solution)/shard_map/ppermute | solution.py:275
  13.3 1.5 %collective-permute-done.other_ref.got_ref.kept_got_ref = f32[1032,128]{1,0:T(8,128)S(1)} collective-permute-done((f32[1032,128]{1,0:T(8,128)S(1)}, f32[1032,128]{1,0:T(8,128)S(1)}, u32[]{:S(2)}, u32[]{:S(2)}) %collective-permute-start) | collective-permute-done | bytes 528416 | tf_op jit(solution)/shard_map/ppermute | solution.py:275
  14.9 13.8 %all_to_all.25 = f32[32,1,2176]{2,1,0:T(1,128)S(1)} all-to-all(f32[32,1,2176]{2,1,0:T(1,128)S(1)} %bitcast.8), channel_id=1, replica_groups=mesh['x'=4,'y'=8,'core'=2,'tp'=8] {'x','y'}, dimensions={0} | all-to-all | bytes 557056 | tf_op jit(solution)/shard_map/all_to_all | solution.py:272
  28.7 0.1 shard_map.96
  28.8 16.8 %all_to_all.26 = f32[32,16,128]{2,1,0:T(8,128)S(1)} all-to-all(f32[32,16,128]{2,1,0:T(8,128)S(1)} %get-tuple-element.22), channel_id=1, replica_groups=mesh['x'=4,'y'=8,'core'=2,'tp'=8] {'x','y'}, dimensions={0} | all-to-all | bytes 524288 | tf_op jit(solution)/shard_map/all_to_all | solution.py:272
  45.6 5.5 %collective-permute-start.1 = (f32[4,128,128]{2,1,0:T(8,128)S(1)}, f32[4,128,128]{2,1,0:T(8,128)S(1)}, u32[]{:S(2)}, u32[]{:S(2)}) collective-permute-start(f32[4,128,128]{2,1,0:T(8,128)S(1)} %bitcast.12), channel_id=1, source_target_pairs={{0,8},{8,0},{1,9},{9,1},{2,10},{10,2},{3,11},{11,3},{4,12},{12,4},... | collective-permute-start | bytes 786440 | tf_op jit(solution)/shard_map/ppermute | solution.py:275
  51.1 0.0 copy-done.4
  51.1 0.0 copy-done.3
  51.1 0.0 copy-start.1
  51.1 0.0 copy-start.5
  51.1 0.0 copy-start.6
  51.1 0.4 shard_map.94.mix_ref
  51.5 0.7 collective-permute-done.1.half_other_ref
  52.2 0.0 copy-done.1
  52.2 0.0 copy-done.5
  52.2 0.9 shard_map.97
  53.2 17.1 %all_to_all.27.sums_ref = f32[8,8,160]{2,1,0:T(8,128)S(1)} all-to-all(f32[8,8,160]{2,1,0:T(8,128)S(1)} %get-tuple-element.23), channel_id=1, replica_groups=mesh['x'=4,'y'=8,'core'=2,'tp'=8] {'tp'}, dimensions={0} | all-to-all | bytes 81920 | tf_op jit(solution)/shard_map/all_to_all | solution.py:312
  70.3 0.9 shard_map.99.own_ref
  71.1 3.6 %collective-permute-start.2 = (f32[1024,128]{1,0:T(8,128)S(1)}, f32[1024,128]{1,0:T(8,128)S(1)}, u32[]{:S(2)}, u32[]{:S(2)}) collective-permute-start(f32[1024,128]{1,0:T(8,128)S(1)} %shard_map.99.own_ref), channel_id=1, source_target_pairs={{0,8},{8,0},{1,9},{9,1},{2,10},{10,2},{3,11},{11,3},{4,12},{12,4},... | collective-permute-start | bytes 1572872 | tf_op jit(solution)/shard_map/ppermute | solution.py:275
  74.8 1.5 %collective-permute-done.2.other_ref = f32[1024,128]{1,0:T(8,128)S(1)} collective-permute-done((f32[1024,128]{1,0:T(8,128)S(1)}, f32[1024,128]{1,0:T(8,128)S(1)}, u32[]{:S(2)}, u32[]{:S(2)}) %collective-permute-start.2) | collective-permute-done | bytes 524320 | tf_op jit(solution)/shard_map/ppermute | solution.py:275
  76.3 13.7 %all_to_all.28.got_ref = f32[32,16,128]{2,1,0:T(8,128)S(1)} all-to-all(f32[32,16,128]{2,1,0:T(8,128)S(1)} %bitcast.14), channel_id=1, replica_groups=mesh['x'=4,'y'=8,'core'=2,'tp'=8] {'x','y'}, dimensions={0} | all-to-all | bytes 524288 | tf_op jit(solution)/shard_map/all_to_all | solution.py:272
  90.1 0.1 shard_map.101
  90.1 16.2 %all_to_all.29 = f32[32,16,128]{2,1,0:T(8,128)S(1)} all-to-all(f32[32,16,128]{2,1,0:T(8,128)S(1)} %shard_map.101), channel_id=1, replica_groups=mesh['x'=4,'y'=8,'core'=2,'tp'=8] {'x','y'}, dimensions={0} | all-to-all | bytes 524288 | tf_op jit(solution)/shard_map/all_to_all | solution.py:272
  106.3 5.5 %collective-permute-start.3 = (f32[4,128,128]{2,1,0:T(8,128)S(1)}, f32[4,128,128]{2,1,0:T(8,128)S(1)}, u32[]{:S(2)}, u32[]{:S(2)}) collective-permute-start(f32[4,128,128]{2,1,0:T(8,128)S(1)} %bitcast.10), channel_id=1, source_target_pairs={{0,8},{8,0},{1,9},{9,1},{2,10},{10,2},{3,11},{11,3},{4,12},{12,4},... | collective-permute-start | bytes 786440 | tf_op jit(solution)/shard_map/ppermute | solution.py:275
  111.8 3.3 %shard_map.98 = (bf16[160,1024]{1,0:T(8,128)(2,1)}, bf16[160,1024]{1,0:T(8,128)(2,1)}, f32[160,1024]{1,0:T(8,128)S(1)}, f32[160,1024]{1,0:T(8,128)S(1)}) custom-call(f32[8,8,160]{2,1,0:T(8,128)S(1)} %all_to_all.27.sums_ref, f32[160,1024]{1,0:T(8,128)S(1)} %get-tuple-element.24.att_ref, bf16[160,1024]{1,0:T(8,128)(2,1)S(1)} %copy-done.5, ...), custom_call_target="tpu_custom_call" | custom-call | flops 262144000 | bytes 3932160 | tf_op jit(solution)/shard_map/pallas_call | solution.py:31
  115.1 0.0 collective-permute-done.3.half_other_ref
  115.1 1.3 %shard_map.102 = (bf16[160,1024]{1,0:T(8,128)(2,1)}, bf16[160,1024]{1,0:T(8,128)(2,1)}) custom-call(s32[1]{0:T(128)} %bitcast.core_ref, f32[160,1024]{1,0:T(8,128)S(1)} %get-tuple-element.28.gk_near_ref, f32[160,1024]{1,0:T(8,128)S(1)} %get-tuple-element.29.gv_near_ref, bf16[160,1024]{1,0:T(8,128)(2,1)S(1)} %copy-done.3, bf16[160,1024]{1,0:T(8,128)(2,1)S(1)} %copy-done.1, ...), custom_call_target="tpu_custom_call" | custom-call | flops 83886080 | bytes 2621440 | tf_op jit(solution)/shard_map/pallas_call | solution.py:31
  (7 shorter events, 0.1 us)
Async XLA Ops:
  0.6 1.0 copy-start
  1.6 1.0 copy-start.2
  2.6 0.7 copy-start.7
  4.5 10.3 %collective-permute-start = (f32[1032,128]{1,0:T(8,128)S(1)}, f32[1032,128]{1,0:T(8,128)S(1)}, u32[]{:S(2)}, u32[]{:S(2)}) collective-permute-start(f32[1032,128]{1,0:T(8,128)S(1)} %get-tuple-element.21.own_ref), channel_id=1, source_target_pairs={{0,8},{8,0},{1,9},{9,1},{2,10},{10,2},{3,11},{11,3},{4,12},{12,4},... | collective-permute-start | bytes 1585160 | tf_op jit(solution)/shard_map/ppermute | solution.py:275
  28.7 22.3 %copy-start.4 = (bf16[160,1024]{1,0:T(8,128)(2,1)S(1)}, bf16[160,1024]{1,0:T(8,128)(2,1)}, u32[]{:S(2)}) copy-start(bf16[160,1024]{1,0:T(8,128)(2,1)} %q_ref.7) | copy-start | bytes 983044
  28.8 22.3 %copy-start.3 = (bf16[160,1024]{1,0:T(8,128)(2,1)S(1)}, bf16[160,1024]{1,0:T(8,128)(2,1)}, u32[]{:S(2)}) copy-start(bf16[160,1024]{1,0:T(8,128)(2,1)} %k_ref.5) | copy-start | bytes 983044
  45.6 6.7 %collective-permute-start.1 = (f32[4,128,128]{2,1,0:T(8,128)S(1)}, f32[4,128,128]{2,1,0:T(8,128)S(1)}, u32[]{:S(2)}, u32[]{:S(2)}) collective-permute-start(f32[4,128,128]{2,1,0:T(8,128)S(1)} %bitcast.12), channel_id=1, source_target_pairs={{0,8},{8,0},{1,9},{9,1},{2,10},{10,2},{3,11},{11,3},{4,12},{12,4},... | collective-permute-start | bytes 786440 | tf_op jit(solution)/shard_map/ppermute | solution.py:275
  51.1 1.1 copy-start.1
  51.1 1.1 copy-start.5
  51.1 1.1 copy-start.6
  71.1 5.2 %collective-permute-start.2 = (f32[1024,128]{1,0:T(8,128)S(1)}, f32[1024,128]{1,0:T(8,128)S(1)}, u32[]{:S(2)}, u32[]{:S(2)}) collective-permute-start(f32[1024,128]{1,0:T(8,128)S(1)} %shard_map.99.own_ref), channel_id=1, source_target_pairs={{0,8},{8,0},{1,9},{9,1},{2,10},{10,2},{3,11},{11,3},{4,12},{12,4},... | collective-permute-start | bytes 1572872 | tf_op jit(solution)/shard_map/ppermute | solution.py:275
  106.3 8.8 %collective-permute-start.3 = (f32[4,128,128]{2,1,0:T(8,128)S(1)}, f32[4,128,128]{2,1,0:T(8,128)S(1)}, u32[]{:S(2)}, u32[]{:S(2)}) collective-permute-start(f32[4,128,128]{2,1,0:T(8,128)S(1)} %bitcast.10), channel_id=1, source_target_pairs={{0,8},{8,0},{1,9},{9,1},{2,10},{10,2},{3,11},{11,3},{4,12},{12,4},... | collective-permute-start | bytes 786440 | tf_op jit(solution)/shard_map/ppermute | solution.py:275

commit v3 on v2

v3 whole, which is shorter than its diff:
```python
import functools

import jax
import jax.numpy as jnp
from jax import lax
from jax.experimental import pallas as pl
from jax.experimental.pallas import tpu as pltpu
from jax.sharding import Mesh
from jax.sharding import PartitionSpec as P

HEAD_COUNT = 64
HEAD = 128
EPSILON = 1e-06
HIGH = lax.Precision.HIGHEST
F32 = jnp.float32
BF16 = jnp.bfloat16
VMEM_LIMIT = 20 * 1024 * 1024
NN = (((1,), (0,)), ((), ()))
NT = (((1,), (1,)), ((), ()))
TN = (((0,), (0,)), ((), ()))


def dot(a, b, dims, precision=None):
    return lax.dot_general(a, b, dims, precision=precision, preferred_element_type=F32)


SPACES = {"s": pltpu.SMEM, "h": pltpu.HBM, "v": pltpu.VMEM, "a": pl.ANY}


def call(kernel, outs, args, flops, bytes_accessed, scratch=()):
    return pl.pallas_call(
        kernel,
        out_shape=[SPACES[m](s, d) for m, s, d in outs],
        in_specs=[pl.BlockSpec(memory_space=SPACES[m]) for m, _ in args],
        out_specs=[pl.BlockSpec(memory_space=SPACES[m]) for m, _, _ in outs],
        scratch_shapes=list(scratch),
        compiler_params=pltpu.CompilerParams(vmem_limit_bytes=VMEM_LIMIT),
        cost_estimate=pl.CostEstimate(
            flops=flops, bytes_accessed=bytes_accessed, transcendentals=0
        ),
    )(*[pltpu.with_memory_space_constraint(a, SPACES[m]) if m in "hv" else a for m, a in args])


def head_cols(h):
    return slice(h * HEAD, (h + 1) * HEAD)


def head_rows(h):
    return slice(h * HEAD, (h + 1) * HEAD)


def local_kernel(
    q_hbm, k_hbm, v_hbm, g_hbm, decay_hbm, gain_hbm,
    pay_ref, kept_ref, inside_ref, across_ref, key_ref, q_ref, k_ref, v_ref, g_ref, gain_ref, decay_ref, sems,
):
    heads, rows = decay_ref.shape
    halves = [slice(0, heads // 2 * HEAD), slice(heads // 2 * HEAD, heads * HEAD)]
    pieces = [(decay_hbm, decay_ref)]
    for cols in halves:
        pieces += [(k_hbm.at[:, cols], k_ref.at[:, cols]), (v_hbm.at[:, cols], v_ref.at[:, cols])]
    pieces += [(q_hbm, q_ref), (g_hbm, g_ref), (gain_hbm, gain_ref)]
    copies = [pltpu.make_async_copy(*piece, sems.at[i]) for i, piece in enumerate(pieces)]
    for copy in copies:
        copy.start()
    first = lax.broadcasted_iota(jnp.int32, (rows, rows), 0)
    second = lax.broadcasted_iota(jnp.int32, (rows, rows), 1)
    copies[0].wait()
    decay = decay_ref[...]
    inside = dot((first >= second).astype(F32), decay, NT, HIGH)
    across = dot(decay, (first <= second).astype(F32), NN, HIGH)
    inside_ref[...] = inside
    across_ref[...] = across
    shares = jnp.exp(inside[rows - 1 : rows, :] - inside)
    kept = jnp.broadcast_to(jnp.exp(across[:, rows - 1 : rows]), (heads, HEAD))
    kept_ref[...] = kept
    pay_ref[heads * HEAD :, :] = kept
    for h in range(heads):
        if h == 0 or h == heads // 2:
            at = 1 if h == 0 else 3
            copies[at].wait()
            copies[at + 1].wait()
        cols = head_cols(h)
        key_decayed = (k_ref[:, cols].astype(F32) * shares[:, h : h + 1]).astype(BF16)
        key_ref[:, cols] = key_decayed
        pay_ref[head_rows(h), :] = dot(key_decayed, v_ref[:, cols], TN)
    for copy in copies[5:]:
        copy.wait()


def forward_join_kernel(core_ref, after_ref, own_ref, other_ref, pay_ref):
    half = pay_ref.shape[0] // 17 * 16 // HEAD
    core = core_ref[0]
    base = pl.multiple_of(core * half * HEAD, half * HEAD)
    kept_own = own_ref[2 * half * HEAD :, :]
    kept_other = other_ref[2 * half * HEAD :, :]
    kept_both = kept_own * kept_other
    kept_second = jnp.where(core == 0, kept_other, kept_own)

    def half_of(rows, i):
        return jnp.where(core == 0, rows[i : i + 1], rows[half + i : half + i + 1])

    for i in range(half):
        here = pl.ds(base + i * HEAD, HEAD)
        own, other = own_ref[here, :], other_ref[here, :]
        first = jnp.where(core == 0, own, other)
        second = jnp.where(core == 0, other, own)
        joined = half_of(kept_second, i) * first + second
        kept = half_of(kept_both, i)
        for part in range(8):
            at = 17 * (8 * i + part)
            pay_ref[at : at + 16, :] = joined[16 * part : 16 * part + 16]
            pay_ref[at + 16 : at + 17, :] = kept


def forward_scan_kernel(got_ref, out_ref, kept_ref):
    count = out_ref.shape[0]
    state = jnp.zeros(out_ref.shape[1:], F32)
    for j in range(count):
        out_ref[j] = state
        kept = got_ref[17 * j + 16 : 17 * j + 17, :]
        kept_ref[j : j + 1, :] = kept
        state = kept * state + got_ref[17 * j : 17 * j + 16, :]


def reverse_join_kernel(core_ref, after_hbm, own_ref, other_ref, kept_own_ref, got_ref, out_ref):
    half = own_ref.shape[0] // HEAD // 2
    core = core_ref[0]
    base = pl.multiple_of(core * half * HEAD, half * HEAD)
    kept_first = jnp.where(core == 0, kept_own_ref[...], got_ref[2 * half * HEAD :, :])
    for i in range(half):
        here = pl.ds(base + i * HEAD, HEAD)
        own, other = own_ref[here, :], other_ref[here, :]
        first = jnp.where(core == 0, own, other)
        second = jnp.where(core == 0, other, own)
        kept = jnp.where(core == 0, kept_first[i : i + 1], kept_first[half + i : half + i + 1])
        out_ref[head_rows(i), :] = first + kept * second


def reverse_scan_kernel(got_ref, kept_ref, out_ref):
    count = out_ref.shape[0]
    state = jnp.zeros(out_ref.shape[1:], F32)
    for j in reversed(range(count)):
        out_ref[j] = state
        state = kept_ref[j : j + 1, :] * state + got_ref[j]


def weights_of(inside_ref, across_ref, h, transposed=False):
    rows = inside_ref.shape[0]
    first = lax.broadcasted_iota(jnp.int32, (rows, rows), 0)
    second = lax.broadcasted_iota(jnp.int32, (rows, rows), 1)
    if transposed:
        spread = across_ref[h : h + 1, :] - inside_ref[:, h : h + 1]
        return jnp.exp(jnp.where(second >= first, spread, -1e30))
    spread = inside_ref[:, h : h + 1] - across_ref[h : h + 1, :]
    return jnp.exp(jnp.where(first >= second, spread, -1e30))


def mixing_kernel(
    q_ref, k_ref, v_ref, g_ref, gain_ref, inside_ref, across_ref,
    near_ref, mix_turned_ref, query_ref, query_turned_ref, weights_ref, weights_turned_ref, scaled_ref,
):
    grown = jnp.exp(inside_ref[...])
    for h in range(inside_ref.shape[1]):
        cols = head_cols(h)
        queries, keys = q_ref[:, cols], k_ref[:, cols]
        weights = weights_of(inside_ref, across_ref, h)
        weights_ref[h] = weights
        mixing = (dot(queries, keys, NT) * weights).astype(BF16)
        near_ref[:, cols] = dot(mixing, v_ref[:, cols], NN)
        weights_turned = weights_of(inside_ref, across_ref, h, True)
        weights_turned_ref[h] = weights_turned
        mix_turned_ref[h] = (dot(keys, queries, NT) * weights_turned).astype(BF16)
        decayed = queries.astype(F32) * grown[:, h : h + 1]
        query_ref[:, cols] = decayed.astype(BF16)
        query_turned_ref[h] = decayed.T.astype(BF16)
        scaled_ref[:, cols] = g_ref[:, cols].astype(F32) * gain_ref[:, cols]


def attend_kernel(
    core_ref, near_ref, query_ref, half_ref, half_other_ref, got_ref, scaled_ref,
    att_ref, sums_ref, state_bf_ref, state_ref,
):
    rows, width = near_ref.shape
    heads = width // HEAD
    half = heads // 2
    core = core_ref[0]
    state_ref[pl.ds(core * half, half)] = half_ref[...]
    state_ref[pl.ds((1 - core) * half, half)] = half_other_ref[...]

    @pl.when(core == 1)
    def _():
        for h in range(heads):
            kept = got_ref[heads * HEAD + h : heads * HEAD + h + 1, :]
            state_ref[h] = kept * state_ref[h] + got_ref[head_rows(h), :]

    squares = jnp.zeros((rows, HEAD), F32)
    crossed = jnp.zeros((rows, HEAD), F32)
    for h in range(heads):
        cols = head_cols(h)
        state = state_ref[h].astype(BF16)
        state_bf_ref[h] = state
        attended = near_ref[:, cols] + dot(query_ref[:, cols], state, NN)
        att_ref[:, cols] = attended
        squares += attended * attended
        crossed += scaled_ref[:, cols] * attended
    ones = jnp.ones((8, HEAD), F32)
    square_rows = dot(ones, squares, NT, HIGH)
    cross_rows = dot(ones, crossed, NT, HIGH)
    for peer in range(sums_ref.shape[0]):
        sums_ref[peer, 0:1, :] = square_rows[0:1]
        sums_ref[peer, 1:2, :] = cross_rows[0:1]


def norm_columns(sums_ref, rows):
    whole = jnp.sum(sums_ref[...], axis=0)
    first = lax.broadcasted_iota(jnp.int32, (rows, rows), 0)
    second = lax.broadcasted_iota(jnp.int32, (rows, rows), 1)
    same = first == second
    square_sum = jnp.sum(jnp.where(same, whole[0:1, :], 0.0), axis=1, keepdims=True)
    cross_sum = jnp.sum(jnp.where(same, whole[1:2, :], 0.0), axis=1, keepdims=True)
    width = HEAD_COUNT * HEAD
    inverse = lax.rsqrt(square_sum / width + EPSILON)
    return inverse, inverse * inverse * inverse * (cross_sum / width)


def norm_grad_kernel(sums_ref, att_ref, scaled_ref, query_turned_ref, pay_ref, gf_ref):
    rows, width = att_ref.shape
    inverse, factor = norm_columns(sums_ref, rows)
    for h in range(width // HEAD):
        cols = head_cols(h)
        grad_flat = (inverse * scaled_ref[:, cols] - att_ref[:, cols] * factor).astype(BF16)
        gf_ref[:, cols] = grad_flat
        pay_ref[head_rows(h), :] = dot(query_turned_ref[h], grad_flat, NN)


def send_out(copies, source, target, sems, i, cols):
    copy = pltpu.make_async_copy(source.at[:, cols], target.at[:, cols], sems.at[i])
    copy.start()
    copies.append(copy)


def near_query_kernel(
    sums_ref, att_ref, gain_ref, gf_ref, k_ref, v_ref, state_ref, inside_ref, weights_ref,
    normed_hbm, gq_hbm, normed_ref, gq_ref, sems,
):
    rows, heads = inside_ref.shape
    inverse, _ = norm_columns(sums_ref, rows)
    grown = jnp.exp(inside_ref[...])
    copies = []
    for h in range(heads):
        cols = head_cols(h)
        normed_ref[:, cols] = (att_ref[:, cols] * inverse * gain_ref[:, cols]).astype(BF16)
        grad_flat = gf_ref[:, cols]
        grad_mix = (dot(grad_flat, v_ref[:, cols], NT) * weights_ref[h]).astype(BF16)
        far = dot(grad_flat, state_ref[h], NT)
        gq_ref[:, cols] = (dot(grad_mix, k_ref[:, cols], NN) + grown[:, h : h + 1] * far).astype(BF16)
        if h % 2:
            pair = slice((h - 1) * HEAD, (h + 1) * HEAD)
            send_out(copies, normed_ref, normed_hbm, sems, h - 1, pair)
            send_out(copies, gq_ref, gq_hbm, sems, h, pair)
    for copy in copies:
        copy.wait()


def near_key_kernel(gf_ref, q_ref, v_ref, mix_turned_ref, weights_turned_ref, gk_ref, gv_ref):
    for h in range(mix_turned_ref.shape[0]):
        cols = head_cols(h)
        grad_flat = gf_ref[:, cols]
        turned = (dot(v_ref[:, cols], grad_flat, NT) * weights_turned_ref[h]).astype(BF16)
        gk_ref[:, cols] = dot(turned, q_ref[:, cols], NN)
        gv_ref[:, cols] = dot(mix_turned_ref[h], grad_flat, NN)


def far_grad_kernel(
    core_ref, gk_near_ref, gv_near_ref, key_ref, v_ref, half_ref, half_other_ref, other_ref, kept_got_ref,
    inside_ref, gk_hbm, gv_hbm, state_ref, gk_ref, gv_ref, sems,
):
    rows, heads = inside_ref.shape
    half = heads // 2
    core = core_ref[0]
    state_ref[pl.ds(core * half, half)] = half_ref[...]
    state_ref[pl.ds((1 - core) * half, half)] = half_other_ref[...]

    @pl.when(core == 0)
    def _():
        for h in range(heads):
            kept = kept_got_ref[heads * HEAD + h : heads * HEAD + h + 1, :]
            state_ref[h] = kept * state_ref[h] + other_ref[head_rows(h), :]

    inside = inside_ref[...]
    shares = jnp.exp(inside[rows - 1 : rows, :] - inside)
    copies = []
    for h in range(heads):
        cols = head_cols(h)
        arriving = state_ref[h].astype(BF16)
        far = dot(v_ref[:, cols], arriving, NT)
        gk_ref[:, cols] = (gk_near_ref[:, cols] + shares[:, h : h + 1] * far).astype(BF16)
        gv_ref[:, cols] = (gv_near_ref[:, cols] + dot(key_ref[:, cols], arriving, NN)).astype(BF16)
        if h % 2:
            pair = slice((h - 1) * HEAD, (h + 1) * HEAD)
            send_out(copies, gk_ref, gk_hbm, sems, h - 1, pair)
            send_out(copies, gv_ref, gv_hbm, sems, h, pair)
    for copy in copies:
        copy.wait()


def body(chips, tp_size, queries, key_vectors, values, decay_log, norm_gain, grad_out):
    rows, width = queries.shape
    heads = decay_log.shape[1]
    half = heads // 2
    slab = half * HEAD // chips
    core = lax.axis_index("core").astype(jnp.int32).reshape(1)
    gain = norm_gain.reshape(1, width)
    wide, tile = (rows, width), (chips, slab, HEAD)
    state_rows, half_state = (heads * HEAD, HEAD), (half, HEAD, HEAD)
    whole, size = rows * width, heads * HEAD * HEAD

    def across_chips(array):
        return lax.all_to_all(array, ("x", "y"), 0, 0)

    def swap(array):
        return lax.ppermute(array, "core", [(0, 1), (1, 0)])

    wide_bf, wide_f32 = ("v", wide, BF16), ("v", wide, F32)
    square, per_token = (heads, rows, rows), ("v", (rows, heads), F32)
    inputs = [queries, key_vectors, values, grad_out, decay_log.T, gain]
    own, kept_own, inside, across, key_decayed, q, k, v, g, gain = call(
        local_kernel,
        [
            ("v", (heads * HEAD + heads, HEAD), F32), ("v", (heads, HEAD), F32), per_token,
            ("v", (heads, rows), F32), wide_bf, wide_bf, wide_bf, wide_bf, wide_bf, ("v", (1, width), F32),
        ],
        [("h", a) for a in inputs],
        2 * whole * HEAD, 8 * whole,
        scratch=[pltpu.VMEM((heads, rows), F32), pltpu.SemaphoreType.DMA((8,))],
    )
    got = swap(own)
    near, mixing_turned, query_decayed, query_turned, weights, weights_turned, scaled = call(
        mixing_kernel,
        [
            wide_f32, ("v", square, BF16), wide_bf, ("v", (heads, HEAD, rows), BF16), ("v", square, F32),
            ("v", square, F32), wide_f32,
        ],
        [("v", a) for a in (q, k, v, g, gain, inside, across)],
        6 * whole * rows, 12 * whole,
    )
    (pay,) = call(
        forward_join_kernel,
        [("v", (chips * (slab + 1), HEAD), F32)],
        [("s", core), ("a", query_decayed), ("v", own), ("v", got)],
        2 * size, 12 * size,
    )
    pay = across_chips(pay.reshape(chips, 1, (slab + 1) * HEAD)).reshape(chips * (slab + 1), HEAD)
    tiles, kept_chips = call(
        forward_scan_kernel,
        [("v", tile, F32), ("v", (chips, HEAD), F32)],
        [("v", pay)],
        size, 4 * size,
    )
    half_in = across_chips(tiles).reshape(half_state)
    half_other = swap(half_in)
    attended, sums, entering = call(
        attend_kernel,
        [wide_f32, ("v", (tp_size, 2, rows), F32), ("v", (heads, HEAD, HEAD), BF16)],
        [("s", core)] + [("v", a) for a in (near, query_decayed, half_in, half_other, got, scaled)],
        2 * whole * HEAD, 12 * whole,
        scratch=[pltpu.VMEM((heads, HEAD, HEAD), F32)],
    )
    sums = lax.all_to_all(sums, "tp", 0, 0)
    back, grad_flat = call(
        norm_grad_kernel,
        [("v", state_rows, F32), wide_bf],
        [("v", a) for a in (sums, attended, scaled, query_turned)],
        2 * whole * HEAD, 12 * whole,
    )
    back_other = swap(back)
    outputs = [pltpu.VMEM(wide, BF16), pltpu.VMEM(wide, BF16), pltpu.SemaphoreType.DMA((heads,))]
    normed, grad_query = call(
        near_query_kernel,
        [("h", wide, BF16), ("h", wide, BF16)],
        [("v", a) for a in (sums, attended, gain, grad_flat, k, v, entering, inside, weights)],
        6 * whole * rows, 16 * whole, scratch=outputs,
    )
    (pay_back,) = call(
        reverse_join_kernel,
        [("v", (half * HEAD, HEAD), F32)],
        [("s", core), ("h", grad_query)] + [("v", a) for a in (back, back_other, kept_own, got)],
        2 * size, 12 * size,
    )
    grad_key_near, grad_value_near = call(
        near_key_kernel,
        [wide_f32, wide_f32],
        [("v", a) for a in (grad_flat, q, v, mixing_turned, weights_turned)],
        6 * whole * rows, 16 * whole,
    )
    (tiles_back,) = call(
        reverse_scan_kernel,
        [("v", tile, F32)],
        [("v", across_chips(pay_back.reshape(tile))), ("v", kept_chips)],
        size, 4 * size,
    )
    half_back = across_chips(tiles_back).reshape(half_state)
    half_back_other = swap(half_back)
    far_args = (
        grad_key_near, grad_value_near, key_decayed, v, half_back, half_back_other, back_other, got, inside
    )
    grad_key, grad_value = call(
        far_grad_kernel,
        [("h", wide, BF16), ("h", wide, BF16)],
        [("s", core)] + [("v", a) for a in far_args],
        4 * whole * HEAD, 16 * whole,
        scratch=[pltpu.VMEM((heads, HEAD, HEAD), F32), *outputs],
    )
    return normed, grad_query, grad_key, grad_value


def solution(mesh):
    seq, tp = mesh.shape["seq"], mesh.shape["tp"]
    fine = Mesh(mesh.devices.reshape(seq // 16, 8, 2, tp), ("x", "y", "core", "tp"))
    spec = P(("x", "y", "core"), "tp")
    return jax.shard_map(
        functools.partial(body, seq // 2, tp),
        mesh=fine,
        in_specs=(spec, spec, spec, spec, P("tp"), spec),
        out_specs=(spec, spec, spec, spec),
        check_vma=False,
    )
```

time: 117 us -> 112 us (0.957)
  local copies, waits for them, and re-layouts: 2.66 us -> 0 us
  waiting for transfers between devices: 3.74 us -> 1.15 us
    unnamed x16 -> x0, local copies, waits for them, and re-layouts: 2.66 us -> none
    ppermute x4, waiting for transfers between devices: 3.74 us -> 1.15 us  [swap(): return lax.ppermute(array, 'core', [(0, 1), (1, 0)])]
    pallas_call x10 -> x11, Pallas kernels: 8.29 us -> 9.35 us  [call(): pl.pallas_call(kernel, out_shape=[SPACES[m](s, d) for m, s, d in outs], i...]
  transfers between devices with their start and end apart: 4 -> 4, of which waited for: 3 -> 1; matrix products, arithmetic and copies ran while one was open for 0% -> 0% of each run, Pallas kernels for 3% -> 4%
where the time goes in v3:
time: 112 us
  blocking collectives  77.2 us (69%)
  starting transfers between devices  23.5 us (21%)
  Pallas kernels  9.35 us (8%)
  waiting for transfers between devices  1.15 us (1%)
    all_to_all x4, blocking collectives, across_chips(): return lax.all_to_all(array, ('x', 'y'), 0, 0)  60.7 us
    ppermute x4, starting transfers between devices, swap(): return lax.ppermute(array, 'core', [(0, 1), (1, 0)])  23.5 us
    all_to_all x1, blocking collectives, body(): sums = lax.all_to_all(sums, 'tp', 0, 0)  16.5 us
    pallas_call x11, Pallas kernels, call(): pl.pallas_call(kernel, out_shape=[SPACES[m](s, d) for m, s, d in outs], i...  9.35 us
  transfers between devices with their start and end apart: 4, of which 1 were waited for; matrix products, arithmetic and copies ran while one was open for 0% of the time, Pallas kernels for 4%

profile of v3, /device:TPU:1, one launch (start us, length us, event | category | flops | bytes accessed | tf_op | source)
XLA Modules:
  0.0 111.9 jit_solution(4417209205034575567)
XLA Ops:
  0.6 2.0 %shard_map.93 = (f32[1032,128]{1,0:T(8,128)S(1)}, f32[8,128]{1,0:T(8,128)S(1)}, f32[160,8]{1,0:T(8,128)S(1)}, f32[8,160]{1,0:T(8,128)S(1)}, bf16[160,1024]{1,0:T...) custom-call(bf16[160,1024]{1,0:T(8,128)(2,1)} %q_hbm.1, ...), custom_call_target="tpu_custom_call" | custom-call | flops 41943040 | bytes 1310720 | tf_op jit(solution)/shard_map/pallas_call | solution.py:31
  2.7 8.8 %collective-permute-start = (f32[1032,128]{1,0:T(8,128)S(1)}, f32[1032,128]{1,0:T(8,128)S(1)}, u32[]{:S(2)}, u32[]{:S(2)}) collective-permute-start(f32[1032,128]{1,0:T(8,128)S(1)} %get-tuple-element.43.own_ref), channel_id=1, source_target_pairs={{0,8},{8,0},{1,9},{9,1},{2,10},{10,2},{3,11},{11,3},{4,12},{12,4},... | collective-permute-start | bytes 1585160 | tf_op jit(solution)/shard_map/ppermute | solution.py:322
  11.5 1.5 %shard_map.94 = (f32[160,1024]{1,0:T(8,128)S(1)}, bf16[8,160,160]{2,1,0:T(8,128)(2,1)S(1)}, bf16[160,1024]{1,0:T(8,128)(2,1)S(1)}, bf16[8,128,160]{2,1,0:T(8,128...) custom-call(bf16[160,1024]{1,0:T(8,128)(2,1)S(1)} %get-tuple-element.34.q_ref, ...), custom_call_target="tpu_custom_call" | custom-call | flops 157286400 | bytes 1966080 | tf_op jit(solution)/shard_map/pallas_call | solution.py:31
  13.0 0.0 collective-permute-done.other_ref.got_ref.kept_got_ref
  13.0 0.1 shard_map.95
  13.1 14.1 %all_to_all.25 = f32[32,1,2176]{2,1,0:T(1,128)S(1)} all-to-all(f32[32,1,2176]{2,1,0:T(1,128)S(1)} %bitcast.9), channel_id=1, replica_groups=mesh['x'=4,'y'=8,'core'=2,'tp'=8] {'x','y'}, dimensions={0} | all-to-all | bytes 557056 | tf_op jit(solution)/shard_map/all_to_all | solution.py:319
  27.2 0.1 shard_map.96
  27.3 16.3 %all_to_all.26 = f32[32,16,128]{2,1,0:T(8,128)S(1)} all-to-all(f32[32,16,128]{2,1,0:T(8,128)S(1)} %get-tuple-element.44), channel_id=1, replica_groups=mesh['x'=4,'y'=8,'core'=2,'tp'=8] {'x','y'}, dimensions={0} | all-to-all | bytes 524288 | tf_op jit(solution)/shard_map/all_to_all | solution.py:319
  43.6 5.5 %collective-permute-start.1 = (f32[4,128,128]{2,1,0:T(8,128)S(1)}, f32[4,128,128]{2,1,0:T(8,128)S(1)}, u32[]{:S(2)}, u32[]{:S(2)}) collective-permute-start(f32[4,128,128]{2,1,0:T(8,128)S(1)} %bitcast.12), channel_id=1, source_target_pairs={{0,8},{8,0},{1,9},{9,1},{2,10},{10,2},{3,11},{11,3},{4,12},{12,4},... | collective-permute-start | bytes 786440 | tf_op jit(solution)/shard_map/ppermute | solution.py:322
  49.1 1.1 %collective-permute-done.1.half_other_ref = f32[4,128,128]{2,1,0:T(8,128)S(1)} collective-permute-done((f32[4,128,128]{2,1,0:T(8,128)S(1)}, f32[4,128,128]{2,1,0:T(8,128)S(1)}, u32[]{:S(2)}, u32[]{:S(2)}) %collective-permute-start.1) | collective-permute-done | bytes 262176 | tf_op jit(solution)/shard_map/ppermute | solution.py:322
  50.3 0.7 shard_map.97
  51.0 16.5 %all_to_all.27.sums_ref = f32[8,2,160]{2,1,0:T(2,128)S(1)} all-to-all(f32[8,2,160]{2,1,0:T(2,128)S(1)} %get-tuple-element.46), channel_id=1, replica_groups=mesh['x'=4,'y'=8,'core'=2,'tp'=8] {'tp'}, dimensions={0} | all-to-all | bytes 20480 | tf_op jit(solution)/shard_map/all_to_all | solution.py:369
  67.5 0.4 shard_map.98
  67.9 3.7 %collective-permute-start.2 = (f32[1024,128]{1,0:T(8,128)S(1)}, f32[1024,128]{1,0:T(8,128)S(1)}, u32[]{:S(2)}, u32[]{:S(2)}) collective-permute-start(f32[1024,128]{1,0:T(8,128)S(1)} %get-tuple-element.59.own_ref), channel_id=1, source_target_pairs={{0,8},{8,0},{1,9},{9,1},{2,10},{10,2},{3,11},{11,3},{4,12},{12,4},... | collective-permute-start | bytes 1572872 | tf_op jit(solution)/shard_map/ppermute | solution.py:322
  71.6 1.8 %shard_map.99 = (bf16[160,1024]{1,0:T(8,128)(2,1)}, bf16[160,1024]{1,0:T(8,128)(2,1)}) custom-call(f32[8,2,160]{2,1,0:T(2,128)S(1)} %all_to_all.27.sums_ref, f32[160,1024]{1,0:T(8,128)S(1)} %get-tuple-element.47.att_ref, f32[1,1024]{1,0:T(1,128)S(1)} %get-tuple-element.38.gain_ref, bf16[160,1024]{1,0:T(8,128)(2,1)S(1)} %get-tuple-element.49.gf_ref, ...), custom_call_target="tpu_custom_call" | custom-call | flops 157286400 | bytes 2621440 | tf_op jit(solution)/shard_map/pallas_call | solution.py:31
  73.4 0.0 collective-permute-done.2.other_ref
  73.4 14.3 %all_to_all.28.got_ref = f32[32,16,128]{2,1,0:T(8,128)S(1)} all-to-all(f32[32,16,128]{2,1,0:T(8,128)S(1)} %bitcast.14), channel_id=1, replica_groups=mesh['x'=4,'y'=8,'core'=2,'tp'=8] {'x','y'}, dimensions={0} | all-to-all | bytes 524288 | tf_op jit(solution)/shard_map/all_to_all | solution.py:319
  87.8 0.1 shard_map.102
  87.8 15.9 %all_to_all.29 = f32[32,16,128]{2,1,0:T(8,128)S(1)} all-to-all(f32[32,16,128]{2,1,0:T(8,128)S(1)} %shard_map.102), channel_id=1, replica_groups=mesh['x'=4,'y'=8,'core'=2,'tp'=8] {'x','y'}, dimensions={0} | all-to-all | bytes 524288 | tf_op jit(solution)/shard_map/all_to_all | solution.py:319
  103.7 5.5 %collective-permute-start.3 = (f32[4,128,128]{2,1,0:T(8,128)S(1)}, f32[4,128,128]{2,1,0:T(8,128)S(1)}, u32[]{:S(2)}, u32[]{:S(2)}) collective-permute-start(f32[4,128,128]{2,1,0:T(8,128)S(1)} %bitcast.10), channel_id=1, source_target_pairs={{0,8},{8,0},{1,9},{9,1},{2,10},{10,2},{3,11},{11,3},{4,12},{12,4},... | collective-permute-start | bytes 786440 | tf_op jit(solution)/shard_map/ppermute | solution.py:322
  109.2 1.4 %shard_map.100 = (f32[160,1024]{1,0:T(8,128)S(1)}, f32[160,1024]{1,0:T(8,128)S(1)}) custom-call(bf16[160,1024]{1,0:T(8,128)(2,1)S(1)} %get-tuple-element.49.gf_ref, bf16[160,1024]{1,0:T(8,128)(2,1)S(1)} %get-tuple-element.34.q_ref, bf16[160,1024]{1,0:T(8,128)(2,1)S(1)} %get-tuple-element.36.v_ref, bf16[8,160,160]{2,1,0:T(8,128)(2,1)S(1)} %get-tuple-element.54.mix_turned_ref, ...), custom_call_target="tpu_custom_call" | custom-call | flops 157286400 | bytes 2621440 | tf_op jit(solution)/shard_map/pallas_call | solution.py:31
  110.7 0.0 collective-permute-done.3.half_other_ref
  110.7 1.2 %shard_map.103 = (bf16[160,1024]{1,0:T(8,128)(2,1)}, bf16[160,1024]{1,0:T(8,128)(2,1)}) custom-call(s32[1]{0:T(128)} %bitcast.core_ref, f32[160,1024]{1,0:T(8,128)S(1)} %get-tuple-element.56.gk_near_ref, f32[160,1024]{1,0:T(8,128)S(1)} %get-tuple-element.57.gv_near_ref, bf16[160,1024]{1,0:T(8,128)(2,1)S(1)} %get-tuple-element.58.key_ref, ...), custom_call_target="tpu_custom_call" | custom-call | flops 83886080 | bytes 2621440 | tf_op jit(solution)/shard_map/pallas_call | solution.py:31
  (1 shorter events, 0.0 us)
Async XLA Ops:
  2.7 10.3 %collective-permute-start = (f32[1032,128]{1,0:T(8,128)S(1)}, f32[1032,128]{1,0:T(8,128)S(1)}, u32[]{:S(2)}, u32[]{:S(2)}) collective-permute-start(f32[1032,128]{1,0:T(8,128)S(1)} %get-tuple-element.43.own_ref), channel_id=1, source_target_pairs={{0,8},{8,0},{1,9},{9,1},{2,10},{10,2},{3,11},{11,3},{4,12},{12,4},... | collective-permute-start | bytes 1585160 | tf_op jit(solution)/shard_map/ppermute | solution.py:322
  43.6 6.7 %collective-permute-start.1 = (f32[4,128,128]{2,1,0:T(8,128)S(1)}, f32[4,128,128]{2,1,0:T(8,128)S(1)}, u32[]{:S(2)}, u32[]{:S(2)}) collective-permute-start(f32[4,128,128]{2,1,0:T(8,128)S(1)} %bitcast.12), channel_id=1, source_target_pairs={{0,8},{8,0},{1,9},{9,1},{2,10},{10,2},{3,11},{11,3},{4,12},{12,4},... | collective-permute-start | bytes 786440 | tf_op jit(solution)/shard_map/ppermute | solution.py:322
  67.9 5.5 %collective-permute-start.2 = (f32[1024,128]{1,0:T(8,128)S(1)}, f32[1024,128]{1,0:T(8,128)S(1)}, u32[]{:S(2)}, u32[]{:S(2)}) collective-permute-start(f32[1024,128]{1,0:T(8,128)S(1)} %get-tuple-element.59.own_ref), channel_id=1, source_target_pairs={{0,8},{8,0},{1,9},{9,1},{2,10},{10,2},{3,11},{11,3},{4,12},{12,4},... | collective-permute-start | bytes 1572872 | tf_op jit(solution)/shard_map/ppermute | solution.py:322
  103.7 6.9 %collective-permute-start.3 = (f32[4,128,128]{2,1,0:T(8,128)S(1)}, f32[4,128,128]{2,1,0:T(8,128)S(1)}, u32[]{:S(2)}, u32[]{:S(2)}) collective-permute-start(f32[4,128,128]{2,1,0:T(8,128)S(1)} %bitcast.10), channel_id=1, source_target_pairs={{0,8},{8,0},{1,9},{9,1},{2,10},{10,2},{3,11},{11,3},{4,12},{12,4},... | collective-permute-start | bytes 786440 | tf_op jit(solution)/shard_map/ppermute | solution.py:322

commit v4 on v3

--- a/solution.py
+++ b/solution.py
@@ -27,13 +27,14 @@
 SPACES = {"s": pltpu.SMEM, "h": pltpu.HBM, "v": pltpu.VMEM, "a": pl.ANY}
 
 
-def call(kernel, outs, args, flops, bytes_accessed, scratch=()):
+def call(kernel, outs, args, flops, bytes_accessed, scratch=(), aliases=()):
     return pl.pallas_call(
         kernel,
         out_shape=[SPACES[m](s, d) for m, s, d in outs],
         in_specs=[pl.BlockSpec(memory_space=SPACES[m]) for m, _ in args],
         out_specs=[pl.BlockSpec(memory_space=SPACES[m]) for m, _, _ in outs],
         scratch_shapes=list(scratch),
+        input_output_aliases=dict(aliases),
         compiler_params=pltpu.CompilerParams(vmem_limit_bytes=VMEM_LIMIT),
         cost_estimate=pl.CostEstimate(
             flops=flops, bytes_accessed=bytes_accessed, transcendentals=0
@@ -54,11 +55,9 @@
     pay_ref, kept_ref, inside_ref, across_ref, key_ref, q_ref, k_ref, v_ref, g_ref, gain_ref, decay_ref, sems,
 ):
     heads, rows = decay_ref.shape
-    halves = [slice(0, heads // 2 * HEAD), slice(heads // 2 * HEAD, heads * HEAD)]
-    pieces = [(decay_hbm, decay_ref)]
-    for cols in halves:
-        pieces += [(k_hbm.at[:, cols], k_ref.at[:, cols]), (v_hbm.at[:, cols], v_ref.at[:, cols])]
-    pieces += [(q_hbm, q_ref), (g_hbm, g_ref), (gain_hbm, gain_ref)]
+    pieces = [
+        (decay_hbm, decay_ref), (k_hbm, k_ref), (v_hbm, v_ref), (q_hbm, q_ref), (g_hbm, g_ref), (gain_hbm, gain_ref)
+    ]
     copies = [pltpu.make_async_copy(*piece, sems.at[i]) for i, piece in enumerate(pieces)]
     for copy in copies:
         copy.start()
@@ -66,8 +65,15 @@
     second = lax.broadcasted_iota(jnp.int32, (rows, rows), 1)
     copies[0].wait()
     decay = decay_ref[...]
-    inside = dot((first >= second).astype(F32), decay, NT, HIGH)
-    across = dot(decay, (first <= second).astype(F32), NN, HIGH)
+    high = decay.astype(BF16)
+    rest = decay - high.astype(F32)
+    middle = rest.astype(BF16)
+    low = (rest - middle.astype(F32)).astype(BF16)
+    terms = jnp.concatenate([high, middle, low], axis=0)
+    sums = dot(terms, (first <= second).astype(BF16), NN)
+    across = sums[:heads] + (sums[heads : 2 * heads] + sums[2 * heads :])
+    sums = dot((first >= second).astype(BF16), terms, NT)
+    inside = sums[:, :heads] + (sums[:, heads : 2 * heads] + sums[:, 2 * heads :])
     inside_ref[...] = inside
     across_ref[...] = across
     shares = jnp.exp(inside[rows - 1 : rows, :] - inside)
@@ -75,15 +81,14 @@
     kept_ref[...] = kept
     pay_ref[heads * HEAD :, :] = kept
     for h in range(heads):
-        if h == 0 or h == heads // 2:
-            at = 1 if h == 0 else 3
-            copies[at].wait()
-            copies[at + 1].wait()
+        if h == 0:
+            copies[1].wait()
+            copies[2].wait()
         cols = head_cols(h)
         key_decayed = (k_ref[:, cols].astype(F32) * shares[:, h : h + 1]).astype(BF16)
         key_ref[:, cols] = key_decayed
         pay_ref[head_rows(h), :] = dot(key_decayed, v_ref[:, cols], TN)
-    for copy in copies[5:]:
+    for copy in copies[3:]:
         copy.wait()
 
 
@@ -176,39 +181,49 @@
         scaled_ref[:, cols] = g_ref[:, cols].astype(F32) * gain_ref[:, cols]
 
 
-def attend_kernel(
-    core_ref, near_ref, query_ref, half_ref, half_other_ref, got_ref, scaled_ref,
-    att_ref, sums_ref, state_bf_ref, state_ref,
-):
-    rows, width = near_ref.shape
-    heads = width // HEAD
-    half = heads // 2
-    core = core_ref[0]
-    state_ref[pl.ds(core * half, half)] = half_ref[...]
-    state_ref[pl.ds((1 - core) * half, half)] = half_other_ref[...]
-
-    @pl.when(core == 1)
-    def _():
-        for h in range(heads):
-            kept = got_ref[heads * HEAD + h : heads * HEAD + h + 1, :]
-            state_ref[h] = kept * state_ref[h] + got_ref[head_rows(h), :]
-
-    squares = jnp.zeros((rows, HEAD), F32)
-    crossed = jnp.zeros((rows, HEAD), F32)
-    for h in range(heads):
-        cols = head_cols(h)
-        state = state_ref[h].astype(BF16)
-        state_bf_ref[h] = state
+def attend_half(
+    base, core, near_ref, query_ref, half_ref, got_ref, scaled_ref, att_ref, entering_ref, squares, crossed
+):
+    heads = entering_ref.shape[0]
+    for i in range(heads // 2):
+        h = base + i
+        cols = pl.ds(pl.multiple_of(h * HEAD, HEAD), HEAD)
+        kept = got_ref[pl.ds(heads * HEAD + h, 1), :]
+        state = half_ref[i]
+        state = jnp.where(core == 0, state, kept * state + got_ref[cols, :]).astype(BF16)
+        entering_ref[h] = state
         attended = near_ref[:, cols] + dot(query_ref[:, cols], state, NN)
         att_ref[:, cols] = attended
         squares += attended * attended
         crossed += scaled_ref[:, cols] * attended
-    ones = jnp.ones((8, HEAD), F32)
-    square_rows = dot(ones, squares, NT, HIGH)
-    cross_rows = dot(ones, crossed, NT, HIGH)
+    return squares, crossed
+
+
+def attend_own_kernel(
+    core_ref, near_ref, query_ref, half_ref, got_ref, scaled_ref, att_ref, entering_ref, squares_ref, crossed_ref
+):
+    core = core_ref[0]
+    zero = jnp.zeros(squares_ref.shape, F32)
+    squares_ref[...], crossed_ref[...] = attend_half(
+        core * (entering_ref.shape[0] // 2), core, near_ref, query_ref, half_ref, got_ref, scaled_ref,
+        att_ref, entering_ref, zero, zero,
+    )
+
+
+def attend_other_kernel(
+    core_ref, near_ref, query_ref, half_ref, got_ref, scaled_ref, squares_ref, crossed_ref,
+    att_in_ref, entering_in_ref, att_ref, entering_ref, sums_ref,
+):
+    core = core_ref[0]
+    squares, crossed = attend_half(
+        (1 - core) * (entering_ref.shape[0] // 2), core, near_ref, query_ref, half_ref, got_ref, scaled_ref,
+        att_ref, entering_ref, squares_ref[...], crossed_ref[...],
+    )
+    sums = jnp.concatenate(
+        [jnp.sum(squares, axis=1, keepdims=True), jnp.sum(crossed, axis=1, keepdims=True)], axis=1
+    ).T
     for peer in range(sums_ref.shape[0]):
-        sums_ref[peer, 0:1, :] = square_rows[0:1]
-        sums_ref[peer, 1:2, :] = cross_rows[0:1]
+        sums_ref[peer] = sums
 
 
 def norm_columns(sums_ref, rows):
@@ -332,7 +347,7 @@
         ],
         [("h", a) for a in inputs],
         2 * whole * HEAD, 8 * whole,
-        scratch=[pltpu.VMEM((heads, rows), F32), pltpu.SemaphoreType.DMA((8,))],
+        scratch=[pltpu.VMEM((heads, rows), F32), pltpu.SemaphoreType.DMA((6,))],
     )
     got = swap(own)
     near, mixing_turned, query_decayed, query_turned, weights, weights_turned, scaled = call(
@@ -359,12 +374,19 @@
     )
     half_in = across_chips(tiles).reshape(half_state)
     half_other = swap(half_in)
-    attended, sums, entering = call(
-        attend_kernel,
-        [wide_f32, ("v", (tp_size, 2, rows), F32), ("v", (heads, HEAD, HEAD), BF16)],
-        [("s", core)] + [("v", a) for a in (near, query_decayed, half_in, half_other, got, scaled)],
-        2 * whole * HEAD, 12 * whole,
-        scratch=[pltpu.VMEM((heads, HEAD, HEAD), F32)],
+    entering_bf, column = ("v", (heads, HEAD, HEAD), BF16), ("v", (rows, HEAD), F32)
+    attended, entering, squares, crossed = call(
+        attend_own_kernel,
+        [wide_f32, entering_bf, column, column],
+        [("s", core)] + [("v", a) for a in (near, query_decayed, half_in, got, scaled)],
+        whole * HEAD, 6 * whole,
+    )
+    other_args = (near, query_decayed, half_other, got, scaled, squares, crossed, attended, entering)
+    attended, entering, sums = call(
+        attend_other_kernel,
+        [wide_f32, entering_bf, ("v", (tp_size, 2, rows), F32)],
+        [("s", core)] + [("v", a) for a in other_args],
+        whole * HEAD, 6 * whole, aliases={8: 0, 9: 1},
     )
     sums = lax.all_to_all(sums, "tp", 0, 0)
     back, grad_flat = call(

time: 112 us -> 112 us (level)
    pallas_call x11 -> x12, Pallas kernels: 9.35 us -> 8.93 us  [call(): pl.pallas_call(kernel, out_shape=[SPACES[m](s, d) for m, s, d in outs], i...]
where the time goes in v4:
time: 112 us; the launch traced here: 111 us
  blocking collectives  77.2 us (69%)
  starting transfers between devices  23.5 us (21%)
  Pallas kernels  8.93 us (8%)
    all_to_all x4, blocking collectives, across_chips(): return lax.all_to_all(array, ('x', 'y'), 0, 0)  60.7 us
    ppermute x4, starting transfers between devices, swap(): return lax.ppermute(array, 'core', [(0, 1), (1, 0)])  23.5 us
    all_to_all x1, blocking collectives, body(): sums = lax.all_to_all(sums, 'tp', 0, 0)  16.5 us
    pallas_call x12, Pallas kernels, call(): pl.pallas_call(kernel, out_shape=[SPACES[m](s, d) for m, s, d in outs], i...  8.93 us
  transfers between devices with their start and end apart: 4, of which 1 were waited for; matrix products, arithmetic and copies ran while one was open for 0% of the time, Pallas kernels for 4%

profile of v4, /device:TPU:1, one launch (start us, length us, event | category | flops | bytes accessed | tf_op | source)
XLA Modules:
  0.0 111.3 jit_solution(13175317609487517828)
XLA Ops:
  0.6 1.7 %shard_map.93 = (f32[1032,128]{1,0:T(8,128)S(1)}, f32[8,128]{1,0:T(8,128)S(1)}, f32[160,8]{1,0:T(8,128)S(1)}, f32[8,160]{1,0:T(8,128)S(1)}, bf16[160,1024]{1,0:T...) custom-call(bf16[160,1024]{1,0:T(8,128)(2,1)} %q_hbm.1, ...), custom_call_target="tpu_custom_call" | custom-call | flops 41943040 | bytes 1310720 | tf_op jit(solution)/shard_map/pallas_call | solution.py:31
  2.4 8.8 %collective-permute-start = (f32[1032,128]{1,0:T(8,128)S(1)}, f32[1032,128]{1,0:T(8,128)S(1)}, u32[]{:S(2)}, u32[]{:S(2)}) collective-permute-start(f32[1032,128]{1,0:T(8,128)S(1)} %get-tuple-element.47.own_ref), channel_id=1, source_target_pairs={{0,8},{8,0},{1,9},{9,1},{2,10},{10,2},{3,11},{11,3},{4,12},{12,4},... | collective-permute-start | bytes 1585160 | tf_op jit(solution)/shard_map/ppermute | solution.py:337
  11.2 1.5 %shard_map.94 = (f32[160,1024]{1,0:T(8,128)S(1)}, bf16[8,160,160]{2,1,0:T(8,128)(2,1)S(1)}, bf16[160,1024]{1,0:T(8,128)(2,1)S(1)}, bf16[8,128,160]{2,1,0:T(8,128...) custom-call(bf16[160,1024]{1,0:T(8,128)(2,1)S(1)} %get-tuple-element.38.q_ref, ...), custom_call_target="tpu_custom_call" | custom-call | flops 157286400 | bytes 1966080 | tf_op jit(solution)/shard_map/pallas_call | solution.py:31
  12.7 0.0 collective-permute-done.other_ref.got_ref.kept_got_ref
  12.7 0.1 shard_map.95
  12.8 14.1 %all_to_all.25 = f32[32,1,2176]{2,1,0:T(1,128)S(1)} all-to-all(f32[32,1,2176]{2,1,0:T(1,128)S(1)} %bitcast.9), channel_id=1, replica_groups=mesh['x'=4,'y'=8,'core'=2,'tp'=8] {'x','y'}, dimensions={0} | all-to-all | bytes 557056 | tf_op jit(solution)/shard_map/all_to_all | solution.py:334
  26.9 0.1 shard_map.96
  26.9 16.4 %all_to_all.26 = f32[32,16,128]{2,1,0:T(8,128)S(1)} all-to-all(f32[32,16,128]{2,1,0:T(8,128)S(1)} %get-tuple-element.48), channel_id=1, replica_groups=mesh['x'=4,'y'=8,'core'=2,'tp'=8] {'x','y'}, dimensions={0} | all-to-all | bytes 524288 | tf_op jit(solution)/shard_map/all_to_all | solution.py:334
  43.3 5.5 %collective-permute-start.1 = (f32[4,128,128]{2,1,0:T(8,128)S(1)}, f32[4,128,128]{2,1,0:T(8,128)S(1)}, u32[]{:S(2)}, u32[]{:S(2)}) collective-permute-start(f32[4,128,128]{2,1,0:T(8,128)S(1)} %bitcast.13), channel_id=1, source_target_pairs={{0,8},{8,0},{1,9},{9,1},{2,10},{10,2},{3,11},{11,3},{4,12},{12,4},... | collective-permute-start | bytes 786440 | tf_op jit(solution)/shard_map/ppermute | solution.py:337
  48.8 0.2 shard_map.97
  49.1 0.9 collective-permute-done.1.half_ref
  49.9 0.4 shard_map.98
  50.3 16.5 %all_to_all.27.sums_ref = f32[8,2,160]{2,1,0:T(2,128)S(1)} all-to-all(f32[8,2,160]{2,1,0:T(2,128)S(1)} %get-tuple-element.54), channel_id=1, replica_groups=mesh['x'=4,'y'=8,'core'=2,'tp'=8] {'tp'}, dimensions={0} | all-to-all | bytes 20480 | tf_op jit(solution)/shard_map/all_to_all | solution.py:391
  66.8 0.4 shard_map.99
  67.2 3.7 %collective-permute-start.2 = (f32[1024,128]{1,0:T(8,128)S(1)}, f32[1024,128]{1,0:T(8,128)S(1)}, u32[]{:S(2)}, u32[]{:S(2)}) collective-permute-start(f32[1024,128]{1,0:T(8,128)S(1)} %get-tuple-element.67.own_ref), channel_id=1, source_target_pairs={{0,8},{8,0},{1,9},{9,1},{2,10},{10,2},{3,11},{11,3},{4,12},{12,4},... | collective-permute-start | bytes 1572872 | tf_op jit(solution)/shard_map/ppermute | solution.py:337
  71.0 1.8 %shard_map.100 = (bf16[160,1024]{1,0:T(8,128)(2,1)}, bf16[160,1024]{1,0:T(8,128)(2,1)}) custom-call(f32[8,2,160]{2,1,0:T(2,128)S(1)} %all_to_all.27.sums_ref, f32[160,1024]{1,0:T(8,128)S(1)} %get-tuple-element.55.att_ref, f32[1,1024]{1,0:T(1,128)S(1)} %get-tuple-element.42.gain_ref, bf16[160,1024]{1,0:T(8,128)(2,1)S(1)} %get-tuple-element.57.gf_ref, ...), custom_call_target="tpu_custom_call" | custom-call | flops 157286400 | bytes 2621440 | tf_op jit(solution)/shard_map/pallas_call | solution.py:31
  72.8 0.0 collective-permute-done.2.other_ref
  72.8 0.1 shard_map.102
  72.8 14.3 %all_to_all.28.got_ref = f32[32,16,128]{2,1,0:T(8,128)S(1)} all-to-all(f32[32,16,128]{2,1,0:T(8,128)S(1)} %bitcast.12), channel_id=1, replica_groups=mesh['x'=4,'y'=8,'core'=2,'tp'=8] {'x','y'}, dimensions={0} | all-to-all | bytes 524288 | tf_op jit(solution)/shard_map/all_to_all | solution.py:334
  87.2 0.1 shard_map.103
  87.2 15.9 %all_to_all.29 = f32[32,16,128]{2,1,0:T(8,128)S(1)} all-to-all(f32[32,16,128]{2,1,0:T(8,128)S(1)} %shard_map.103), channel_id=1, replica_groups=mesh['x'=4,'y'=8,'core'=2,'tp'=8] {'x','y'}, dimensions={0} | all-to-all | bytes 524288 | tf_op jit(solution)/shard_map/all_to_all | solution.py:334
  103.1 5.5 %collective-permute-start.3 = (f32[4,128,128]{2,1,0:T(8,128)S(1)}, f32[4,128,128]{2,1,0:T(8,128)S(1)}, u32[]{:S(2)}, u32[]{:S(2)}) collective-permute-start(f32[4,128,128]{2,1,0:T(8,128)S(1)} %bitcast.10), channel_id=1, source_target_pairs={{0,8},{8,0},{1,9},{9,1},{2,10},{10,2},{3,11},{11,3},{4,12},{12,4},... | collective-permute-start | bytes 786440 | tf_op jit(solution)/shard_map/ppermute | solution.py:337
  108.6 1.4 %shard_map.101 = (f32[160,1024]{1,0:T(8,128)S(1)}, f32[160,1024]{1,0:T(8,128)S(1)}) custom-call(bf16[160,1024]{1,0:T(8,128)(2,1)S(1)} %get-tuple-element.57.gf_ref, bf16[160,1024]{1,0:T(8,128)(2,1)S(1)} %get-tuple-element.38.q_ref, bf16[160,1024]{1,0:T(8,128)(2,1)S(1)} %get-tuple-element.40.v_ref, bf16[8,160,160]{2,1,0:T(8,128)(2,1)S(1)} %get-tuple-element.62.mix_turned_ref, ...), custom_call_target="tpu_custom_call" | custom-call | flops 157286400 | bytes 2621440 | tf_op jit(solution)/shard_map/pallas_call | solution.py:31
  110.0 0.0 collective-permute-done.3.half_other_ref
  110.0 1.2 %shard_map.104 = (bf16[160,1024]{1,0:T(8,128)(2,1)}, bf16[160,1024]{1,0:T(8,128)(2,1)}) custom-call(s32[1]{0:T(128)} %bitcast.core_ref, f32[160,1024]{1,0:T(8,128)S(1)} %get-tuple-element.64.gk_near_ref, f32[160,1024]{1,0:T(8,128)S(1)} %get-tuple-element.65.gv_near_ref, bf16[160,1024]{1,0:T(8,128)(2,1)S(1)} %get-tuple-element.66.key_ref, ...), custom_call_target="tpu_custom_call" | custom-call | flops 83886080 | bytes 2621440 | tf_op jit(solution)/shard_map/pallas_call | solution.py:31
Async XLA Ops:
  2.4 10.3 %collective-permute-start = (f32[1032,128]{1,0:T(8,128)S(1)}, f32[1032,128]{1,0:T(8,128)S(1)}, u32[]{:S(2)}, u32[]{:S(2)}) collective-permute-start(f32[1032,128]{1,0:T(8,128)S(1)} %get-tuple-element.47.own_ref), channel_id=1, source_target_pairs={{0,8},{8,0},{1,9},{9,1},{2,10},{10,2},{3,11},{11,3},{4,12},{12,4},... | collective-permute-start | bytes 1585160 | tf_op jit(solution)/shard_map/ppermute | solution.py:337
  43.3 6.7 %collective-permute-start.1 = (f32[4,128,128]{2,1,0:T(8,128)S(1)}, f32[4,128,128]{2,1,0:T(8,128)S(1)}, u32[]{:S(2)}, u32[]{:S(2)}) collective-permute-start(f32[4,128,128]{2,1,0:T(8,128)S(1)} %bitcast.13), channel_id=1, source_target_pairs={{0,8},{8,0},{1,9},{9,1},{2,10},{10,2},{3,11},{11,3},{4,12},{12,4},... | collective-permute-start | bytes 786440 | tf_op jit(solution)/shard_map/ppermute | solution.py:337
  67.2 5.5 %collective-permute-start.2 = (f32[1024,128]{1,0:T(8,128)S(1)}, f32[1024,128]{1,0:T(8,128)S(1)}, u32[]{:S(2)}, u32[]{:S(2)}) collective-permute-start(f32[1024,128]{1,0:T(8,128)S(1)} %get-tuple-element.67.own_ref), channel_id=1, source_target_pairs={{0,8},{8,0},{1,9},{9,1},{2,10},{10,2},{3,11},{11,3},{4,12},{12,4},... | collective-permute-start | bytes 1572872 | tf_op jit(solution)/shard_map/ppermute | solution.py:337
  103.1 6.9 %collective-permute-start.3 = (f32[4,128,128]{2,1,0:T(8,128)S(1)}, f32[4,128,128]{2,1,0:T(8,128)S(1)}, u32[]{:S(2)}, u32[]{:S(2)}) collective-permute-start(f32[4,128,128]{2,1,0:T(8,128)S(1)} %bitcast.10), channel_id=1, source_target_pairs={{0,8},{8,0},{1,9},{9,1},{2,10},{10,2},{3,11},{11,3},{4,12},{12,4},... | collective-permute-start | bytes 786440 | tf_op jit(solution)/shard_map/ppermute | solution.py:337

commit v5 on v4

v5 whole, which is shorter than its diff:
```python
import functools

import jax
import jax.numpy as jnp
from jax import lax
from jax.experimental import pallas as pl
from jax.experimental.pallas import tpu as pltpu
from jax.sharding import Mesh
from jax.sharding import PartitionSpec as P

HEAD_COUNT = 64
HEAD = 128
EPSILON = 1e-06
HIGH = lax.Precision.HIGHEST
F32 = jnp.float32
BF16 = jnp.bfloat16
VMEM_LIMIT = 20 * 1024 * 1024
NN = (((1,), (0,)), ((), ()))
NT = (((1,), (1,)), ((), ()))
TN = (((0,), (0,)), ((), ()))


def dot(a, b, dims, precision=None):
    return lax.dot_general(a, b, dims, precision=precision, preferred_element_type=F32)


SPACES = {"s": pltpu.SMEM, "h": pltpu.HBM, "v": pltpu.VMEM, "a": pl.ANY}


def call(kernel, outs, args, flops, bytes_accessed, scratch=(), aliases=()):
    return pl.pallas_call(
        kernel,
        out_shape=[SPACES[m](s, d) for m, s, d in outs],
        in_specs=[pl.BlockSpec(memory_space=SPACES[m]) for m, _ in args],
        out_specs=[pl.BlockSpec(memory_space=SPACES[m]) for m, _, _ in outs],
        scratch_shapes=list(scratch),
        input_output_aliases=dict(aliases),
        compiler_params=pltpu.CompilerParams(vmem_limit_bytes=VMEM_LIMIT),
        cost_estimate=pl.CostEstimate(
            flops=flops, bytes_accessed=bytes_accessed, transcendentals=0
        ),
    )(*[pltpu.with_memory_space_constraint(a, SPACES[m]) if m in "hv" else a for m, a in args])


def head_cols(h):
    return slice(h * HEAD, (h + 1) * HEAD)


def head_rows(h):
    return slice(h * HEAD, (h + 1) * HEAD)


def deal_halves(core, state_of, half, keep_ref, send_ref):
    for i in range(half):
        low, high = state_of(i), state_of(half + i)
        keep_ref[head_rows(i), :] = jnp.where(core == 0, low, high)
        send_ref[head_rows(i), :] = jnp.where(core == 0, high, low)


def local_kernel(
    core_ref, q_hbm, k_hbm, v_hbm, g_hbm, decay_hbm, gain_hbm,
    keep_ref, send_ref, kept_ref, inside_ref, across_ref, key_ref, q_ref, k_ref, v_ref, g_ref, gain_ref, decay_ref, sems,
):
    heads, rows = decay_ref.shape
    pieces = [
        (decay_hbm, decay_ref), (k_hbm, k_ref), (v_hbm, v_ref), (q_hbm, q_ref), (g_hbm, g_ref), (gain_hbm, gain_ref)
    ]
    copies = [pltpu.make_async_copy(*piece, sems.at[i]) for i, piece in enumerate(pieces)]
    for copy in copies:
        copy.start()
    first = lax.broadcasted_iota(jnp.int32, (rows, rows), 0)
    second = lax.broadcasted_iota(jnp.int32, (rows, rows), 1)
    copies[0].wait()
    decay = decay_ref[...]
    high = decay.astype(BF16)
    rest = decay - high.astype(F32)
    middle = rest.astype(BF16)
    low = (rest - middle.astype(F32)).astype(BF16)
    terms = jnp.concatenate([high, middle, low], axis=0)
    sums = dot(terms, (first <= second).astype(BF16), NN)
    across = sums[:heads] + (sums[heads : 2 * heads] + sums[2 * heads :])
    sums = dot((first >= second).astype(BF16), terms, NT)
    inside = sums[:, :heads] + (sums[:, heads : 2 * heads] + sums[:, 2 * heads :])
    inside_ref[...] = inside
    across_ref[...] = across
    shares = jnp.exp(inside[rows - 1 : rows, :] - inside)
    kept = jnp.broadcast_to(jnp.exp(across[:, rows - 1 : rows]), (heads, HEAD))
    kept_ref[...] = kept
    send_ref[heads // 2 * HEAD :, :] = kept
    copies[1].wait()
    copies[2].wait()

    def state_of(h):
        cols = head_cols(h)
        key_decayed = (k_ref[:, cols].astype(F32) * shares[:, h : h + 1]).astype(BF16)
        key_ref[:, cols] = key_decayed
        return dot(key_decayed, v_ref[:, cols], TN)

    deal_halves(core_ref[0], state_of, heads // 2, keep_ref, send_ref)
    for copy in copies[3:]:
        copy.wait()


def kept_rows(core, own_ref, got_ref, i):
    half = got_ref.shape[0] // (HEAD + 2)
    at = got_ref.shape[0] - 2 * half
    own = jnp.where(core == 0, own_ref[i : i + 1, :], own_ref[half + i : half + i + 1, :])
    got = jnp.where(core == 0, got_ref[at + i : at + i + 1, :], got_ref[at + half + i : at + half + i + 1, :])
    return jnp.where(core == 0, own, got), jnp.where(core == 0, got, own)


def in_order(core, own, got):
    return jnp.where(core == 0, own, got), jnp.where(core == 0, got, own)


def forward_join_kernel(core_ref, after_ref, keep_ref, got_ref, kept_ref, pay_ref):
    core = core_ref[0]
    for i in range(keep_ref.shape[0] // HEAD):
        first, second = in_order(core, keep_ref[head_rows(i), :], got_ref[head_rows(i), :])
        kept_first, kept_second = kept_rows(core, kept_ref, got_ref, i)
        joined = kept_second * first + second
        for part in range(8):
            at = 17 * (8 * i + part)
            pay_ref[at : at + 16, :] = joined[16 * part : 16 * part + 16]
            pay_ref[at + 16 : at + 17, :] = kept_first * kept_second


def forward_scan_kernel(got_ref, out_ref, kept_ref):
    count = out_ref.shape[0]
    state = jnp.zeros(out_ref.shape[1:], F32)
    for j in range(count):
        out_ref[j] = state
        kept = got_ref[17 * j + 16 : 17 * j + 17, :]
        kept_ref[j : j + 1, :] = kept
        state = kept * state + got_ref[17 * j : 17 * j + 16, :]


def reverse_join_kernel(core_ref, after_ref, keep_ref, got_ref, kept_ref, got_kept_ref, out_ref):
    core = core_ref[0]
    for i in range(keep_ref.shape[0] // HEAD):
        first, second = in_order(core, keep_ref[head_rows(i), :], got_ref[head_rows(i), :])
        kept_first, _ = kept_rows(core, kept_ref, got_kept_ref, i)
        out_ref[head_rows(i), :] = first + kept_first * second


def reverse_scan_kernel(got_ref, kept_ref, out_ref):
    count = out_ref.shape[0]
    state = jnp.zeros(out_ref.shape[1:], F32)
    for j in reversed(range(count)):
        out_ref[j] = state
        state = kept_ref[j : j + 1, :] * state + got_ref[j]


def weights_of(inside_ref, across_ref, h, transposed=False):
    rows = inside_ref.shape[0]
    first = lax.broadcasted_iota(jnp.int32, (rows, rows), 0)
    second = lax.broadcasted_iota(jnp.int32, (rows, rows), 1)
    if transposed:
        spread = across_ref[h : h + 1, :] - inside_ref[:, h : h + 1]
        return jnp.exp(jnp.where(second >= first, spread, -1e30))
    spread = inside_ref[:, h : h + 1] - across_ref[h : h + 1, :]
    return jnp.exp(jnp.where(first >= second, spread, -1e30))


def mixing_of(
    q_ref, k_ref, v_ref, g_ref, gain_ref, inside_ref, across_ref,
    near_ref, mix_turned_ref, query_ref, query_turned_ref, weights_ref, weights_turned_ref, scaled_ref,
):
    grown = jnp.exp(inside_ref[...])
    for h in range(inside_ref.shape[1]):
        cols = head_cols(h)
        queries, keys = q_ref[:, cols], k_ref[:, cols]
        weights = weights_of(inside_ref, across_ref, h)
        weights_ref[h] = weights
        mixing = (dot(queries, keys, NT) * weights).astype(BF16)
        near_ref[:, cols] = dot(mixing, v_ref[:, cols], NN)
        weights_turned = weights_of(inside_ref, across_ref, h, True)
        weights_turned_ref[h] = weights_turned
        mix_turned_ref[h] = (dot(keys, queries, NT) * weights_turned).astype(BF16)
        decayed = queries.astype(F32) * grown[:, h : h + 1]
        query_ref[:, cols] = decayed.astype(BF16)
        query_turned_ref[h] = decayed.T.astype(BF16)
        scaled_ref[:, cols] = g_ref[:, cols].astype(F32) * gain_ref[:, cols]


def mixing_first_kernel(core_ref, *refs):
    @pl.when(core_ref[0] == 0)
    def _():
        mixing_of(*refs)


def enter_kernel(core_ref, half_ref, keep_ref, got_ref, kept_ref, *refs):
    inputs, (own_ref, send_ref, *outputs) = refs[:7], refs[14:]
    core = core_ref[0]
    for i in range(half_ref.shape[0]):
        kept_first, _ = kept_rows(core, kept_ref, got_ref, i)
        first, _ = in_order(core, keep_ref[head_rows(i), :], got_ref[head_rows(i), :])
        state = half_ref[i]
        later = kept_first * state + first
        own_ref[i] = jnp.where(core == 0, state, later)
        send_ref[i] = jnp.where(core == 0, later, state)

    @pl.when(core == 1)
    def _():
        mixing_of(*inputs, *outputs)


def attend_half(base, near_ref, query_ref, half_ref, scaled_ref, att_ref, entering_ref, squares, crossed):
    for i in range(half_ref.shape[0]):
        h = base + i
        cols = pl.ds(pl.multiple_of(h * HEAD, HEAD), HEAD)
        state = half_ref[i].astype(BF16)
        entering_ref[h] = state
        attended = near_ref[:, cols] + dot(query_ref[:, cols], state, NN)
        att_ref[:, cols] = attended
        squares += attended * attended
        crossed += scaled_ref[:, cols] * attended
    return squares, crossed


def attend_own_kernel(
    core_ref, near_ref, query_ref, half_ref, scaled_ref, att_ref, entering_ref, squares_ref, crossed_ref
):
    zero = jnp.zeros(squares_ref.shape, F32)
    squares_ref[...], crossed_ref[...] = attend_half(
        core_ref[0] * half_ref.shape[0], near_ref, query_ref, half_ref, scaled_ref, att_ref, entering_ref, zero, zero
    )


def attend_other_kernel(
    core_ref, near_ref, query_ref, half_ref, scaled_ref, squares_ref, crossed_ref,
    att_in_ref, entering_in_ref, att_ref, entering_ref, sums_ref,
):
    squares, crossed = attend_half(
        (1 - core_ref[0]) * half_ref.shape[0], near_ref, query_ref, half_ref, scaled_ref, att_ref, entering_ref,
        squares_ref[...], crossed_ref[...],
    )
    sums = jnp.concatenate(
        [jnp.sum(squares, axis=1, keepdims=True), jnp.sum(crossed, axis=1, keepdims=True)], axis=1
    ).T
    for peer in range(sums_ref.shape[0]):
        sums_ref[peer] = sums


def norm_columns(sums_ref, rows):
    whole = jnp.sum(sums_ref[...], axis=0)
    first = lax.broadcasted_iota(jnp.int32, (rows, rows), 0)
    second = lax.broadcasted_iota(jnp.int32, (rows, rows), 1)
    same = first == second
    square_sum = jnp.sum(jnp.where(same, whole[0:1, :], 0.0), axis=1, keepdims=True)
    cross_sum = jnp.sum(jnp.where(same, whole[1:2, :], 0.0), axis=1, keepdims=True)
    width = HEAD_COUNT * HEAD
    inverse = lax.rsqrt(square_sum / width + EPSILON)
    return inverse, inverse * inverse * inverse * (cross_sum / width)


def norm_grad_kernel(core_ref, sums_ref, att_ref, scaled_ref, query_turned_ref, keep_ref, send_ref, gf_ref):
    rows, width = att_ref.shape
    inverse, factor = norm_columns(sums_ref, rows)

    def state_of(h):
        cols = head_cols(h)
        grad_flat = (inverse * scaled_ref[:, cols] - att_ref[:, cols] * factor).astype(BF16)
        gf_ref[:, cols] = grad_flat
        return dot(query_turned_ref[h], grad_flat, NN)

    deal_halves(core_ref[0], state_of, width // HEAD // 2, keep_ref, send_ref)


def send_out(copies, source, target, sems, i, cols):
    copy = pltpu.make_async_copy(source.at[:, cols], target.at[:, cols], sems.at[i])
    copy.start()
    copies.append(copy)


def near_grad(
    sums_ref, att_ref, gain_ref, gf_ref, q_ref, k_ref, v_ref, state_ref, inside_ref, weights_ref,
    weights_turned_ref, mix_turned_ref, normed_hbm, gq_hbm, gk_ref, gv_ref, normed_ref, gq_ref, sems,
):
    rows, heads = inside_ref.shape
    inverse, _ = norm_columns(sums_ref, rows)
    grown = jnp.exp(inside_ref[...])
    copies = []
    for h in range(heads):
        cols = head_cols(h)
        normed_ref[:, cols] = (att_ref[:, cols] * inverse * gain_ref[:, cols]).astype(BF16)
        grad_flat = gf_ref[:, cols]
        grad_mix = (dot(grad_flat, v_ref[:, cols], NT) * weights_ref[h]).astype(BF16)
        far = dot(grad_flat, state_ref[h], NT)
        gq_ref[:, cols] = (dot(grad_mix, k_ref[:, cols], NN) + grown[:, h : h + 1] * far).astype(BF16)
        if h % 2:
            pair = slice((h - 1) * HEAD, (h + 1) * HEAD)
            send_out(copies, normed_ref, normed_hbm, sems, h - 1, pair)
            send_out(copies, gq_ref, gq_hbm, sems, h, pair)
    for h in range(heads):
        cols = head_cols(h)
        grad_flat = gf_ref[:, cols]
        turned = (dot(v_ref[:, cols], grad_flat, NT) * weights_turned_ref[h]).astype(BF16)
        gk_ref[:, cols] = dot(turned, q_ref[:, cols], NN)
        gv_ref[:, cols] = dot(mix_turned_ref[h], grad_flat, NN)
    for copy in copies:
        copy.wait()


def near_first_kernel(core_ref, *refs):
    @pl.when(core_ref[0] == 0)
    def _():
        near_grad(*refs)


def leave_kernel(core_ref, half_ref, keep_ref, got_ref, kept_ref, got_kept_ref, *refs):
    inputs, (own_ref, send_ref, *outputs) = refs[:12], refs[16:]
    core = core_ref[0]
    for i in range(half_ref.shape[0]):
        _, kept_second = kept_rows(core, kept_ref, got_kept_ref, i)
        _, second = in_order(core, keep_ref[head_rows(i), :], got_ref[head_rows(i), :])
        state = half_ref[i]
        earlier = second + kept_second * state
        own_ref[i] = jnp.where(core == 0, earlier, state)
        send_ref[i] = jnp.where(core == 0, state, earlier)

    @pl.when(core == 1)
    def _():
        near_grad(*inputs, *outputs)


def far_half(
    base, gk_near_ref, gv_near_ref, key_ref, v_ref, half_ref, inside_ref, gk_hbm, gv_hbm, gk_ref, gv_ref, sems
):
    rows, heads = inside_ref.shape
    inside = inside_ref[...]
    shares = jnp.exp(inside[rows - 1 : rows, :] - inside)
    head = lax.broadcasted_iota(jnp.int32, (rows, heads), 1)
    copies = []
    for i in range(half_ref.shape[0]):
        cols = pl.ds(pl.multiple_of((base + i) * HEAD, HEAD), HEAD)
        share = jnp.sum(jnp.where(head == base + i, shares, 0.0), axis=1, keepdims=True)
        arriving = half_ref[i].astype(BF16)
        far = dot(v_ref[:, cols], arriving, NT)
        gk_ref[:, cols] = (gk_near_ref[:, cols] + share * far).astype(BF16)
        gv_ref[:, cols] = (gv_near_ref[:, cols] + dot(key_ref[:, cols], arriving, NN)).astype(BF16)
        if i % 2:
            pair = pl.ds(pl.multiple_of((base + i - 1) * HEAD, 2 * HEAD), 2 * HEAD)
            send_out(copies, gk_ref, gk_hbm, sems, i - 1, pair)
            send_out(copies, gv_ref, gv_hbm, sems, i, pair)
    for copy in copies:
        copy.wait()


def far_own_kernel(core_ref, gk_near_ref, gv_near_ref, key_ref, v_ref, half_ref, inside_ref, *refs):
    base = core_ref[0] * half_ref.shape[0]
    far_half(base, gk_near_ref, gv_near_ref, key_ref, v_ref, half_ref, inside_ref, *refs)


def far_other_kernel(core_ref, gk_near_ref, gv_near_ref, key_ref, v_ref, half_ref, inside_ref, gk_in, gv_in, *refs):
    base = (1 - core_ref[0]) * half_ref.shape[0]
    far_half(base, gk_near_ref, gv_near_ref, key_ref, v_ref, half_ref, inside_ref, *refs)


def body(chips, tp_size, queries, key_vectors, values, decay_log, norm_gain, grad_out):
    rows, width = queries.shape
    heads = decay_log.shape[1]
    half = heads // 2
    slab = half * HEAD // chips
    core = lax.axis_index("core").astype(jnp.int32).reshape(1)
    gain = norm_gain.reshape(1, width)
    wide, tile, half_state = (rows, width), (chips, slab, HEAD), (half, HEAD, HEAD)
    whole, size = rows * width, heads * HEAD * HEAD

    def across_chips(array):
        return lax.all_to_all(array, ("x", "y"), 0, 0)

    def swap(array):
        return lax.ppermute(array, "core", [(0, 1), (1, 0)])

    wide_bf, wide_f32 = ("v", wide, BF16), ("v", wide, F32)
    square, per_token = (heads, rows, rows), ("v", (rows, heads), F32)
    half_rows, half_tile = ("v", (half * HEAD, HEAD), F32), ("v", half_state, F32)
    on_core = ("s", core)

    def vmem(*arrays):
        return [("v", a) for a in arrays]

    def like(outs, arrays):
        return [(m, a) for (m, _, _), a in zip(outs, arrays)]

    inputs = [queries, key_vectors, values, grad_out, decay_log.T, gain]
    keep, send, kept, inside, across, key_decayed, q, k, v, g, gain = call(
        local_kernel,
        [
            half_rows, ("v", (half * HEAD + heads, HEAD), F32), ("v", (heads, HEAD), F32), per_token,
            ("v", (heads, rows), F32), wide_bf, wide_bf, wide_bf, wide_bf, wide_bf, ("v", (1, width), F32),
        ],
        [on_core] + [("h", a) for a in inputs],
        2 * whole * HEAD, 8 * whole,
        scratch=[pltpu.VMEM((heads, rows), F32), pltpu.SemaphoreType.DMA((6,))],
    )
    got = swap(send)
    mixing_args = vmem(q, k, v, g, gain, inside, across)
    mixing_outs = [
        wide_f32, ("v", square, BF16), wide_bf, ("v", (heads, HEAD, rows), BF16), ("v", square, F32),
        ("v", square, F32), wide_f32,
    ]
    mixing_done = call(mixing_first_kernel, mixing_outs, [on_core] + mixing_args, 6 * whole * rows, 12 * whole)
    (pay,) = call(
        forward_join_kernel,
        [("v", (chips * (slab + 1), HEAD), F32)],
        [on_core, ("a", mixing_done[0])] + vmem(keep, got, kept),
        2 * size, 12 * size,
    )
    pay = across_chips(pay.reshape(chips, 1, (slab + 1) * HEAD)).reshape(chips * (slab + 1), HEAD)
    tiles, kept_chips = call(
        forward_scan_kernel,
        [("v", tile, F32), ("v", (chips, HEAD), F32)],
        vmem(pay),
        size, 4 * size,
    )
    half_in = across_chips(tiles).reshape(half_state)
    half_own, half_send, near, mixing_turned, query_decayed, query_turned, weights, weights_turned, scaled = call(
        enter_kernel,
        [half_tile, half_tile] + mixing_outs,
        [on_core] + vmem(half_in, keep, got, kept) + mixing_args + like(mixing_outs, mixing_done),
        6 * whole * rows, 12 * whole, aliases={12 + i: 2 + i for i in range(7)},
    )
    half_other = swap(half_send)
    entering_bf, column = ("v", (heads, HEAD, HEAD), BF16), ("v", (rows, HEAD), F32)
    attended, entering, squares, crossed = call(
        attend_own_kernel,
        [wide_f32, entering_bf, column, column],
        [on_core] + vmem(near, query_decayed, half_own, scaled),
        whole * HEAD, 6 * whole,
    )
    attended, entering, sums = call(
        attend_other_kernel,
        [wide_f32, entering_bf, ("v", (tp_size, 2, rows), F32)],
        [on_core] + vmem(near, query_decayed, half_other, scaled, squares, crossed, attended, entering),
        whole * HEAD, 6 * whole, aliases={7: 0, 8: 1},
    )
    sums = lax.all_to_all(sums, "tp", 0, 0)
    back_keep, back_send, grad_flat = call(
        norm_grad_kernel,
        [half_rows, half_rows, wide_bf],
        [on_core] + vmem(sums, attended, scaled, query_turned),
        2 * whole * HEAD, 12 * whole,
    )
    back_got = swap(back_send)
    near_args = vmem(
        sums, attended, gain, grad_flat, q, k, v, entering, inside, weights, weights_turned, mixing_turned
    )
    near_outs = [("h", wide, BF16), ("h", wide, BF16), wide_f32, wide_f32]
    outputs = [pltpu.VMEM(wide, BF16), pltpu.VMEM(wide, BF16), pltpu.SemaphoreType.DMA((heads,))]
    near_done = call(
        near_first_kernel, near_outs, [on_core] + near_args, 12 * whole * rows, 16 * whole, scratch=outputs
    )
    (pay_back,) = call(
        reverse_join_kernel,
        [half_rows],
        [on_core, ("a", near_done[2])] + vmem(back_keep, back_got, kept, got),
        2 * size, 12 * size,
    )
    (tiles_back,) = call(
        reverse_scan_kernel,
        [("v", tile, F32)],
        vmem(across_chips(pay_back.reshape(tile)), kept_chips),
        size, 4 * size,
    )
    half_back = across_chips(tiles_back).reshape(half_state)
    arriving_own, arriving_send, normed, grad_query, grad_key_near, grad_value_near = call(
        leave_kernel,
        [half_tile, half_tile] + near_outs,
        [on_core] + vmem(half_back, back_keep, back_got, kept, got) + near_args + like(near_outs, near_done),
        12 * whole * rows, 16 * whole, scratch=outputs, aliases={18 + i: 2 + i for i in range(4)},
    )
    arriving_other = swap(arriving_send)
    far_outs = [("h", wide, BF16), ("h", wide, BF16)]
    far_args = vmem(grad_key_near, grad_value_near, key_decayed, v)
    far_done = call(
        far_own_kernel, far_outs, [on_core] + far_args + vmem(arriving_own, inside),
        2 * whole * HEAD, 8 * whole, scratch=outputs,
    )
    grad_key, grad_value = call(
        far_other_kernel, far_outs,
        [on_core] + far_args + vmem(arriving_other, inside) + like(far_outs, far_done),
        2 * whole * HEAD, 8 * whole, scratch=outputs, aliases={7: 0, 8: 1},
    )
    return normed, grad_query, grad_key, grad_value


def solution(mesh):
    seq, tp = mesh.shape["seq"], mesh.shape["tp"]
    fine = Mesh(mesh.devices.reshape(seq // 16, 8, 2, tp), ("x", "y", "core", "tp"))
    spec = P(("x", "y", "core"), "tp")
    return jax.shard_map(
        functools.partial(body, seq // 2, tp),
        mesh=fine,
        in_specs=(spec, spec, spec, spec, P("tp"), spec),
        out_specs=(spec, spec, spec, spec),
        check_vma=False,
    )
```

time: 112 us -> 109 us (0.973)
  starting transfers between devices: 23.5 us -> 19.8 us
  waiting for transfers between devices: 0.9 us -> 3.19 us
    ppermute x4, starting transfers between devices: 23.5 us -> 19.8 us  [swap(): return lax.ppermute(array, 'core', [(0, 1), (1, 0)])]
    ppermute x4, waiting for transfers between devices: 0.9 us -> 3.19 us  [swap(): return lax.ppermute(array, 'core', [(0, 1), (1, 0)])]
    pallas_call x12 -> x14, Pallas kernels: 8.93 us -> 9.11 us  [call(): pl.pallas_call(kernel, out_shape=[SPACES[m](s, d) for m, s, d in outs], i...]
  transfers between devices with their start and end apart: 4 -> 4, of which waited for: 1 -> 4; matrix products, arithmetic and copies ran while one was open for 0% -> 0% of each run, Pallas kernels for 4% -> 1%
where the time goes in v5:
time: 109 us
  blocking collectives  76.2 us (70%)
  starting transfers between devices  19.8 us (18%)
  Pallas kernels  9.11 us (8%)
  waiting for transfers between devices  3.19 us (3%)
    all_to_all x4, blocking collectives, across_chips(): return lax.all_to_all(array, ('x', 'y'), 0, 0)  59.7 us
    ppermute x4, starting transfers between devices, swap(): return lax.ppermute(array, 'core', [(0, 1), (1, 0)])  19.8 us
    all_to_all x1, blocking collectives, body(): sums = lax.all_to_all(sums, 'tp', 0, 0)  16.5 us
    pallas_call x14, Pallas kernels, call(): pl.pallas_call(kernel, out_shape=[SPACES[m](s, d) for m, s, d in outs], i...  9.11 us
    ppermute x4, waiting for transfers between devices, swap(): return lax.ppermute(array, 'core', [(0, 1), (1, 0)])  3.19 us
  transfers between devices with their start and end apart: 4, of which 4 were waited for; matrix products, arithmetic and copies ran while one was open for 0% of the time, Pallas kernels for 1%

profile of v5, /device:TPU:1, one launch (start us, length us, event | category | flops | bytes accessed | tf_op | source)
XLA Modules:
  0.0 109.0 jit_solution(11483434946385547866)
XLA Ops:
  0.6 1.7 %shard_map.93 = (f32[512,128]{1,0:T(8,128)S(1)}, f32[520,128]{1,0:T(8,128)S(1)}, f32[8,128]{1,0:T(8,128)S(1)}, f32[160,8]{1,0:T(8,128)S(1)}, f32[8,160]{1,0:T(8,...) custom-call(s32[1]{0:T(128)} %bitcast.core_ref, ...), custom_call_target="tpu_custom_call" | custom-call | flops 41943040 | bytes 1310720 | tf_op jit(solution)/shard_map/pallas_call | solution.py:31
  2.4 8.8 %collective-permute-start = (f32[520,128]{1,0:T(8,128)S(1)}, f32[520,128]{1,0:T(8,128)S(1)}, u32[]{:S(2)}, u32[]{:S(2)}) collective-permute-start(f32[520,128]{1,0:T(8,128)S(1)} %get-tuple-element.66), channel_id=1, source_target_pairs={{0,8},{8,0},{1,9},{9,1},{2,10},{10,2},{3,11},{11,3},{4,12},{12,4},... | collective-permute-start | bytes 798728 | tf_op jit(solution)/shard_map/ppermute | solution.py:374
  11.2 1.1 %collective-permute-done.got_ref.got_kept_ref = f32[520,128]{1,0:T(8,128)S(1)} collective-permute-done((f32[520,128]{1,0:T(8,128)S(1)}, f32[520,128]{1,0:T(8,128)S(1)}, u32[]{:S(2)}, u32[]{:S(2)}) %collective-permute-start) | collective-permute-done | bytes 266272 | tf_op jit(solution)/shard_map/ppermute | solution.py:374
  12.4 13.8 %all_to_all.25 = f32[32,1,2176]{2,1,0:T(1,128)S(1)} all-to-all(f32[32,1,2176]{2,1,0:T(1,128)S(1)} %bitcast.9), channel_id=1, replica_groups=mesh['x'=4,'y'=8,'core'=2,'tp'=8] {'x','y'}, dimensions={0} | all-to-all | bytes 557056 | tf_op jit(solution)/shard_map/all_to_all | solution.py:371
  26.2 0.1 shard_map.96
  26.3 16.5 %all_to_all.26 = f32[32,16,128]{2,1,0:T(8,128)S(1)} all-to-all(f32[32,16,128]{2,1,0:T(8,128)S(1)} %get-tuple-element.68), channel_id=1, replica_groups=mesh['x'=4,'y'=8,'core'=2,'tp'=8] {'x','y'}, dimensions={0} | all-to-all | bytes 524288 | tf_op jit(solution)/shard_map/all_to_all | solution.py:371
  42.8 1.6 %shard_map.97 = (f32[4,128,128]{2,1,0:T(8,128)S(1)}, f32[4,128,128]{2,1,0:T(8,128)S(1)}, f32[160,1024]{1,0:T(8,128)S(1)}, bf16[8,160,160]{2,1,0:T(8,128)(2,1)S(1...) custom-call(s32[1]{0:T(128)} %bitcast.core_ref, ...), custom_call_target="tpu_custom_call", output_to_operand_aliasing={{2}: (12, {}), {3}: (13, {}), {4}: (14, {}), {5}: (15, {}),... | custom-call | flops 157286400 | bytes 1966080 | tf_op jit(solution)/shard_map/pallas_call | solution.py:31
  44.3 4.0 %collective-permute-start.1 = (f32[4,128,128]{2,1,0:T(8,128)S(1)}, f32[4,128,128]{2,1,0:T(8,128)S(1)}, u32[]{:S(2)}, u32[]{:S(2)}) collective-permute-start(f32[4,128,128]{2,1,0:T(8,128)S(1)} %get-tuple-element.77), channel_id=1, source_target_pairs={{0,8},{8,0},{1,9},{9,1},{2,10},{10,2},{3,11},{11,3},{4,12},{12,4},... | collective-permute-start | bytes 786440 | tf_op jit(solution)/shard_map/ppermute | solution.py:374
  48.3 0.2 shard_map.98
  48.6 0.9 collective-permute-done.1.half_ref
  49.5 0.4 shard_map.99
  49.8 16.5 %all_to_all.27.sums_ref.refs_0_ = f32[8,2,160]{2,1,0:T(2,128)S(1)} all-to-all(f32[8,2,160]{2,1,0:T(2,128)S(1)} %get-tuple-element.84), channel_id=1, replica_groups=mesh['x'=4,'y'=8,'core'=2,'tp'=8] {'tp'}, dimensions={0} | all-to-all | bytes 20480 | tf_op jit(solution)/shard_map/all_to_all | solution.py:439
  66.3 0.4 shard_map.100
  66.8 3.7 %collective-permute-start.2 = (f32[512,128]{1,0:T(8,128)S(1)}, f32[512,128]{1,0:T(8,128)S(1)}, u32[]{:S(2)}, u32[]{:S(2)}) collective-permute-start(f32[512,128]{1,0:T(8,128)S(1)} %get-tuple-element.94), channel_id=1, source_target_pairs={{0,8},{8,0},{1,9},{9,1},{2,10},{10,2},{3,11},{11,3},{4,12},{12,4},... | collective-permute-start | bytes 786440 | tf_op jit(solution)/shard_map/ppermute | solution.py:374
  70.5 0.1 shard_map.101
  70.6 1.0 collective-permute-done.2.got_ref
  71.7 13.7 %all_to_all.28.got_ref = f32[32,16,128]{2,1,0:T(8,128)S(1)} all-to-all(f32[32,16,128]{2,1,0:T(8,128)S(1)} %bitcast.12), channel_id=1, replica_groups=mesh['x'=4,'y'=8,'core'=2,'tp'=8] {'x','y'}, dimensions={0} | all-to-all | bytes 524288 | tf_op jit(solution)/shard_map/all_to_all | solution.py:371
  85.4 0.1 shard_map.103
  85.5 15.7 %all_to_all.29 = f32[32,16,128]{2,1,0:T(8,128)S(1)} all-to-all(f32[32,16,128]{2,1,0:T(8,128)S(1)} %shard_map.103), channel_id=1, replica_groups=mesh['x'=4,'y'=8,'core'=2,'tp'=8] {'x','y'}, dimensions={0} | all-to-all | bytes 524288 | tf_op jit(solution)/shard_map/all_to_all | solution.py:371
  101.2 2.4 %shard_map.104 = (f32[4,128,128]{2,1,0:T(8,128)S(1)}, f32[4,128,128]{2,1,0:T(8,128)S(1)}, bf16[160,1024]{1,0:T(8,128)(2,1)}, bf16[160,1024]{1,0:T(8,128)(2,1)}, ...) custom-call(s32[1]{0:T(128)} %bitcast.core_ref, ...), custom_call_target="tpu_custom_call", output_to_operand_aliasing={{2}: (18, {}), {3}: (19, {}), {4}: (20, {}), {5}: (21, {})} | custom-call | flops 314572800 | bytes 2621440 | tf_op jit(solution)/shard_map/pallas_call | solution.py:31
  103.6 3.3 %collective-permute-start.3 = (f32[4,128,128]{2,1,0:T(8,128)S(1)}, f32[4,128,128]{2,1,0:T(8,128)S(1)}, u32[]{:S(2)}, u32[]{:S(2)}) collective-permute-start(f32[4,128,128]{2,1,0:T(8,128)S(1)} %get-tuple-element.104), channel_id=1, source_target_pairs={{0,8},{8,0},{1,9},{9,1},{2,10},{10,2},{3,11},{11,3},{4,12},{12,4},... | collective-permute-start | bytes 786440 | tf_op jit(solution)/shard_map/ppermute | solution.py:374
  106.9 1.0 shard_map.105
  107.9 0.1 collective-permute-done.3.half_ref
  108.0 1.0 shard_map.106
  (3 shorter events, 0.1 us)
Async XLA Ops:
  2.4 9.9 %collective-permute-start = (f32[520,128]{1,0:T(8,128)S(1)}, f32[520,128]{1,0:T(8,128)S(1)}, u32[]{:S(2)}, u32[]{:S(2)}) collective-permute-start(f32[520,128]{1,0:T(8,128)S(1)} %get-tuple-element.66), channel_id=1, source_target_pairs={{0,8},{8,0},{1,9},{9,1},{2,10},{10,2},{3,11},{11,3},{4,12},{12,4},... | collective-permute-start | bytes 798728 | tf_op jit(solution)/shard_map/ppermute | solution.py:374
  44.3 5.1 %collective-permute-start.1 = (f32[4,128,128]{2,1,0:T(8,128)S(1)}, f32[4,128,128]{2,1,0:T(8,128)S(1)}, u32[]{:S(2)}, u32[]{:S(2)}) collective-permute-start(f32[4,128,128]{2,1,0:T(8,128)S(1)} %get-tuple-element.77), channel_id=1, source_target_pairs={{0,8},{8,0},{1,9},{9,1},{2,10},{10,2},{3,11},{11,3},{4,12},{12,4},... | collective-permute-start | bytes 786440 | tf_op jit(solution)/shard_map/ppermute | solution.py:374
  66.8 4.9 %collective-permute-start.2 = (f32[512,128]{1,0:T(8,128)S(1)}, f32[512,128]{1,0:T(8,128)S(1)}, u32[]{:S(2)}, u32[]{:S(2)}) collective-permute-start(f32[512,128]{1,0:T(8,128)S(1)} %get-tuple-element.94), channel_id=1, source_target_pairs={{0,8},{8,0},{1,9},{9,1},{2,10},{10,2},{3,11},{11,3},{4,12},{12,4},... | collective-permute-start | bytes 786440 | tf_op jit(solution)/shard_map/ppermute | solution.py:374
  103.6 4.4 %collective-permute-start.3 = (f32[4,128,128]{2,1,0:T(8,128)S(1)}, f32[4,128,128]{2,1,0:T(8,128)S(1)}, u32[]{:S(2)}, u32[]{:S(2)}) collective-permute-start(f32[4,128,128]{2,1,0:T(8,128)S(1)} %get-tuple-element.104), channel_id=1, source_target_pairs={{0,8},{8,0},{1,9},{9,1},{2,10},{10,2},{3,11},{11,3},{4,12},{12,4},... | collective-permute-start | bytes 786440 | tf_op jit(solution)/shard_map/ppermute | solution.py:374

commit v6 on v5

--- a/solution.py
+++ b/solution.py
@@ -183,7 +183,7 @@
         scaled_ref[:, cols] = g_ref[:, cols].astype(F32) * gain_ref[:, cols]
 
 
-def mixing_first_kernel(core_ref, *refs):
+def mixing_first_kernel(core_ref, after_ref, *refs):
     @pl.when(core_ref[0] == 0)
     def _():
         mixing_of(*refs)
@@ -401,7 +401,7 @@
         wide_f32, ("v", square, BF16), wide_bf, ("v", (heads, HEAD, rows), BF16), ("v", square, F32),
         ("v", square, F32), wide_f32,
     ]
-    mixing_done = call(mixing_first_kernel, mixing_outs, [on_core] + mixing_args, 6 * whole * rows, 12 * whole)
+    mixing_done = call(mixing_first_kernel, mixing_outs, [on_core, ("a", got)] + mixing_args, 6 * whole * rows, 12 * whole)
     (pay,) = call(
         forward_join_kernel,
         [("v", (chips * (slab + 1), HEAD), F32)],

time: 109 us -> 109 us (level)
  blocking collectives: 76.2 us -> 74.6 us
    all_to_all x4, blocking collectives: 59.7 us -> 58.1 us  [across_chips(): return lax.all_to_all(array, ('x', 'y'), 0, 0)]
where the time goes in v6:
time: 109 us; the launch traced here: 108 us
  blocking collectives  74.6 us (68%)
  starting transfers between devices  20.5 us (19%)
  Pallas kernels  9.11 us (8%)
  waiting for transfers between devices  3.21 us (3%)
    all_to_all x4, blocking collectives, across_chips(): return lax.all_to_all(array, ('x', 'y'), 0, 0)  58.1 us
    ppermute x4, starting transfers between devices, swap(): return lax.ppermute(array, 'core', [(0, 1), (1, 0)])  20.5 us
    all_to_all x1, blocking collectives, body(): sums = lax.all_to_all(sums, 'tp', 0, 0)  16.5 us
    pallas_call x14, Pallas kernels, call(): pl.pallas_call(kernel, out_shape=[SPACES[m](s, d) for m, s, d in outs], i...  9.11 us
    ppermute x4, waiting for transfers between devices, swap(): return lax.ppermute(array, 'core', [(0, 1), (1, 0)])  3.21 us
  transfers between devices with their start and end apart: 4, of which 4 were waited for; matrix products, arithmetic and copies ran while one was open for 0% of the time, Pallas kernels for 1%

profile of v6, /device:TPU:1, one launch (start us, length us, event | category | flops | bytes accessed | tf_op | source)
XLA Modules:
  0.0 108.1 jit_solution(4786742280525111773)
XLA Ops:
  0.6 1.7 %shard_map.93 = (f32[512,128]{1,0:T(8,128)S(1)}, f32[520,128]{1,0:T(8,128)S(1)}, f32[8,128]{1,0:T(8,128)S(1)}, f32[160,8]{1,0:T(8,128)S(1)}, f32[8,160]{1,0:T(8,...) custom-call(s32[1]{0:T(128)} %bitcast.core_ref, ...), custom_call_target="tpu_custom_call" | custom-call | flops 41943040 | bytes 1310720 | tf_op jit(solution)/shard_map/pallas_call | solution.py:31
  2.4 8.8 %collective-permute-start = (f32[520,128]{1,0:T(8,128)S(1)}, f32[520,128]{1,0:T(8,128)S(1)}, u32[]{:S(2)}, u32[]{:S(2)}) collective-permute-start(f32[520,128]{1,0:T(8,128)S(1)} %get-tuple-element.57), channel_id=1, source_target_pairs={{0,8},{8,0},{1,9},{9,1},{2,10},{10,2},{3,11},{11,3},{4,12},{12,4},... | collective-permute-start | bytes 798728 | tf_op jit(solution)/shard_map/ppermute | solution.py:374
  11.2 1.1 %collective-permute-done.after_ref.got_ref.got_kept_ref = f32[520,128]{1,0:T(8,128)S(1)} collective-permute-done((f32[520,128]{1,0:T(8,128)S(1)}, f32[520,128]{1,0:T(8,128)S(1)}, u32[]{:S(2)}, u32[]{:S(2)}) %collective-permute-start) | collective-permute-done | bytes 266272 | tf_op jit(solution)/shard_map/ppermute | solution.py:374
  12.4 13.8 %all_to_all.25 = f32[32,1,2176]{2,1,0:T(1,128)S(1)} all-to-all(f32[32,1,2176]{2,1,0:T(1,128)S(1)} %bitcast.9), channel_id=1, replica_groups=mesh['x'=4,'y'=8,'core'=2,'tp'=8] {'x','y'}, dimensions={0} | all-to-all | bytes 557056 | tf_op jit(solution)/shard_map/all_to_all | solution.py:371
  26.2 0.1 shard_map.96
  26.3 14.9 %all_to_all.26 = f32[32,16,128]{2,1,0:T(8,128)S(1)} all-to-all(f32[32,16,128]{2,1,0:T(8,128)S(1)} %get-tuple-element.68), channel_id=1, replica_groups=mesh['x'=4,'y'=8,'core'=2,'tp'=8] {'x','y'}, dimensions={0} | all-to-all | bytes 524288 | tf_op jit(solution)/shard_map/all_to_all | solution.py:371
  41.2 1.6 %shard_map.97 = (f32[4,128,128]{2,1,0:T(8,128)S(1)}, f32[4,128,128]{2,1,0:T(8,128)S(1)}, f32[160,1024]{1,0:T(8,128)S(1)}, bf16[8,160,160]{2,1,0:T(8,128)(2,1)S(1...) custom-call(s32[1]{0:T(128)} %bitcast.core_ref, ...), custom_call_target="tpu_custom_call", output_to_operand_aliasing={{2}: (12, {}), {3}: (13, {}), {4}: (14, {}), {5}: (15, {}),... | custom-call | flops 157286400 | bytes 1966080 | tf_op jit(solution)/shard_map/pallas_call | solution.py:31
  42.8 4.7 %collective-permute-start.1 = (f32[4,128,128]{2,1,0:T(8,128)S(1)}, f32[4,128,128]{2,1,0:T(8,128)S(1)}, u32[]{:S(2)}, u32[]{:S(2)}) collective-permute-start(f32[4,128,128]{2,1,0:T(8,128)S(1)} %get-tuple-element.77), channel_id=1, source_target_pairs={{0,8},{8,0},{1,9},{9,1},{2,10},{10,2},{3,11},{11,3},{4,12},{12,4},... | collective-permute-start | bytes 786440 | tf_op jit(solution)/shard_map/ppermute | solution.py:374
  47.5 0.2 shard_map.98
  47.7 0.9 collective-permute-done.1.half_ref
  48.6 0.4 shard_map.99
  49.0 16.5 %all_to_all.27.sums_ref.refs_0_ = f32[8,2,160]{2,1,0:T(2,128)S(1)} all-to-all(f32[8,2,160]{2,1,0:T(2,128)S(1)} %get-tuple-element.84), channel_id=1, replica_groups=mesh['x'=4,'y'=8,'core'=2,'tp'=8] {'tp'}, dimensions={0} | all-to-all | bytes 20480 | tf_op jit(solution)/shard_map/all_to_all | solution.py:439
  65.5 0.5 shard_map.100
  66.0 3.7 %collective-permute-start.2 = (f32[512,128]{1,0:T(8,128)S(1)}, f32[512,128]{1,0:T(8,128)S(1)}, u32[]{:S(2)}, u32[]{:S(2)}) collective-permute-start(f32[512,128]{1,0:T(8,128)S(1)} %get-tuple-element.94), channel_id=1, source_target_pairs={{0,8},{8,0},{1,9},{9,1},{2,10},{10,2},{3,11},{11,3},{4,12},{12,4},... | collective-permute-start | bytes 786440 | tf_op jit(solution)/shard_map/ppermute | solution.py:374
  69.7 0.1 shard_map.101
  69.8 1.0 collective-permute-done.2.got_ref
  70.9 13.6 %all_to_all.28.got_ref = f32[32,16,128]{2,1,0:T(8,128)S(1)} all-to-all(f32[32,16,128]{2,1,0:T(8,128)S(1)} %bitcast.12), channel_id=1, replica_groups=mesh['x'=4,'y'=8,'core'=2,'tp'=8] {'x','y'}, dimensions={0} | all-to-all | bytes 524288 | tf_op jit(solution)/shard_map/all_to_all | solution.py:371
  84.5 0.1 shard_map.103
  84.5 15.7 %all_to_all.29 = f32[32,16,128]{2,1,0:T(8,128)S(1)} all-to-all(f32[32,16,128]{2,1,0:T(8,128)S(1)} %shard_map.103), channel_id=1, replica_groups=mesh['x'=4,'y'=8,'core'=2,'tp'=8] {'x','y'}, dimensions={0} | all-to-all | bytes 524288 | tf_op jit(solution)/shard_map/all_to_all | solution.py:371
  100.2 2.4 %shard_map.104 = (f32[4,128,128]{2,1,0:T(8,128)S(1)}, f32[4,128,128]{2,1,0:T(8,128)S(1)}, bf16[160,1024]{1,0:T(8,128)(2,1)}, bf16[160,1024]{1,0:T(8,128)(2,1)}, ...) custom-call(s32[1]{0:T(128)} %bitcast.core_ref, ...), custom_call_target="tpu_custom_call", output_to_operand_aliasing={{2}: (18, {}), {3}: (19, {}), {4}: (20, {}), {5}: (21, {})} | custom-call | flops 314572800 | bytes 2621440 | tf_op jit(solution)/shard_map/pallas_call | solution.py:31
  102.7 3.3 %collective-permute-start.3 = (f32[4,128,128]{2,1,0:T(8,128)S(1)}, f32[4,128,128]{2,1,0:T(8,128)S(1)}, u32[]{:S(2)}, u32[]{:S(2)}) collective-permute-start(f32[4,128,128]{2,1,0:T(8,128)S(1)} %get-tuple-element.104), channel_id=1, source_target_pairs={{0,8},{8,0},{1,9},{9,1},{2,10},{10,2},{3,11},{11,3},{4,12},{12,4},... | collective-permute-start | bytes 786440 | tf_op jit(solution)/shard_map/ppermute | solution.py:374
  105.9 1.0 shard_map.105
  107.0 0.1 collective-permute-done.3.half_ref
  107.1 1.0 shard_map.106
  (3 shorter events, 0.1 us)
Async XLA Ops:
  2.4 9.9 %collective-permute-start = (f32[520,128]{1,0:T(8,128)S(1)}, f32[520,128]{1,0:T(8,128)S(1)}, u32[]{:S(2)}, u32[]{:S(2)}) collective-permute-start(f32[520,128]{1,0:T(8,128)S(1)} %get-tuple-element.57), channel_id=1, source_target_pairs={{0,8},{8,0},{1,9},{9,1},{2,10},{10,2},{3,11},{11,3},{4,12},{12,4},... | collective-permute-start | bytes 798728 | tf_op jit(solution)/shard_map/ppermute | solution.py:374
  42.8 5.9 %collective-permute-start.1 = (f32[4,128,128]{2,1,0:T(8,128)S(1)}, f32[4,128,128]{2,1,0:T(8,128)S(1)}, u32[]{:S(2)}, u32[]{:S(2)}) collective-permute-start(f32[4,128,128]{2,1,0:T(8,128)S(1)} %get-tuple-element.77), channel_id=1, source_target_pairs={{0,8},{8,0},{1,9},{9,1},{2,10},{10,2},{3,11},{11,3},{4,12},{12,4},... | collective-permute-start | bytes 786440 | tf_op jit(solution)/shard_map/ppermute | solution.py:374
  66.0 4.9 %collective-permute-start.2 = (f32[512,128]{1,0:T(8,128)S(1)}, f32[512,128]{1,0:T(8,128)S(1)}, u32[]{:S(2)}, u32[]{:S(2)}) collective-permute-start(f32[512,128]{1,0:T(8,128)S(1)} %get-tuple-element.94), channel_id=1, source_target_pairs={{0,8},{8,0},{1,9},{9,1},{2,10},{10,2},{3,11},{11,3},{4,12},{12,4},... | collective-permute-start | bytes 786440 | tf_op jit(solution)/shard_map/ppermute | solution.py:374
  102.7 4.4 %collective-permute-start.3 = (f32[4,128,128]{2,1,0:T(8,128)S(1)}, f32[4,128,128]{2,1,0:T(8,128)S(1)}, u32[]{:S(2)}, u32[]{:S(2)}) collective-permute-start(f32[4,128,128]{2,1,0:T(8,128)S(1)} %get-tuple-element.104), channel_id=1, source_target_pairs={{0,8},{8,0},{1,9},{9,1},{2,10},{10,2},{3,11},{11,3},{4,12},{12,4},... | collective-permute-start | bytes 786440 | tf_op jit(solution)/shard_map/ppermute | solution.py:374

commit v7 on v6

--- a/solution.py
+++ b/solution.py
@@ -50,16 +50,18 @@
     return slice(h * HEAD, (h + 1) * HEAD)
 
 
-def deal_halves(core, state_of, half, keep_ref, send_ref):
-    for i in range(half):
-        low, high = state_of(i), state_of(half + i)
-        keep_ref[head_rows(i), :] = jnp.where(core == 0, low, high)
-        send_ref[head_rows(i), :] = jnp.where(core == 0, high, low)
+def half_of_heads(core, half, sent, state_of, out_ref):
+    for place in range(2):
+
+        @pl.when(core == place)
+        def _(first=(place ^ sent) * half):
+            for i in range(half):
+                out_ref[head_rows(i), :] = state_of(first + i)
 
 
 def local_kernel(
     core_ref, q_hbm, k_hbm, v_hbm, g_hbm, decay_hbm, gain_hbm,
-    keep_ref, send_ref, kept_ref, inside_ref, across_ref, key_ref, q_ref, k_ref, v_ref, g_ref, gain_ref, decay_ref, sems,
+    send_ref, kept_ref, inside_ref, across_ref, q_ref, k_ref, v_ref, g_ref, gain_ref, decay_ref, sems,
 ):
     heads, rows = decay_ref.shape
     pieces = [
@@ -93,12 +95,25 @@
     def state_of(h):
         cols = head_cols(h)
         key_decayed = (k_ref[:, cols].astype(F32) * shares[:, h : h + 1]).astype(BF16)
-        key_ref[:, cols] = key_decayed
         return dot(key_decayed, v_ref[:, cols], TN)
 
-    deal_halves(core_ref[0], state_of, heads // 2, keep_ref, send_ref)
+    half_of_heads(core_ref[0], heads // 2, 1, state_of, send_ref)
     for copy in copies[3:]:
         copy.wait()
+
+
+def local_keep_kernel(core_ref, k_ref, v_ref, inside_ref, keep_ref, key_ref):
+    rows, heads = inside_ref.shape
+    inside = inside_ref[...]
+    shares = jnp.exp(inside[rows - 1 : rows, :] - inside)
+    for h in range(heads):
+        cols = head_cols(h)
+        key_ref[:, cols] = (k_ref[:, cols].astype(F32) * shares[:, h : h + 1]).astype(BF16)
+
+    def state_of(h):
+        return dot(key_ref[:, head_cols(h)], v_ref[:, head_cols(h)], TN)
+
+    half_of_heads(core_ref[0], heads // 2, 0, state_of, keep_ref)
 
 
 def kept_rows(core, own_ref, got_ref, i):
@@ -254,17 +269,30 @@
     return inverse, inverse * inverse * inverse * (cross_sum / width)
 
 
-def norm_grad_kernel(core_ref, sums_ref, att_ref, scaled_ref, query_turned_ref, keep_ref, send_ref, gf_ref):
+def norm_grad_kernel(core_ref, sums_ref, att_ref, scaled_ref, query_turned_ref, send_ref, columns_ref):
     rows, width = att_ref.shape
     inverse, factor = norm_columns(sums_ref, rows)
+    columns_ref[...] = jnp.concatenate([inverse, factor], axis=1)
 
     def state_of(h):
         cols = head_cols(h)
         grad_flat = (inverse * scaled_ref[:, cols] - att_ref[:, cols] * factor).astype(BF16)
-        gf_ref[:, cols] = grad_flat
         return dot(query_turned_ref[h], grad_flat, NN)
 
-    deal_halves(core_ref[0], state_of, width // HEAD // 2, keep_ref, send_ref)
+    half_of_heads(core_ref[0], width // HEAD // 2, 1, state_of, send_ref)
+
+
+def norm_grad_keep_kernel(core_ref, columns_ref, att_ref, scaled_ref, query_turned_ref, keep_ref, gf_ref):
+    width = att_ref.shape[1]
+    inverse, factor = columns_ref[:, 0:1], columns_ref[:, 1:2]
+    for h in range(width // HEAD):
+        cols = head_cols(h)
+        gf_ref[:, cols] = (inverse * scaled_ref[:, cols] - att_ref[:, cols] * factor).astype(BF16)
+
+    def state_of(h):
+        return dot(query_turned_ref[h], gf_ref[:, head_cols(h)], NN)
+
+    half_of_heads(core_ref[0], width // HEAD // 2, 0, state_of, keep_ref)
 
 
 def send_out(copies, source, target, sems, i, cols):
@@ -274,11 +302,11 @@
 
 
 def near_grad(
-    sums_ref, att_ref, gain_ref, gf_ref, q_ref, k_ref, v_ref, state_ref, inside_ref, weights_ref,
+    columns_ref, att_ref, gain_ref, gf_ref, q_ref, k_ref, v_ref, state_ref, inside_ref, weights_ref,
     weights_turned_ref, mix_turned_ref, normed_hbm, gq_hbm, gk_ref, gv_ref, normed_ref, gq_ref, sems,
 ):
     rows, heads = inside_ref.shape
-    inverse, _ = norm_columns(sums_ref, rows)
+    inverse = columns_ref[:, 0:1]
     grown = jnp.exp(inside_ref[...])
     copies = []
     for h in range(heads):
@@ -385,17 +413,20 @@
         return [(m, a) for (m, _, _), a in zip(outs, arrays)]
 
     inputs = [queries, key_vectors, values, grad_out, decay_log.T, gain]
-    keep, send, kept, inside, across, key_decayed, q, k, v, g, gain = call(
+    send, kept, inside, across, q, k, v, g, gain = call(
         local_kernel,
         [
-            half_rows, ("v", (half * HEAD + heads, HEAD), F32), ("v", (heads, HEAD), F32), per_token,
-            ("v", (heads, rows), F32), wide_bf, wide_bf, wide_bf, wide_bf, wide_bf, ("v", (1, width), F32),
+            ("v", (half * HEAD + heads, HEAD), F32), ("v", (heads, HEAD), F32), per_token,
+            ("v", (heads, rows), F32), wide_bf, wide_bf, wide_bf, wide_bf, ("v", (1, width), F32),
         ],
         [on_core] + [("h", a) for a in inputs],
         2 * whole * HEAD, 8 * whole,
         scratch=[pltpu.VMEM((heads, rows), F32), pltpu.SemaphoreType.DMA((6,))],
     )
     got = swap(send)
+    keep, key_decayed = call(
+        local_keep_kernel, [half_rows, wide_bf], [on_core] + vmem(k, v, inside), whole * HEAD, 4 * whole
+    )
     mixing_args = vmem(q, k, v, g, gain, inside, across)
     mixing_outs = [
         wide_f32, ("v", square, BF16), wide_bf, ("v", (heads, HEAD, rows), BF16), ("v", square, F32),
@@ -437,15 +468,21 @@
         whole * HEAD, 6 * whole, aliases={7: 0, 8: 1},
     )
     sums = lax.all_to_all(sums, "tp", 0, 0)
-    back_keep, back_send, grad_flat = call(
+    back_send, columns = call(
         norm_grad_kernel,
-        [half_rows, half_rows, wide_bf],
+        [half_rows, ("v", (rows, 2), F32)],
         [on_core] + vmem(sums, attended, scaled, query_turned),
-        2 * whole * HEAD, 12 * whole,
+        whole * HEAD, 6 * whole,
     )
     back_got = swap(back_send)
+    back_keep, grad_flat = call(
+        norm_grad_keep_kernel,
+        [half_rows, wide_bf],
+        [on_core] + vmem(columns, attended, scaled, query_turned),
+        whole * HEAD, 6 * whole,
+    )
     near_args = vmem(
-        sums, attended, gain, grad_flat, q, k, v, entering, inside, weights, weights_turned, mixing_turned
+        columns, attended, gain, grad_flat, q, k, v, entering, inside, weights, weights_turned, mixing_turned
     )
     near_outs = [("h", wide, BF16), ("h", wide, BF16), wide_f32, wide_f32]
     outputs = [pltpu.VMEM(wide, BF16), pltpu.VMEM(wide, BF16), pltpu.SemaphoreType.DMA((heads,))]

time: 109 us -> 108 us (level)
    pallas_call x14 -> x16, Pallas kernels: 9.11 us -> 9.79 us  [call(): pl.pallas_call(kernel, out_shape=[SPACES[m](s, d) for m, s, d in outs], i...]
  transfers between devices with their start and end apart: 4 -> 4, of which waited for: 4 -> 4; matrix products, arithmetic and copies ran while one was open for 0% -> 0% of each run, Pallas kernels for 1% -> 2%
where the time goes in v7:
time: 108 us
  blocking collectives  73.6 us (68%)
  starting transfers between devices  21.1 us (20%)
  Pallas kernels  9.79 us (9%)
  waiting for transfers between devices  2.28 us (2%)
    all_to_all x4, blocking collectives, across_chips(): return lax.all_to_all(array, ('x', 'y'), 0, 0)  57.1 us
    ppermute x4, starting transfers between devices, swap(): return lax.ppermute(array, 'core', [(0, 1), (1, 0)])  21.1 us
    all_to_all x1, blocking collectives, body(): sums = lax.all_to_all(sums, 'tp', 0, 0)  16.5 us
    pallas_call x16, Pallas kernels, call(): pl.pallas_call(kernel, out_shape=[SPACES[m](s, d) for m, s, d in outs], i...  9.79 us
    ppermute x4, waiting for transfers between devices, swap(): return lax.ppermute(array, 'core', [(0, 1), (1, 0)])  2.28 us
  transfers between devices with their start and end apart: 4, of which 4 were waited for; matrix products, arithmetic and copies ran while one was open for 0% of the time, Pallas kernels for 2%

profile of v7, /device:TPU:1, one launch (start us, length us, event | category | flops | bytes accessed | tf_op | source)
XLA Modules:
  0.0 107.5 jit_solution(1684479710916640605)
XLA Ops:
  0.6 1.6 %shard_map.93 = (f32[520,128]{1,0:T(8,128)S(1)}, f32[8,128]{1,0:T(8,128)S(1)}, f32[160,8]{1,0:T(8,128)S(1)}, f32[8,160]{1,0:T(8,128)S(1)}, bf16[160,1024]{1,0:T(...) custom-call(s32[1]{0:T(128)} %bitcast.core_ref, ...), custom_call_target="tpu_custom_call" | custom-call | flops 41943040 | bytes 1310720 | tf_op jit(solution)/shard_map/pallas_call | solution.py:31
  2.2 8.8 %collective-permute-start = (f32[520,128]{1,0:T(8,128)S(1)}, f32[520,128]{1,0:T(8,128)S(1)}, u32[]{:S(2)}, u32[]{:S(2)}) collective-permute-start(f32[520,128]{1,0:T(8,128)S(1)} %get-tuple-element.58), channel_id=1, source_target_pairs={{0,8},{8,0},{1,9},{9,1},{2,10},{10,2},{3,11},{11,3},{4,12},{12,4},... | collective-permute-start | bytes 798728 | tf_op jit(solution)/shard_map/ppermute | solution.py:402
  11.0 0.5 shard_map.95
  11.5 0.6 collective-permute-done.after_ref.got_ref.got_kept_ref
  12.2 0.1 shard_map.96
  12.2 13.8 %all_to_all.25 = f32[32,1,2176]{2,1,0:T(1,128)S(1)} all-to-all(f32[32,1,2176]{2,1,0:T(1,128)S(1)} %bitcast.9), channel_id=1, replica_groups=mesh['x'=4,'y'=8,'core'=2,'tp'=8] {'x','y'}, dimensions={0} | all-to-all | bytes 557056 | tf_op jit(solution)/shard_map/all_to_all | solution.py:399
  26.0 0.1 shard_map.97
  26.1 14.9 %all_to_all.26 = f32[32,16,128]{2,1,0:T(8,128)S(1)} all-to-all(f32[32,16,128]{2,1,0:T(8,128)S(1)} %get-tuple-element.69), channel_id=1, replica_groups=mesh['x'=4,'y'=8,'core'=2,'tp'=8] {'x','y'}, dimensions={0} | all-to-all | bytes 524288 | tf_op jit(solution)/shard_map/all_to_all | solution.py:399
  41.0 1.6 %shard_map.98 = (f32[4,128,128]{2,1,0:T(8,128)S(1)}, f32[4,128,128]{2,1,0:T(8,128)S(1)}, f32[160,1024]{1,0:T(8,128)S(1)}, bf16[8,160,160]{2,1,0:T(8,128)(2,1)S(1...) custom-call(s32[1]{0:T(128)} %bitcast.core_ref, ...), custom_call_target="tpu_custom_call", output_to_operand_aliasing={{2}: (12, {}), {3}: (13, {}), {4}: (14, {}), {5}: (15, {}),... | custom-call | flops 157286400 | bytes 1966080 | tf_op jit(solution)/shard_map/pallas_call | solution.py:31
  42.6 4.7 %collective-permute-start.1 = (f32[4,128,128]{2,1,0:T(8,128)S(1)}, f32[4,128,128]{2,1,0:T(8,128)S(1)}, u32[]{:S(2)}, u32[]{:S(2)}) collective-permute-start(f32[4,128,128]{2,1,0:T(8,128)S(1)} %get-tuple-element.78), channel_id=1, source_target_pairs={{0,8},{8,0},{1,9},{9,1},{2,10},{10,2},{3,11},{11,3},{4,12},{12,4},... | collective-permute-start | bytes 786440 | tf_op jit(solution)/shard_map/ppermute | solution.py:402
  47.3 0.2 shard_map.99
  47.6 0.9 collective-permute-done.1.half_ref
  48.5 0.4 shard_map.100
  48.8 16.5 %all_to_all.27.sums_ref = f32[8,2,160]{2,1,0:T(2,128)S(1)} all-to-all(f32[8,2,160]{2,1,0:T(2,128)S(1)} %get-tuple-element.85), channel_id=1, replica_groups=mesh['x'=4,'y'=8,'core'=2,'tp'=8] {'tp'}, dimensions={0} | all-to-all | bytes 20480 | tf_op jit(solution)/shard_map/all_to_all | solution.py:470
  65.3 0.4 shard_map.101
  65.7 3.7 %collective-permute-start.2 = (f32[512,128]{1,0:T(8,128)S(1)}, f32[512,128]{1,0:T(8,128)S(1)}, u32[]{:S(2)}, u32[]{:S(2)}) collective-permute-start(f32[512,128]{1,0:T(8,128)S(1)} %get-tuple-element.96), channel_id=1, source_target_pairs={{0,8},{8,0},{1,9},{9,1},{2,10},{10,2},{3,11},{11,3},{4,12},{12,4},... | collective-permute-start | bytes 786440 | tf_op jit(solution)/shard_map/ppermute | solution.py:402
  69.4 0.4 shard_map.102
  69.8 0.1 shard_map.103
  69.9 0.6 collective-permute-done.2.got_ref
  70.6 13.6 %all_to_all.28.got_ref = f32[32,16,128]{2,1,0:T(8,128)S(1)} all-to-all(f32[32,16,128]{2,1,0:T(8,128)S(1)} %bitcast.12), channel_id=1, replica_groups=mesh['x'=4,'y'=8,'core'=2,'tp'=8] {'x','y'}, dimensions={0} | all-to-all | bytes 524288 | tf_op jit(solution)/shard_map/all_to_all | solution.py:399
  84.2 0.1 shard_map.105
  84.3 14.7 %all_to_all.29 = f32[32,16,128]{2,1,0:T(8,128)S(1)} all-to-all(f32[32,16,128]{2,1,0:T(8,128)S(1)} %shard_map.105), channel_id=1, replica_groups=mesh['x'=4,'y'=8,'core'=2,'tp'=8] {'x','y'}, dimensions={0} | all-to-all | bytes 524288 | tf_op jit(solution)/shard_map/all_to_all | solution.py:399
  99.0 2.4 %shard_map.106 = (f32[4,128,128]{2,1,0:T(8,128)S(1)}, f32[4,128,128]{2,1,0:T(8,128)S(1)}, bf16[160,1024]{1,0:T(8,128)(2,1)}, bf16[160,1024]{1,0:T(8,128)(2,1)}, ...) custom-call(s32[1]{0:T(128)} %bitcast.core_ref, ...), custom_call_target="tpu_custom_call", output_to_operand_aliasing={{2}: (18, {}), {3}: (19, {}), {4}: (20, {}), {5}: (21, {})} | custom-call | flops 314572800 | bytes 2621440 | tf_op jit(solution)/shard_map/pallas_call | solution.py:31
  101.5 3.9 %collective-permute-start.3 = (f32[4,128,128]{2,1,0:T(8,128)S(1)}, f32[4,128,128]{2,1,0:T(8,128)S(1)}, u32[]{:S(2)}, u32[]{:S(2)}) collective-permute-start(f32[4,128,128]{2,1,0:T(8,128)S(1)} %get-tuple-element.106), channel_id=1, source_target_pairs={{0,8},{8,0},{1,9},{9,1},{2,10},{10,2},{3,11},{11,3},{4,12},{12,4},... | collective-permute-start | bytes 786440 | tf_op jit(solution)/shard_map/ppermute | solution.py:402
  105.4 1.0 shard_map.107
  106.4 0.1 collective-permute-done.3.half_ref
  106.5 1.0 shard_map.108
  (2 shorter events, 0.0 us)
Async XLA Ops:
  2.2 9.9 %collective-permute-start = (f32[520,128]{1,0:T(8,128)S(1)}, f32[520,128]{1,0:T(8,128)S(1)}, u32[]{:S(2)}, u32[]{:S(2)}) collective-permute-start(f32[520,128]{1,0:T(8,128)S(1)} %get-tuple-element.58), channel_id=1, source_target_pairs={{0,8},{8,0},{1,9},{9,1},{2,10},{10,2},{3,11},{11,3},{4,12},{12,4},... | collective-permute-start | bytes 798728 | tf_op jit(solution)/shard_map/ppermute | solution.py:402
  42.6 5.9 %collective-permute-start.1 = (f32[4,128,128]{2,1,0:T(8,128)S(1)}, f32[4,128,128]{2,1,0:T(8,128)S(1)}, u32[]{:S(2)}, u32[]{:S(2)}) collective-permute-start(f32[4,128,128]{2,1,0:T(8,128)S(1)} %get-tuple-element.78), channel_id=1, source_target_pairs={{0,8},{8,0},{1,9},{9,1},{2,10},{10,2},{3,11},{11,3},{4,12},{12,4},... | collective-permute-start | bytes 786440 | tf_op jit(solution)/shard_map/ppermute | solution.py:402
  65.7 4.9 %collective-permute-start.2 = (f32[512,128]{1,0:T(8,128)S(1)}, f32[512,128]{1,0:T(8,128)S(1)}, u32[]{:S(2)}, u32[]{:S(2)}) collective-permute-start(f32[512,128]{1,0:T(8,128)S(1)} %get-tuple-element.96), channel_id=1, source_target_pairs={{0,8},{8,0},{1,9},{9,1},{2,10},{10,2},{3,11},{11,3},{4,12},{12,4},... | collective-permute-start | bytes 786440 | tf_op jit(solution)/shard_map/ppermute | solution.py:402
  101.5 5.0 %collective-permute-start.3 = (f32[4,128,128]{2,1,0:T(8,128)S(1)}, f32[4,128,128]{2,1,0:T(8,128)S(1)}, u32[]{:S(2)}, u32[]{:S(2)}) collective-permute-start(f32[4,128,128]{2,1,0:T(8,128)S(1)} %get-tuple-element.106), channel_id=1, source_target_pairs={{0,8},{8,0},{1,9},{9,1},{2,10},{10,2},{3,11},{11,3},{4,12},{12,4},... | collective-permute-start | bytes 786440 | tf_op jit(solution)/shard_map/ppermute | solution.py:402

commit v8 on v7

--- a/solution.py
+++ b/solution.py
@@ -432,7 +432,7 @@
         wide_f32, ("v", square, BF16), wide_bf, ("v", (heads, HEAD, rows), BF16), ("v", square, F32),
         ("v", square, F32), wide_f32,
     ]
-    mixing_done = call(mixing_first_kernel, mixing_outs, [on_core, ("a", got)] + mixing_args, 6 * whole * rows, 12 * whole)
+    mixing_done = call(mixing_first_kernel, mixing_outs, [on_core, ("a", keep)] + mixing_args, 6 * whole * rows, 12 * whole)
     (pay,) = call(
         forward_join_kernel,
         [("v", (chips * (slab + 1), HEAD), F32)],

time: 108 us -> 108 us (level)
  no operation moved by 1% of the time
where the time goes in v8:
time: 108 us
  blocking collectives  74.4 us (69%)
  starting transfers between devices  20.5 us (19%)
  Pallas kernels  9.76 us (9%)
  waiting for transfers between devices  2.27 us (2%)
    all_to_all x4, blocking collectives, across_chips(): return lax.all_to_all(array, ('x', 'y'), 0, 0)  57.9 us
    ppermute x4, starting transfers between devices, swap(): return lax.ppermute(array, 'core', [(0, 1), (1, 0)])  20.5 us
    all_to_all x1, blocking collectives, body(): sums = lax.all_to_all(sums, 'tp', 0, 0)  16.5 us
    pallas_call x16, Pallas kernels, call(): pl.pallas_call(kernel, out_shape=[SPACES[m](s, d) for m, s, d in outs], i...  9.76 us
    ppermute x4, waiting for transfers between devices, swap(): return lax.ppermute(array, 'core', [(0, 1), (1, 0)])  2.27 us
  transfers between devices with their start and end apart: 4, of which 4 were waited for; matrix products, arithmetic and copies ran while one was open for 0% of the time, Pallas kernels for 2%

profile of v8, /device:TPU:1, one launch (start us, length us, event | category | flops | bytes accessed | tf_op | source)
XLA Modules:
  0.0 107.7 jit_solution(15219952050324110971)
XLA Ops:
  0.6 1.6 %shard_map.93 = (f32[520,128]{1,0:T(8,128)S(1)}, f32[8,128]{1,0:T(8,128)S(1)}, f32[160,8]{1,0:T(8,128)S(1)}, f32[8,160]{1,0:T(8,128)S(1)}, bf16[160,1024]{1,0:T(...) custom-call(s32[1]{0:T(128)} %bitcast.core_ref, ...), custom_call_target="tpu_custom_call" | custom-call | flops 41943040 | bytes 1310720 | tf_op jit(solution)/shard_map/pallas_call | solution.py:31
  2.2 8.8 %collective-permute-start = (f32[520,128]{1,0:T(8,128)S(1)}, f32[520,128]{1,0:T(8,128)S(1)}, u32[]{:S(2)}, u32[]{:S(2)}) collective-permute-start(f32[520,128]{1,0:T(8,128)S(1)} %get-tuple-element.67), channel_id=1, source_target_pairs={{0,8},{8,0},{1,9},{9,1},{2,10},{10,2},{3,11},{11,3},{4,12},{12,4},... | collective-permute-start | bytes 798728 | tf_op jit(solution)/shard_map/ppermute | solution.py:402
  11.0 0.5 shard_map.94
  11.6 0.6 collective-permute-done.got_ref.got_kept_ref
  12.1 0.1 shard_map.96
  12.2 13.8 %all_to_all.25 = f32[32,1,2176]{2,1,0:T(1,128)S(1)} all-to-all(f32[32,1,2176]{2,1,0:T(1,128)S(1)} %bitcast.9), channel_id=1, replica_groups=mesh['x'=4,'y'=8,'core'=2,'tp'=8] {'x','y'}, dimensions={0} | all-to-all | bytes 557056 | tf_op jit(solution)/shard_map/all_to_all | solution.py:399
  26.0 0.1 shard_map.97
  26.1 15.8 %all_to_all.26 = f32[32,16,128]{2,1,0:T(8,128)S(1)} all-to-all(f32[32,16,128]{2,1,0:T(8,128)S(1)} %get-tuple-element.69), channel_id=1, replica_groups=mesh['x'=4,'y'=8,'core'=2,'tp'=8] {'x','y'}, dimensions={0} | all-to-all | bytes 524288 | tf_op jit(solution)/shard_map/all_to_all | solution.py:399
  41.8 1.6 %shard_map.98 = (f32[4,128,128]{2,1,0:T(8,128)S(1)}, f32[4,128,128]{2,1,0:T(8,128)S(1)}, f32[160,1024]{1,0:T(8,128)S(1)}, bf16[8,160,160]{2,1,0:T(8,128)(2,1)S(1...) custom-call(s32[1]{0:T(128)} %bitcast.core_ref, ...), custom_call_target="tpu_custom_call", output_to_operand_aliasing={{2}: (12, {}), {3}: (13, {}), {4}: (14, {}), {5}: (15, {}),... | custom-call | flops 157286400 | bytes 1966080 | tf_op jit(solution)/shard_map/pallas_call | solution.py:31
  43.4 4.2 %collective-permute-start.1 = (f32[4,128,128]{2,1,0:T(8,128)S(1)}, f32[4,128,128]{2,1,0:T(8,128)S(1)}, u32[]{:S(2)}, u32[]{:S(2)}) collective-permute-start(f32[4,128,128]{2,1,0:T(8,128)S(1)} %get-tuple-element.78), channel_id=1, source_target_pairs={{0,8},{8,0},{1,9},{9,1},{2,10},{10,2},{3,11},{11,3},{4,12},{12,4},... | collective-permute-start | bytes 786440 | tf_op jit(solution)/shard_map/ppermute | solution.py:402
  47.6 0.2 shard_map.99
  47.8 0.9 collective-permute-done.1.half_ref
  48.7 0.4 shard_map.100
  49.1 16.5 %all_to_all.27.sums_ref = f32[8,2,160]{2,1,0:T(2,128)S(1)} all-to-all(f32[8,2,160]{2,1,0:T(2,128)S(1)} %get-tuple-element.85), channel_id=1, replica_groups=mesh['x'=4,'y'=8,'core'=2,'tp'=8] {'tp'}, dimensions={0} | all-to-all | bytes 20480 | tf_op jit(solution)/shard_map/all_to_all | solution.py:470
  65.6 0.4 shard_map.101
  65.9 3.7 %collective-permute-start.2 = (f32[512,128]{1,0:T(8,128)S(1)}, f32[512,128]{1,0:T(8,128)S(1)}, u32[]{:S(2)}, u32[]{:S(2)}) collective-permute-start(f32[512,128]{1,0:T(8,128)S(1)} %get-tuple-element.96), channel_id=1, source_target_pairs={{0,8},{8,0},{1,9},{9,1},{2,10},{10,2},{3,11},{11,3},{4,12},{12,4},... | collective-permute-start | bytes 786440 | tf_op jit(solution)/shard_map/ppermute | solution.py:402
  69.7 0.4 shard_map.102
  70.1 0.1 shard_map.103
  70.2 0.6 collective-permute-done.2.got_ref
  70.9 13.6 %all_to_all.28.got_ref = f32[32,16,128]{2,1,0:T(8,128)S(1)} all-to-all(f32[32,16,128]{2,1,0:T(8,128)S(1)} %bitcast.12), channel_id=1, replica_groups=mesh['x'=4,'y'=8,'core'=2,'tp'=8] {'x','y'}, dimensions={0} | all-to-all | bytes 524288 | tf_op jit(solution)/shard_map/all_to_all | solution.py:399
  84.4 0.1 shard_map.105
  84.5 14.7 %all_to_all.29 = f32[32,16,128]{2,1,0:T(8,128)S(1)} all-to-all(f32[32,16,128]{2,1,0:T(8,128)S(1)} %shard_map.105), channel_id=1, replica_groups=mesh['x'=4,'y'=8,'core'=2,'tp'=8] {'x','y'}, dimensions={0} | all-to-all | bytes 524288 | tf_op jit(solution)/shard_map/all_to_all | solution.py:399
  99.2 2.4 %shard_map.106 = (f32[4,128,128]{2,1,0:T(8,128)S(1)}, f32[4,128,128]{2,1,0:T(8,128)S(1)}, bf16[160,1024]{1,0:T(8,128)(2,1)}, bf16[160,1024]{1,0:T(8,128)(2,1)}, ...) custom-call(s32[1]{0:T(128)} %bitcast.core_ref, ...), custom_call_target="tpu_custom_call", output_to_operand_aliasing={{2}: (18, {}), {3}: (19, {}), {4}: (20, {}), {5}: (21, {})} | custom-call | flops 314572800 | bytes 2621440 | tf_op jit(solution)/shard_map/pallas_call | solution.py:31
  101.7 3.9 %collective-permute-start.3 = (f32[4,128,128]{2,1,0:T(8,128)S(1)}, f32[4,128,128]{2,1,0:T(8,128)S(1)}, u32[]{:S(2)}, u32[]{:S(2)}) collective-permute-start(f32[4,128,128]{2,1,0:T(8,128)S(1)} %get-tuple-element.106), channel_id=1, source_target_pairs={{0,8},{8,0},{1,9},{9,1},{2,10},{10,2},{3,11},{11,3},{4,12},{12,4},... | collective-permute-start | bytes 786440 | tf_op jit(solution)/shard_map/ppermute | solution.py:402
  105.6 1.0 shard_map.107
  106.6 0.1 collective-permute-done.3.half_ref
  106.7 1.0 shard_map.108
  (2 shorter events, 0.1 us)
Async XLA Ops:
  2.2 9.9 %collective-permute-start = (f32[520,128]{1,0:T(8,128)S(1)}, f32[520,128]{1,0:T(8,128)S(1)}, u32[]{:S(2)}, u32[]{:S(2)}) collective-permute-start(f32[520,128]{1,0:T(8,128)S(1)} %get-tuple-element.67), channel_id=1, source_target_pairs={{0,8},{8,0},{1,9},{9,1},{2,10},{10,2},{3,11},{11,3},{4,12},{12,4},... | collective-permute-start | bytes 798728 | tf_op jit(solution)/shard_map/ppermute | solution.py:402
  43.4 5.3 %collective-permute-start.1 = (f32[4,128,128]{2,1,0:T(8,128)S(1)}, f32[4,128,128]{2,1,0:T(8,128)S(1)}, u32[]{:S(2)}, u32[]{:S(2)}) collective-permute-start(f32[4,128,128]{2,1,0:T(8,128)S(1)} %get-tuple-element.78), channel_id=1, source_target_pairs={{0,8},{8,0},{1,9},{9,1},{2,10},{10,2},{3,11},{11,3},{4,12},{12,4},... | collective-permute-start | bytes 786440 | tf_op jit(solution)/shard_map/ppermute | solution.py:402
  65.9 4.9 %collective-permute-start.2 = (f32[512,128]{1,0:T(8,128)S(1)}, f32[512,128]{1,0:T(8,128)S(1)}, u32[]{:S(2)}, u32[]{:S(2)}) collective-permute-start(f32[512,128]{1,0:T(8,128)S(1)} %get-tuple-element.96), channel_id=1, source_target_pairs={{0,8},{8,0},{1,9},{9,1},{2,10},{10,2},{3,11},{11,3},{4,12},{12,4},... | collective-permute-start | bytes 786440 | tf_op jit(solution)/shard_map/ppermute | solution.py:402
  101.7 5.0 %collective-permute-start.3 = (f32[4,128,128]{2,1,0:T(8,128)S(1)}, f32[4,128,128]{2,1,0:T(8,128)S(1)}, u32[]{:S(2)}, u32[]{:S(2)}) collective-permute-start(f32[4,128,128]{2,1,0:T(8,128)S(1)} %get-tuple-element.106), channel_id=1, source_target_pairs={{0,8},{8,0},{1,9},{9,1},{2,10},{10,2},{3,11},{11,3},{4,12},{12,4},... | collective-permute-start | bytes 786440 | tf_op jit(solution)/shard_map/ppermute | solution.py:402

commit v9 on v7

--- a/solution.py
+++ b/solution.py
@@ -140,10 +140,14 @@
             pay_ref[at + 16 : at + 17, :] = kept_first * kept_second
 
 
+def chips_in_order(count):
+    return [y * (count // 8) + x for x in range(count // 8) for y in range(8)]
+
+
 def forward_scan_kernel(got_ref, out_ref, kept_ref):
     count = out_ref.shape[0]
     state = jnp.zeros(out_ref.shape[1:], F32)
-    for j in range(count):
+    for j in chips_in_order(count):
         out_ref[j] = state
         kept = got_ref[17 * j + 16 : 17 * j + 17, :]
         kept_ref[j : j + 1, :] = kept
@@ -161,7 +165,7 @@
 def reverse_scan_kernel(got_ref, kept_ref, out_ref):
     count = out_ref.shape[0]
     state = jnp.zeros(out_ref.shape[1:], F32)
-    for j in reversed(range(count)):
+    for j in reversed(chips_in_order(count)):
         out_ref[j] = state
         state = kept_ref[j : j + 1, :] * state + got_ref[j]
 
@@ -396,7 +400,7 @@
     whole, size = rows * width, heads * HEAD * HEAD
 
     def across_chips(array):
-        return lax.all_to_all(array, ("x", "y"), 0, 0)
+        return lax.all_to_all(array, ("y", "x"), 0, 0)
 
     def swap(array):
         return lax.ppermute(array, "core", [(0, 1), (1, 0)])

time: 108 us -> 108 us (level)
  no operation moved by 1% of the time
where the time goes in v9:
time: 108 us
  blocking collectives  73 us (68%)
  starting transfers between devices  21.8 us (20%)
  Pallas kernels  9.79 us (9%)
  waiting for transfers between devices  2.28 us (2%)
    all_to_all x4, blocking collectives, across_chips(): return lax.all_to_all(array, ('y', 'x'), 0, 0)  56.5 us
    ppermute x4, starting transfers between devices, swap(): return lax.ppermute(array, 'core', [(0, 1), (1, 0)])  21.8 us
    all_to_all x1, blocking collectives, body(): sums = lax.all_to_all(sums, 'tp', 0, 0)  16.5 us
    pallas_call x16, Pallas kernels, call(): pl.pallas_call(kernel, out_shape=[SPACES[m](s, d) for m, s, d in outs], i...  9.79 us
    ppermute x4, waiting for transfers between devices, swap(): return lax.ppermute(array, 'core', [(0, 1), (1, 0)])  2.28 us
  transfers between devices with their start and end apart: 4, of which 4 were waited for; matrix products, arithmetic and copies ran while one was open for 0% of the time, Pallas kernels for 2%

profile of v9, /device:TPU:1, one launch (start us, length us, event | category | flops | bytes accessed | tf_op | source)
XLA Modules:
  0.0 107.7 jit_solution(1740037020597975368)
XLA Ops:
  0.6 1.6 %shard_map.93 = (f32[520,128]{1,0:T(8,128)S(1)}, f32[8,128]{1,0:T(8,128)S(1)}, f32[160,8]{1,0:T(8,128)S(1)}, f32[8,160]{1,0:T(8,128)S(1)}, bf16[160,1024]{1,0:T(...) custom-call(s32[1]{0:T(128)} %bitcast.core_ref, ...), custom_call_target="tpu_custom_call" | custom-call | flops 41943040 | bytes 1310720 | tf_op jit(solution)/shard_map/pallas_call | solution.py:31
  2.2 8.8 %collective-permute-start = (f32[520,128]{1,0:T(8,128)S(1)}, f32[520,128]{1,0:T(8,128)S(1)}, u32[]{:S(2)}, u32[]{:S(2)}) collective-permute-start(f32[520,128]{1,0:T(8,128)S(1)} %get-tuple-element.58), channel_id=1, source_target_pairs={{0,8},{8,0},{1,9},{9,1},{2,10},{10,2},{3,11},{11,3},{4,12},{12,4},... | collective-permute-start | bytes 798728 | tf_op jit(solution)/shard_map/ppermute | solution.py:406
  11.0 0.5 shard_map.95
  11.5 0.6 collective-permute-done.after_ref.got_ref.got_kept_ref
  12.2 0.1 shard_map.96
  12.2 14.6 %all_to_all.25 = f32[32,1,2176]{2,1,0:T(1,128)S(1)} all-to-all(f32[32,1,2176]{2,1,0:T(1,128)S(1)} %bitcast.9), channel_id=1, replica_groups=mesh['x'=4,'y'=8,'core'=2,'tp'=8] {'y','x'}, dimensions={0} | all-to-all | bytes 557056 | tf_op jit(solution)/shard_map/all_to_all | solution.py:403
  26.8 0.1 shard_map.97
  26.9 14.2 %all_to_all.26 = f32[32,16,128]{2,1,0:T(8,128)S(1)} all-to-all(f32[32,16,128]{2,1,0:T(8,128)S(1)} %get-tuple-element.69), channel_id=1, replica_groups=mesh['x'=4,'y'=8,'core'=2,'tp'=8] {'y','x'}, dimensions={0} | all-to-all | bytes 524288 | tf_op jit(solution)/shard_map/all_to_all | solution.py:403
  41.1 1.6 %shard_map.98 = (f32[4,128,128]{2,1,0:T(8,128)S(1)}, f32[4,128,128]{2,1,0:T(8,128)S(1)}, f32[160,1024]{1,0:T(8,128)S(1)}, bf16[8,160,160]{2,1,0:T(8,128)(2,1)S(1...) custom-call(s32[1]{0:T(128)} %bitcast.core_ref, ...), custom_call_target="tpu_custom_call", output_to_operand_aliasing={{2}: (12, {}), {3}: (13, {}), {4}: (14, {}), {5}: (15, {}),... | custom-call | flops 157286400 | bytes 1966080 | tf_op jit(solution)/shard_map/pallas_call | solution.py:31
  42.7 5.3 %collective-permute-start.1 = (f32[4,128,128]{2,1,0:T(8,128)S(1)}, f32[4,128,128]{2,1,0:T(8,128)S(1)}, u32[]{:S(2)}, u32[]{:S(2)}) collective-permute-start(f32[4,128,128]{2,1,0:T(8,128)S(1)} %get-tuple-element.78), channel_id=1, source_target_pairs={{0,8},{8,0},{1,9},{9,1},{2,10},{10,2},{3,11},{11,3},{4,12},{12,4},... | collective-permute-start | bytes 786440 | tf_op jit(solution)/shard_map/ppermute | solution.py:406
  48.1 0.2 shard_map.99
  48.3 0.9 collective-permute-done.1.half_ref
  49.2 0.4 shard_map.100
  49.6 16.5 %all_to_all.27.sums_ref = f32[8,2,160]{2,1,0:T(2,128)S(1)} all-to-all(f32[8,2,160]{2,1,0:T(2,128)S(1)} %get-tuple-element.85), channel_id=1, replica_groups=mesh['x'=4,'y'=8,'core'=2,'tp'=8] {'tp'}, dimensions={0} | all-to-all | bytes 20480 | tf_op jit(solution)/shard_map/all_to_all | solution.py:474
  66.0 0.4 shard_map.101
  66.4 3.7 %collective-permute-start.2 = (f32[512,128]{1,0:T(8,128)S(1)}, f32[512,128]{1,0:T(8,128)S(1)}, u32[]{:S(2)}, u32[]{:S(2)}) collective-permute-start(f32[512,128]{1,0:T(8,128)S(1)} %get-tuple-element.96), channel_id=1, source_target_pairs={{0,8},{8,0},{1,9},{9,1},{2,10},{10,2},{3,11},{11,3},{4,12},{12,4},... | collective-permute-start | bytes 786440 | tf_op jit(solution)/shard_map/ppermute | solution.py:406
  70.1 0.4 shard_map.102
  70.5 0.1 shard_map.103
  70.6 0.6 collective-permute-done.2.got_ref
  71.3 13.4 %all_to_all.28.got_ref = f32[32,16,128]{2,1,0:T(8,128)S(1)} all-to-all(f32[32,16,128]{2,1,0:T(8,128)S(1)} %bitcast.12), channel_id=1, replica_groups=mesh['x'=4,'y'=8,'core'=2,'tp'=8] {'y','x'}, dimensions={0} | all-to-all | bytes 524288 | tf_op jit(solution)/shard_map/all_to_all | solution.py:403
  84.7 0.1 shard_map.105
  84.8 14.3 %all_to_all.29 = f32[32,16,128]{2,1,0:T(8,128)S(1)} all-to-all(f32[32,16,128]{2,1,0:T(8,128)S(1)} %shard_map.105), channel_id=1, replica_groups=mesh['x'=4,'y'=8,'core'=2,'tp'=8] {'y','x'}, dimensions={0} | all-to-all | bytes 524288 | tf_op jit(solution)/shard_map/all_to_all | solution.py:403
  99.1 2.4 %shard_map.106 = (f32[4,128,128]{2,1,0:T(8,128)S(1)}, f32[4,128,128]{2,1,0:T(8,128)S(1)}, bf16[160,1024]{1,0:T(8,128)(2,1)}, bf16[160,1024]{1,0:T(8,128)(2,1)}, ...) custom-call(s32[1]{0:T(128)} %bitcast.core_ref, ...), custom_call_target="tpu_custom_call", output_to_operand_aliasing={{2}: (18, {}), {3}: (19, {}), {4}: (20, {}), {5}: (21, {})} | custom-call | flops 314572800 | bytes 2621440 | tf_op jit(solution)/shard_map/pallas_call | solution.py:31
  101.5 4.0 %collective-permute-start.3 = (f32[4,128,128]{2,1,0:T(8,128)S(1)}, f32[4,128,128]{2,1,0:T(8,128)S(1)}, u32[]{:S(2)}, u32[]{:S(2)}) collective-permute-start(f32[4,128,128]{2,1,0:T(8,128)S(1)} %get-tuple-element.106), channel_id=1, source_target_pairs={{0,8},{8,0},{1,9},{9,1},{2,10},{10,2},{3,11},{11,3},{4,12},{12,4},... | collective-permute-start | bytes 786440 | tf_op jit(solution)/shard_map/ppermute | solution.py:406
  105.5 1.0 shard_map.107
  106.5 0.1 collective-permute-done.3.half_ref
  106.7 1.0 shard_map.108
  (2 shorter events, 0.0 us)
Async XLA Ops:
  2.2 9.9 %collective-permute-start = (f32[520,128]{1,0:T(8,128)S(1)}, f32[520,128]{1,0:T(8,128)S(1)}, u32[]{:S(2)}, u32[]{:S(2)}) collective-permute-start(f32[520,128]{1,0:T(8,128)S(1)} %get-tuple-element.58), channel_id=1, source_target_pairs={{0,8},{8,0},{1,9},{9,1},{2,10},{10,2},{3,11},{11,3},{4,12},{12,4},... | collective-permute-start | bytes 798728 | tf_op jit(solution)/shard_map/ppermute | solution.py:406
  42.7 6.5 %collective-permute-start.1 = (f32[4,128,128]{2,1,0:T(8,128)S(1)}, f32[4,128,128]{2,1,0:T(8,128)S(1)}, u32[]{:S(2)}, u32[]{:S(2)}) collective-permute-start(f32[4,128,128]{2,1,0:T(8,128)S(1)} %get-tuple-element.78), channel_id=1, source_target_pairs={{0,8},{8,0},{1,9},{9,1},{2,10},{10,2},{3,11},{11,3},{4,12},{12,4},... | collective-permute-start | bytes 786440 | tf_op jit(solution)/shard_map/ppermute | solution.py:406
  66.4 4.9 %collective-permute-start.2 = (f32[512,128]{1,0:T(8,128)S(1)}, f32[512,128]{1,0:T(8,128)S(1)}, u32[]{:S(2)}, u32[]{:S(2)}) collective-permute-start(f32[512,128]{1,0:T(8,128)S(1)} %get-tuple-element.96), channel_id=1, source_target_pairs={{0,8},{8,0},{1,9},{9,1},{2,10},{10,2},{3,11},{11,3},{4,12},{12,4},... | collective-permute-start | bytes 786440 | tf_op jit(solution)/shard_map/ppermute | solution.py:406
  101.5 5.1 %collective-permute-start.3 = (f32[4,128,128]{2,1,0:T(8,128)S(1)}, f32[4,128,128]{2,1,0:T(8,128)S(1)}, u32[]{:S(2)}, u32[]{:S(2)}) collective-permute-start(f32[4,128,128]{2,1,0:T(8,128)S(1)} %get-tuple-element.106), channel_id=1, source_target_pairs={{0,8},{8,0},{1,9},{9,1},{2,10},{10,2},{3,11},{11,3},{4,12},{12,4},... | collective-permute-start | bytes 786440 | tf_op jit(solution)/shard_map/ppermute | solution.py:406
